TPU v7x, 32 devices: a whole 2x2x4 slice. The times are simulated.
32 devices in a mesh: ctx: 16 (over z, y, x), head: 2 (over core).
Axes of the slice: x: 2, y: 2, z: 4, core: 2. Of those that a mesh axis runs over, the one named last changes fastest.
Arguments:
- queries: bfloat16 [2048, 3072], P('ctx', 'head'), may hold values from -6 to 6
- keys: bfloat16 [2048, 3072], P('ctx', 'head'), may hold values from -6 to 6
- values: bfloat16 [2048, 3072], P('ctx', 'head'), may hold values from -30 to 30
- decay_log: float32 [32, 2048], P('head', 'ctx'), may hold values from -1 to 0
- norm_gain: float32 [3072], P('head'), may hold values from 0.25 to 1.75
- out_grad: bfloat16 [2048, 3072], P('ctx', 'head'), may hold values from -6 to 6
- doc_lengths: int32 [16], replicated, may hold values from 1 to 512, 2048 in all
Outputs:
- attn_output: bfloat16 [2048, 3072], P('ctx', 'head')
- query_grad: bfloat16 [2048, 3072], P('ctx', 'head')
- key_grad: bfloat16 [2048, 3072], P('ctx', 'head')
- value_grad: bfloat16 [2048, 3072], P('ctx', 'head')
Inputs may be any that keep to these rules, and one draw needn't show every extreme that they name: `doc_lengths`: the 16 lengths sum to 2048; the longest is exactly 512.
All inputs are finite; a program needn't handle non-finite values.
Results may differ from a plain program's by a relative error of at most 0.01.
Values sent between devices are 32-bit elements; how exact they have to be, the bound alone decides.
No kernel may reach another device: no remote copies, remote signals or barrier semaphores. Data moves between devices by JAX's collectives and lax.ppermute only.
A program may use at most 256 MiB of HBM per device.

v0:
```python
import math

import jax
import jax.numpy as jnp
from jax import lax
from jax.sharding import PartitionSpec as P

EPSILON = 1e-06


def entering(part, axis, combine, identity, reverse):
    count = lax.axis_size(axis)
    place = lax.axis_index(axis)
    ahead = count - 1 - place if reverse else place
    gathered = jax.tree.map(lambda a: lax.all_gather(a, axis), part)
    state = jax.tree.map(lambda a, e: jnp.zeros_like(a) + jnp.asarray(e, a.dtype), part, identity)

    def one(hop, state):
        source = count - 1 - hop if reverse else hop
        return combine(
            state, jax.tree.map(lambda a: lax.dynamic_index_in_dim(a, source, 0, False), gathered)
        )

    return lax.fori_loop(0, ahead, one, state)


def doc_starts(doc_lengths):
    doc_ends = jnp.cumsum(doc_lengths)
    return doc_ends - doc_lengths


def geometry(decay_block, block_start, starts_doc):
    row_count = decay_block.shape[1]
    positions = block_start + jnp.arange(row_count, dtype=jnp.int32)
    doc_index = jnp.sum((starts_doc[None, :] <= positions[:, None]).astype(jnp.int32), axis=1)
    doc_before = jnp.sum((starts_doc <= block_start - 1).astype(jnp.int32))
    carry_mask = (doc_index == doc_before).astype(decay_block.dtype)
    log_cum = jnp.cumsum(decay_block, axis=1)
    causal = positions[:, None] >= positions[None, :]
    same_doc = jnp.logical_and(causal, doc_index[:, None] == doc_index[None, :])
    log_gap = jnp.where(same_doc[None], log_cum[:, :, None] - log_cum[:, None, :], 0.0)
    decay_mask = jnp.exp(log_gap) * same_doc[None].astype(decay_block.dtype)
    keep_last = (doc_index == doc_index[row_count - 1]).astype(decay_block.dtype)
    exit_weight = jnp.exp(log_cum[:, row_count - 1 : row_count] - log_cum) * keep_last[None, :]
    reach_in = carry_mask[None, :] * jnp.exp(log_cum)
    factor = reach_in[:, row_count - 1]
    return (decay_mask, exit_weight, reach_in, factor)


def combine(earlier, later_pair):
    return (earlier[0] * later_pair[0], later_pair[0][:, None, None] * earlier[1] + later_pair[1])


def split_pair(array):
    high = array.astype(jnp.bfloat16)
    low = (array - high.astype(jnp.float32)).astype(jnp.bfloat16)
    return (high, low)


def pair_einsum(form, first, second):
    if first.dtype == jnp.float32:
        high, low = split_pair(first)
        return jnp.einsum(form, high, second, preferred_element_type=jnp.float32) + jnp.einsum(
            form, low, second, preferred_element_type=jnp.float32
        )
    high, low = split_pair(second)
    return jnp.einsum(form, first, high, preferred_element_type=jnp.float32) + jnp.einsum(
        form, first, low, preferred_element_type=jnp.float32
    )


def on_device(queries, keys, values, decay_log, norm_gain, out_grad, doc_lengths):
    row_count, local_width = queries.shape
    head_count = decay_log.shape[0]
    head_width = local_width // head_count
    score_scale = 1.0 / math.sqrt(head_width)
    feature_count = local_width * lax.axis_size("head")
    block_start = lax.axis_index("ctx") * row_count
    starts_doc = doc_starts(doc_lengths)
    decay_mask, exit_weight, reach_in, factor = geometry(decay_log, block_start, starts_doc)
    query_heads = queries.reshape(row_count, head_count, head_width)
    key_heads = keys.reshape(row_count, head_count, head_width)
    value_heads = values.reshape(row_count, head_count, head_width)
    weighted_keys = key_heads.astype(jnp.float32) * exit_weight.T[:, :, None]
    exit_local = pair_einsum("shd,she->hde", weighted_keys, value_heads)
    zero_state = jnp.zeros_like(exit_local)
    prefix_pair = entering(
        (factor, exit_local), "ctx", combine, (jnp.ones_like(factor), zero_state), False
    )
    incoming = prefix_pair[1]
    scores = jnp.einsum("thd,shd->hts", query_heads, key_heads, preferred_element_type=jnp.float32)
    attn_probs = (scores * score_scale * decay_mask).astype(jnp.bfloat16)
    local_part = jnp.einsum(
        "hts,shd->thd", attn_probs, value_heads, preferred_element_type=jnp.float32
    )
    carried = pair_einsum("thd,hde->the", query_heads, incoming)
    attended = (local_part + score_scale * reach_in.T[:, :, None] * carried).reshape(
        row_count, local_width
    )
    square_sum = lax.psum(jnp.sum(attended * attended, axis=1), "head")
    inv_rms = lax.rsqrt(square_sum / feature_count + EPSILON)
    attn_output = (attended * inv_rms[:, None] * norm_gain[None, :]).astype(jnp.bfloat16)
    grad_gain = out_grad.astype(jnp.float32) * norm_gain[None, :]
    grad_dot = lax.psum(jnp.sum(grad_gain * attended, axis=1), "head")
    attended_grad = (
        grad_gain * inv_rms[:, None] - attended * (inv_rms**3 * grad_dot / feature_count)[:, None]
    ).astype(jnp.bfloat16)
    grad_heads = attended_grad.reshape(row_count, head_count, head_width)
    reached_queries = query_heads.astype(jnp.float32) * reach_in.T[:, :, None]
    block_grad = score_scale * pair_einsum("thd,the->hde", reached_queries, grad_heads)
    suffix_pair = entering(
        (factor, block_grad), "ctx", combine, (jnp.ones_like(factor), zero_state), True
    )
    later_state = suffix_pair[1]
    grad_scores = jnp.einsum(
        "thd,shd->hts", grad_heads, value_heads, preferred_element_type=jnp.float32
    )
    score_grad = (grad_scores * score_scale * decay_mask).astype(jnp.bfloat16)
    query_part = jnp.einsum(
        "hts,shd->thd", score_grad, key_heads, preferred_element_type=jnp.float32
    )
    query_part = query_part + score_scale * reach_in.T[:, :, None] * pair_einsum(
        "the,hde->thd", grad_heads, incoming
    )
    key_part = jnp.einsum(
        "hts,thd->shd", score_grad, query_heads, preferred_element_type=jnp.float32
    )
    key_part = key_part + exit_weight.T[:, :, None] * pair_einsum(
        "she,hde->shd", value_heads, later_state
    )
    value_part = jnp.einsum(
        "hts,the->she", attn_probs, grad_heads, preferred_element_type=jnp.float32
    )
    value_part = value_part + exit_weight.T[:, :, None] * pair_einsum(
        "shd,hde->she", key_heads, later_state
    )
    query_grad = query_part.reshape(row_count, local_width).astype(jnp.bfloat16)
    key_grad = key_part.reshape(row_count, local_width).astype(jnp.bfloat16)
    value_grad = value_part.reshape(row_count, local_width).astype(jnp.bfloat16)
    return (attn_output, query_grad, key_grad, value_grad)


def solution(mesh):
    in_specs = (
        P("ctx", "head"),
        P("ctx", "head"),
        P("ctx", "head"),
        P("head", "ctx"),
        P("head"),
        P("ctx", "head"),
        P(),
    )
    out_specs = (P("ctx", "head"), P("ctx", "head"), P("ctx", "head"), P("ctx", "head"))
    return jax.shard_map(
        on_device, mesh=mesh, in_specs=in_specs, out_specs=out_specs, check_vma=False
    )
```

profile of v0, /device:TPU:0, one launch (start us, length us, event | category | flops | bytes accessed | tf_op | source)
XLA Modules:
  0.0 394.5 jit_solution(5258561976258206439)
XLA Ops:
  15.4 1.3 convolution_add_fusion.5
  19.2 44.2 %all-reduce = f32[256]{0:T(256)S(1)} all-reduce(f32[256]{0:T(256)S(1)} %dynamic-update-slice), channel_id=2, replica_groups=mesh['ctx'=16,'head'=2] {'ctx'}, use_global_device_ids=true, to_apply=%add | all-reduce | flops 256 | bytes 2048
  66.1 1.4 fusion.2
  67.5 104.6 %all-gather.6.cloned.1.call-done = f32[256,96,96]{2,1,0:T(8,128)} async-done(((f32[16,96,96]{2,1,0:T(8,128)}), f32[256,96,96]{2,1,0:T(8,128)}) %all-gather.6.cloned.1.call-update) | async-done | bytes 9437200 | tf_op jit(solution)/shard_map/all_gather | solution.py:15
  172.8 1.5 multiply_reduce_fusion
  174.7 2.5 all-reduce.1
  177.1 1.8 fusion.24
  179.3 1.3 fusion.14
  180.7 1.4 fusion.3
  185.7 165.8 %all-gather.8.cloned.1.call-done = f32[256,96,96]{2,1,0:T(8,128)} async-done(((f32[16,96,96]{2,1,0:T(8,128)}), f32[256,96,96]{2,1,0:T(8,128)}) %all-gather.8.cloned.1.call-update) | async-done | bytes 9437200 | tf_op jit(solution)/shard_map/all_gather | solution.py:15
  351.5 30.5 %while.27 = (s32[]{:T(128)}, f32[16,96,96]{2,1,0:T(8,128)S(1)}, s32[]{:T(128)}, f32[16,16]{1,0:T(8,128)}, f32[16,16,96,96]{3,2,1,0:T(8,128)}, /*index=5*/s32[]{:T(128)}, s32[]{:T(128)}, s32[]{:T(128)}, s32[]{:T(128)}) while((s32[]{:T(128)}, f32[16,96,96]{2,1,0:T(8,128)S(1)}, s32[]{:T(128)}, f32[16,16]{1,0:T(8,128)}, ...), condition=%wide.region_11.12_spmd, body=%wide.region_10.11_spmd.sunk | while | flops 294918 | bytes 1769811 | solution.py:24
  352.2 1.3 bitcast_add_fusion.5
  354.3 1.3 bitcast_add_fusion.5
  356.3 1.3 bitcast_add_fusion.5
  358.4 1.3 bitcast_add_fusion.5
  360.4 1.3 bitcast_add_fusion.5
  362.4 1.3 bitcast_add_fusion.5
  364.5 1.3 bitcast_add_fusion.5
  366.5 1.3 bitcast_add_fusion.5
  368.5 1.3 bitcast_add_fusion.5
  370.6 1.3 bitcast_add_fusion.5
  372.6 1.3 bitcast_add_fusion.5
  382.9 1.3 fusion.18
  385.4 1.3 fusion.17
  (81 shorter events, 36.2 us)
Async XLA Ops:
  7.2 164.9 %all-gather.6.cloned.1.call-start = ((), (), s32[]{:S(2)}) async-start(), calls=%async_computation | async-start | bytes 13369344 | tf_op jit(solution)/shard_map/all_gather | solution.py:15
  11.1 161.4 %copy-start.2 = (f32[16,128]{1,0:T(8,128)}, f32[16,128]{1,0:T(8,128)S(1)}, u32[]{:S(2)}) copy-start(f32[16,128]{1,0:T(8,128)S(1)} %reduce_window_sum.18) | copy-start | bytes 24580
  16.8 157.6 %copy-start.5 = (f32[1536]{0:T(1024)S(1)}, f32[1536]{0:T(1024)}, u32[]{:S(2)}) copy-start(f32[1536]{0:T(1024)} %param.15) | copy-start | bytes 18436
  16.8 334.7 %all-gather.8.cloned.1.call-start = ((), (), s32[]{:S(2)}) async-start(), calls=%async_computation.1 | async-start | bytes 13369344 | tf_op jit(solution)/shard_map/all_gather | solution.py:15
  18.8 155.9 %copy-start.3 = (f32[128,16]{0,1:T(8,128)}, f32[128,16]{0,1:T(8,128)S(1)}, u32[]{:S(2)}) copy-start(f32[128,16]{0,1:T(8,128)S(1)} %get-tuple-element.172) | copy-start | bytes 24580
  66.1 106.4 %copy-start.4 = (f32[128,128]{1,0:T(8,128)}, f32[128,128]{1,0:T(8,128)S(1)}, u32[]{:S(2)}) copy-start(f32[128,128]{1,0:T(8,128)S(1)} %get-tuple-element.179) | copy-start | bytes 196612
  66.1 106.4 %copy-start.6 = (pred[128,128]{1,0:T(8,128)(4,1)}, pred[128,128]{1,0:T(8,128)(4,1)S(1)}, u32[]{:S(2)}) copy-start(pred[128,128]{1,0:T(8,128)(4,1)S(1)} %get-tuple-element.178) | copy-start | bytes 49156
  172.1 5.0 %copy-start.7 = (f32[16,16]{1,0:T(8,128)}, f32[16,16]{1,0:T(8,128)S(1)}, u32[]{:S(2)}) copy-start(f32[16,16]{1,0:T(8,128)S(1)} %get-tuple-element.309) | copy-start | bytes 3076
  179.0 5.8 %copy-start.1 = (bf16[128,1536]{0,1:T(8,128)(2,1)S(1)}, bf16[128,1536]{0,1:T(8,128)(2,1)}, u32[]{:S(2)}) copy-start(bf16[128,1536]{0,1:T(8,128)(2,1)} %get-tuple-element.177) | copy-start | bytes 1179652
  182.1 1.7 copy-start
Sparse Core Ops, SparseCore 0:
  16.9 155.0 all-gather.5
  180.8 170.5 all-gather.7
where the time goes:
time: 396 us; the launch traced here: 395 us
  waiting for transfers between devices  270 us (68%)
  blocking collectives  46.7 us (12%)
  other arithmetic  25.8 us (7%)
  local copies, waits for them, and re-layouts  22.3 us (6%)
  between operations  15 us (4%)
  matrix products  13.7 us (3%)
    all_gather x2, waiting for transfers between devices, entering(): gathered = jax.tree.map(lambda a: lax.all_gather(a, axis), part)  270 us
    unnamed x1, blocking collectives  44.2 us
    add x15, other arithmetic, combine(): later_pair[0][:, None, None] * earlier[1] + later_pair[1]  19.6 us
    mul x15, local copies, waits for them, and re-layouts, combine(): later_pair[0][:, None, None] * earlier[1] + later_pair[1]  10.3 us
    unnamed x27, local copies, waits for them, and re-layouts  10.1 us
  transfers between devices with their start and end apart: 2, of which 2 were waited for; matrix products, arithmetic and copies ran while one was open for 3% of the time, Pallas kernels for 0%

commit v1 on v0

v1 whole, which is shorter than its diff:
```python
import functools
import math

import jax
import jax.numpy as jnp
from jax import lax
from jax.experimental import pallas as pl
from jax.experimental.pallas import tpu as pltpu
from jax.sharding import PartitionSpec as P

EPSILON = 1e-06
NEVER = -1e30
F32 = jnp.float32
BF16 = jnp.bfloat16
NN = (((1,), (0,)), ((), ()))
NT = (((1,), (1,)), ((), ()))
TN = (((0,), (0,)), ((), ()))


def dot(a, b, dims=NN):
    return lax.dot_general(a, b, dims, preferred_element_type=F32)


def split3(x):
    a = x.astype(BF16)
    rest = x - a.astype(F32)
    b = rest.astype(BF16)
    return a, b, (rest - b.astype(F32)).astype(BF16)


def exact_dot(x, ones, dims, x_first):
    out = None
    for part in split3(x):
        term = dot(part, ones, dims) if x_first else dot(ones, part, dims)
        out = term if out is None else out + term
    return out


class Plan:
    def __init__(self, tokens, width, heads, pieces):
        self.tokens, self.width, self.heads = tokens, width, heads
        self.dim = width // heads
        self.group = math.lcm(self.dim, 128) // self.dim
        self.lanes = self.group * self.dim
        self.groups = heads // self.group
        self.pieces = pieces
        self.rows = self.dim // pieces
        self.tiles = width // 128
        self.scale = 1.0 / math.sqrt(self.dim)
        self.piece_rows = self.tiles * self.rows
        self.factor_rows = -(-self.tiles // 8) * 8


def iota(shape, dim):
    return lax.broadcasted_iota(jnp.int32, shape, dim)


def tri(n, keep):
    return keep(iota((n, n), 0), iota((n, n), 1)).astype(F32).astype(BF16)


def head_mask(plan, k):
    lane = iota((1, plan.lanes), 1)
    return (lane >= k * plan.dim) & (lane < (k + 1) * plan.dim)


def spread(plan, columns):
    head, lane = iota((plan.heads, plan.width), 0), iota((plan.heads, plan.width), 1)
    ones = ((lane >= head * plan.dim) & (lane < (head + 1) * plan.dim)).astype(F32).astype(BF16)
    high = columns.astype(BF16)
    low = (columns - high.astype(F32)).astype(BF16)
    return dot(high, ones) + dot(low, ones)


def doc_edges(plan, lengths_ref, block_start):
    start = jnp.int32(0)
    last, first = jnp.int32(0), jnp.int32(2**30)
    for i in range(lengths_ref.shape[0]):
        last = jnp.where(start < block_start + plan.tokens, start, last)
        first = jnp.where(start >= block_start, jnp.minimum(first, start), first)
        start = start + lengths_ref[i]
    return last, first


def doc_index(lengths_ref, positions):
    start = jnp.int32(0)
    index = jnp.zeros(positions.shape, jnp.int32)
    for i in range(lengths_ref.shape[0]):
        index = index + (positions >= start).astype(jnp.int32)
        start = start + lengths_ref[i]
    return index


def exit_columns(plan, decay, last, block_start):
    after = tri(plan.tokens, lambda t, u: u > t)
    keep = block_start + iota((plan.tokens, plan.heads), 0) >= last
    return jnp.where(keep, jnp.exp(exact_dot(decay, after, NT, False)), 0.0)


def reach_columns(plan, decay, first, block_start):
    until = tri(plan.tokens, lambda t, u: u <= t)
    carry = block_start + iota((plan.tokens, plan.heads), 0) < first
    return jnp.where(carry, jnp.exp(exact_dot(decay, until, NT, False)), 0.0)


def decay_bias(plan, lengths_ref, block_start):
    n = plan.tokens
    t, s = iota((n, n), 0), iota((n, n), 1)
    same = doc_index(lengths_ref, t + block_start) == doc_index(lengths_ref, s + block_start)
    return jnp.where(same & (t >= s), math.log(plan.scale), NEVER)


def log_sums(plan, decay):
    until = tri(plan.tokens, lambda t, u: u <= t)
    return exact_dot(decay, until, NT, False), exact_dot(decay, until, NT, True)


def own_heads(plan, product, rows):
    out = product[:rows]
    for k in range(1, plan.group):
        out = jnp.where(head_mask(plan, k), product[k * rows : (k + 1) * rows], out)
    return out


def stack_heads(plan, x):
    return jnp.concatenate(
        [jnp.where(head_mask(plan, k), x, jnp.zeros_like(x)) for k in range(plan.group)], axis=0
    )


def lanes_of(plan, g):
    return slice(g * plan.lanes, (g + 1) * plan.lanes)


def store_pieces(plan, mine, state_ref, piece_refs):
    for m, piece in enumerate(piece_refs):
        start = pl.multiple_of((mine ^ m) * plan.rows, plan.rows)
        for j in range(plan.tiles):
            piece[j * plan.rows : (j + 1) * plan.rows, :] = state_ref[
                pl.ds(start, plan.rows), j * 128 : (j + 1) * 128
            ]


def load_pieces(plan, mine, piece_refs, state_ref):
    for m, piece in enumerate(piece_refs):
        start = pl.multiple_of((mine ^ m) * plan.rows, plan.rows)
        for j in range(plan.tiles):
            state_ref[pl.ds(start, plan.rows), j * 128 : (j + 1) * 128] = piece[
                j * plan.rows : (j + 1) * plan.rows, :
            ]


def exit_kernel(plan, place_ref, lengths_ref, decay_ref, keys_ref, values_ref, *refs):
    pieces, (weighted_ref, state_ref) = refs[: plan.pieces], refs[plan.pieces :]
    block_start, mine = place_ref[0], place_ref[1]
    last, first = doc_edges(plan, lengths_ref, block_start)
    decay = decay_ref[...]
    weights = spread(plan, exit_columns(plan, decay, last, block_start))
    for g in range(plan.groups):
        at = lanes_of(plan, g)
        weighted = (keys_ref[:, at].astype(F32) * weights[:, at]).astype(BF16)
        weighted_ref[:, at] = weighted
        state_ref[:, at] = own_heads(plan, dot(weighted, values_ref[:, at], TN), plan.dim)
    store_pieces(plan, mine, state_ref, pieces)
    whole = jnp.exp(jnp.sum(decay, axis=1, keepdims=True))
    whole = jnp.where(first >= block_start + plan.tokens, whole, 0.0)
    head = iota((plan.heads, 128), 0)
    rows = []
    for j in range(plan.tiles):
        lane = iota((plan.heads, 128), 1) + j * 128
        on = (lane >= head * plan.dim) & (lane < (head + 1) * plan.dim)
        rows.append(jnp.sum(jnp.where(on, whole, 0.0), axis=0, keepdims=True))
    rows.append(jnp.zeros((plan.factor_rows - plan.tiles, 128), F32))
    rows = jnp.concatenate(rows, axis=0)
    for piece in pieces:
        piece[plan.piece_rows :, :] = rows


def chain_kernel(plan, reverse, with_carry, place_ref, *refs):
    n = plan.pieces
    pieces, factors = refs[:n], refs[n : 2 * n]
    mine = place_ref[1]
    rows = plan.rows
    order = range(n - 1, -1, -1) if reverse else range(n)
    slot = [mine ^ j for j in range(n)]
    state_scratch, factor_scratch = refs[-2], refs[-1]
    for m in range(n):
        state_scratch[mine ^ m] = pieces[m][: plan.piece_rows, :]
        factor_scratch[mine ^ m] = factors[m][-plan.factor_rows :, :]
    if with_carry:
        held = refs[2 * n][...]
        outs_ref = refs[-3]
    else:
        held = jnp.zeros((plan.piece_rows, 128), F32)
        outs_ref = None
    tiles = [held[j * rows : (j + 1) * rows] for j in range(plan.tiles)]
    for step, b in enumerate(order):
        if with_carry:
            for j in range(plan.tiles):
                outs_ref[b, j * rows : (j + 1) * rows, :] = tiles[j]
            if step == n - 1:
                break
        for j in range(plan.tiles):
            tiles[j] = (
                tiles[j] * factor_scratch[b, j : j + 1, :]
                + state_scratch[b, j * rows : (j + 1) * rows, :]
            )
    if with_carry:
        outs = refs[2 * n + 1 : 3 * n + 1]
        for m in range(n):
            outs[m][...] = outs_ref[mine ^ m]
    else:
        for j in range(plan.tiles):
            refs[2 * n][j * rows : (j + 1) * rows, :] = tiles[j]


def local_kernel(
    plan, place_ref, lengths_ref, decay_ref, queries_ref, keys_ref, values_ref, probs_ref, local_ref, reached_ref
):
    block_start = place_ref[0]
    decay = decay_ref[...]
    last, first = doc_edges(plan, lengths_ref, block_start)
    columns, rows = log_sums(plan, decay)
    bias = decay_bias(plan, lengths_ref, block_start)
    carry = block_start + iota(columns.shape, 0) < first
    reach = spread(plan, jnp.where(carry, jnp.exp(columns), 0.0) * plan.scale)
    n = plan.tokens
    for g in range(plan.groups):
        at = lanes_of(plan, g)
        queries, keys, values = queries_ref[:, at], keys_ref[:, at], values_ref[:, at]
        reached_ref[:, at] = (queries.astype(F32) * reach[:, at]).astype(BF16)
        scores = dot(stack_heads(plan, queries), keys, NT)
        probs = []
        for k in range(plan.group):
            h = g * plan.group + k
            mask = jnp.exp(columns[:, h : h + 1] - rows[h : h + 1, :] + bias)
            probs.append((scores[k * n : (k + 1) * n] * mask).astype(BF16))
        probs = jnp.concatenate(probs, axis=1)
        probs_ref[:, g * plan.group * n : (g + 1) * plan.group * n] = probs
        local_ref[:, at] = dot(probs, stack_heads(plan, values))


def attend_kernel(plan, place_ref, local_ref, reached_ref, out_grad_ref, gain_ref, *refs):
    pieces = refs[: plan.pieces]
    attended_ref, sums_ref, incoming_ref, state_ref = refs[plan.pieces :]
    load_pieces(plan, place_ref[1], pieces, state_ref)
    squares = inner = None
    for g in range(plan.groups):
        at = lanes_of(plan, g)
        incoming = state_ref[:, at].astype(BF16)
        incoming_ref[:, at] = incoming
        attended = local_ref[:, at] + dot(reached_ref[:, at], stack_heads(plan, incoming))
        attended_ref[:, at] = attended
        grad = out_grad_ref[:, at].astype(F32) * gain_ref[:, at]
        square, product = attended * attended, grad * attended
        for j in range(0, plan.lanes, 128):
            squares = square[:, j : j + 128] if squares is None else squares + square[:, j : j + 128]
            inner = product[:, j : j + 128] if inner is None else inner + product[:, j : j + 128]
    lane = iota((plan.tokens, 128), 1)
    sums_ref[...] = jnp.where(
        lane < 64, jnp.sum(squares, axis=1, keepdims=True), jnp.sum(inner, axis=1, keepdims=True)
    )


def grad_kernel(
    plan, features, place_ref, attended_ref, out_grad_ref, gain_ref, sums_ref, other_ref, reached_ref, *refs
):
    pieces, (attended_grad_ref, norm_ref, state_ref) = refs[: plan.pieces], refs[plan.pieces :]
    sums = sums_ref[...] + other_ref[...]
    inverse = lax.rsqrt(sums[:, :1] / features + EPSILON)
    norm_ref[...] = jnp.broadcast_to(inverse, norm_ref.shape)
    slope = inverse * inverse * inverse * sums[:, 64:65] / features
    for g in range(plan.groups):
        at = lanes_of(plan, g)
        grad = out_grad_ref[:, at].astype(F32) * gain_ref[:, at]
        attended_grad = (grad * inverse - attended_ref[:, at] * slope).astype(BF16)
        attended_grad_ref[:, at] = attended_grad
        state_ref[:, at] = own_heads(plan, dot(reached_ref[:, at], attended_grad, TN), plan.dim)
    store_pieces(plan, place_ref[1], state_ref, pieces)


def inner_kernel(
    plan,
    place_ref,
    lengths_ref,
    decay_ref,
    queries_ref,
    keys_ref,
    values_ref,
    gain_ref,
    attended_ref,
    attended_grad_ref,
    norm_ref,
    probs_ref,
    incoming_ref,
    output_ref,
    query_grad_ref,
    key_local_ref,
    value_local_ref,
    weighted_ref,
):
    block_start = place_ref[0]
    decay = decay_ref[...]
    last, first = doc_edges(plan, lengths_ref, block_start)
    columns, rows = log_sums(plan, decay)
    bias = decay_bias(plan, lengths_ref, block_start)
    position = block_start + iota(columns.shape, 0)
    reach = spread(plan, jnp.where(position < first, jnp.exp(columns), 0.0) * plan.scale)
    exits = spread(plan, exit_columns(plan, decay, last, block_start))
    norm = norm_ref[:, :1]
    n = plan.tokens
    for g in range(plan.groups):
        at = lanes_of(plan, g)
        output_ref[:, at] = (attended_ref[:, at] * norm * gain_ref[:, at]).astype(BF16)
        queries, keys, values = queries_ref[:, at], keys_ref[:, at], values_ref[:, at]
        grads = attended_grad_ref[:, at]
        weighted_ref[:, at] = (values.astype(F32) * exits[:, at]).astype(BF16)
        scores = dot(stack_heads(plan, grads), values, NT)
        score_grads = []
        for k in range(plan.group):
            h = g * plan.group + k
            mask = jnp.exp(columns[:, h : h + 1] - rows[h : h + 1, :] + bias)
            score_grads.append((scores[k * n : (k + 1) * n] * mask).astype(BF16))
        score_grads = jnp.concatenate(score_grads, axis=1)
        probs = probs_ref[:, g * plan.group * n : (g + 1) * plan.group * n]
        query_grad = dot(score_grads, stack_heads(plan, keys))
        query_grad += reach[:, at] * dot(grads, stack_heads(plan, incoming_ref[:, at]), NT)
        query_grad_ref[:, at] = query_grad.astype(BF16)
        key_local_ref[:, at] = own_heads(plan, dot(score_grads, queries, TN), n)
        value_local_ref[:, at] = own_heads(plan, dot(probs, grads, TN), n)


def finish_kernel(
    plan, place_ref, key_local_ref, value_local_ref, weighted_values_ref, weighted_keys_ref, *refs
):
    pieces, (key_grad_ref, value_grad_ref, state_ref) = refs[: plan.pieces], refs[plan.pieces :]
    load_pieces(plan, place_ref[1], pieces, state_ref)
    for g in range(plan.groups):
        at = lanes_of(plan, g)
        later = stack_heads(plan, state_ref[:, at].astype(BF16))
        key_grad = key_local_ref[:, at] + dot(weighted_values_ref[:, at], later, NT)
        key_grad_ref[:, at] = key_grad.astype(BF16)
        value_grad = value_local_ref[:, at] + dot(weighted_keys_ref[:, at], later)
        value_grad_ref[:, at] = value_grad.astype(BF16)


SCALAR = pl.BlockSpec(memory_space=pltpu.SMEM)
WHOLE = pl.BlockSpec(memory_space=pltpu.VMEM)


def call(kernel, name, scalars, arrays, outs, scratch=(), flops=0):
    moved = sum(a.size * a.dtype.itemsize for a in (*arrays, *outs))
    return pl.pallas_call(
        kernel,
        name=name,
        out_shape=outs,
        in_specs=[SCALAR] * len(scalars) + [WHOLE] * len(arrays),
        out_specs=[WHOLE] * len(outs),
        scratch_shapes=list(scratch),
        compiler_params=pltpu.CompilerParams(vmem_limit_bytes=40 * 2**20),
        cost_estimate=pl.CostEstimate(flops=flops, bytes_accessed=moved, transcendentals=0),
    )(*scalars, *arrays)


def array(*shape, dtype=F32):
    return jax.ShapeDtypeStruct(shape, dtype)


def exchange(pieces, count):
    return [pieces[0]] + [
        lax.ppermute(piece, "ctx", [(i, i ^ m) for i in range(count)])
        for m, piece in enumerate(pieces)
        if m
    ]


def shift(x, count, by):
    pairs = [(i, i + by) for i in range(count) if 0 <= i + by < count]
    return lax.ppermute(x, "ctx", pairs)


def scan_whole(plan, state, factor, count, reach, sign):
    held = shift(state, count, sign)
    rates = shift(factor, count, sign)
    by = 1
    while by < reach:
        held = held + rates * shift(held, count, sign * by)
        rates = rates * shift(rates, count, sign * by)
        by *= 2
    return held


def on_device(queries, keys, values, decay_log, norm_gain, out_grad, doc_lengths):
    tokens, width = queries.shape
    heads = decay_log.shape[0]
    count = lax.axis_size("ctx")
    features = width * lax.axis_size("head")
    reach = count // 4
    even = reach & (reach - 1) == 0 and (width // heads) % (8 * reach) == 0
    plan = Plan(tokens, width, heads, reach if even else 1)
    n = plan.pieces
    index = lax.axis_index("ctx")
    place = jnp.stack([index * tokens, index % n]).astype(jnp.int32)
    gain = norm_gain.reshape(1, width)
    like = array(tokens, width, dtype=BF16)
    wide = array(tokens, width)
    state = pltpu.VMEM((plan.dim, width), F32)
    piece = array(plan.piece_rows, 128)
    framed = array(plan.piece_rows + plan.factor_rows, 128)

    *pieces, weighted_keys = call(
        functools.partial(exit_kernel, plan),
        "exit_states",
        (place, doc_lengths),
        (decay_log, keys, values),
        [framed] * n + [like],
        [state],
        flops=10**8,
    )
    if even:
        pieces = exchange(pieces, count)
    frames = pieces

    def chain(pieces, reverse, carry=None):
        with_carry = carry is not None
        scratch = [pltpu.VMEM((n, plan.piece_rows, 128), F32), pltpu.VMEM((n, plan.factor_rows, 128), F32)]
        if with_carry:
            scratch = [pltpu.VMEM((n, plan.piece_rows, 128), F32)] + scratch
        return call(
            functools.partial(chain_kernel, plan, reverse, with_carry),
            "prefix_states" if with_carry else "total_state",
            (place,),
            (*pieces, *frames, carry) if with_carry else (*pieces, *frames),
            [piece] * n if with_carry else [piece],
            scratch,
        )

    def entering(pieces, reverse):
        sign = -1 if reverse else 1
        if not even:
            whole = pieces[0][: plan.piece_rows].reshape(plan.tiles, plan.rows, 128)
            factor = frames[0][plan.piece_rows : plan.piece_rows + plan.tiles, None, :]
            return [scan_whole(plan, whole, factor, count, reach, sign).reshape(piece.shape)]
        (total,) = chain(pieces, reverse)
        carry = shift(total, count, sign * n)
        return exchange(chain(pieces, reverse, carry), count)

    incoming = entering(pieces, False)
    probs, local, reached = call(
        functools.partial(local_kernel, plan),
        "local_attention",
        (place, doc_lengths),
        (decay_log, queries, keys, values),
        [array(tokens, heads * tokens, dtype=BF16), wide, like],
        flops=10**9,
    )
    attended, sums, incoming_state = call(
        functools.partial(attend_kernel, plan),
        "attended",
        (place,),
        (local, reached, out_grad, gain, *incoming),
        [wide, array(tokens, 128), array(plan.dim, width, dtype=BF16)],
        [state],
    )
    other = lax.ppermute(sums, "head", [(0, 1), (1, 0)])
    *pieces, attended_grad, norm = call(
        functools.partial(grad_kernel, plan, features),
        "attended_grad",
        (place,),
        (attended, out_grad, gain, sums, other, reached),
        [piece] * n + [like, array(tokens, 128)],
        [state],
    )
    if even:
        pieces = exchange(pieces, count)
    later = entering(pieces, True)
    output, query_grad, key_local, value_local, weighted_values = call(
        functools.partial(inner_kernel, plan),
        "local_grads",
        (place, doc_lengths),
        (
            decay_log,
            queries,
            keys,
            values,
            gain,
            attended,
            attended_grad,
            norm,
            probs,
            incoming_state,
        ),
        [like, like, wide, wide, like],
        flops=10**9,
    )
    key_grad, value_grad = call(
        functools.partial(finish_kernel, plan),
        "key_value_grads",
        (place,),
        (key_local, value_local, weighted_values, weighted_keys, *later),
        [like, like],
        [state],
    )
    return (output, query_grad, key_grad, value_grad)


def solution(mesh):
    in_specs = (
        P("ctx", "head"),
        P("ctx", "head"),
        P("ctx", "head"),
        P("head", "ctx"),
        P("head"),
        P("ctx", "head"),
        P(),
    )
    out_specs = (P("ctx", "head"), P("ctx", "head"), P("ctx", "head"), P("ctx", "head"))
    return jax.shard_map(
        on_device, mesh=mesh, in_specs=in_specs, out_specs=out_specs, check_vma=False
    )
```

time: 396 us -> 66.5 us (0.17)
  waiting for transfers between devices: 270 us -> 27.5 us
  blocking collectives: 46.7 us -> 0 us
  other arithmetic: 25.8 us -> 0.08 us
  starting transfers between devices: 0.08 us -> 20.2 us
  local copies, waits for them, and re-layouts: 22.3 us -> 2.63 us
  Pallas kernels: 0 us -> 15.1 us
  between operations: 15 us -> 0.82 us
  matrix products: 13.7 us -> 0 us
    all_gather x2 -> x0, waiting for transfers between devices: 270 us -> none  [entering(): gathered = jax.tree.map(lambda a: lax.all_gather(a, axis), part)]
    unnamed x1 -> x0, blocking collectives: 44.2 us -> none
    ppermute x0 -> x15, waiting for transfers between devices: none -> 27.5 us  [the longest x12 17.4 us: exchange(): lax.ppermute(piece, 'ctx', [(i, i ^ m) for i in range(count)])]
    ppermute x0 -> x15, starting transfers between devices: none -> 20.2 us  [the longest x12 15.2 us: exchange(): lax.ppermute(piece, 'ctx', [(i, i ^ m) for i in range(count)])]
    add x16 -> x0, other arithmetic: 19.7 us -> none  [the longest x15 19.6 us: combine(): later_pair[0][:, None, None] * earlier[1] + later_pair[1]]
    pallas_call x0 -> x10, Pallas kernels: none -> 15.1 us  [call(): pl.pallas_call(kernel, name=name, out_shape=outs, in_specs=[SCALAR] * len...]
    dot_general x18 -> x0, matrix products: 13.7 us -> none  [the longest x2 2.64 us: pair_einsum(): jnp.einsum(form, low, second, preferred_element_type=jnp.float32)]
    mul x15 -> x0, local copies, waits for them, and re-layouts: 10.3 us -> none  [combine(): later_pair[0][:, None, None] * earlier[1] + later_pair[1]]
  transfers between devices with their start and end apart: 2 -> 15, of which waited for: 2 -> 11; matrix products, arithmetic and copies ran while one was open for 3% -> 0% of each run, Pallas kernels for 0% -> 10%
where the time goes in v1:
time: 66.5 us; the launch traced here: 66.3 us
  waiting for transfers between devices  27.5 us (41%)
  starting transfers between devices  20.2 us (30%)
  Pallas kernels  15.1 us (23%)
  local copies, waits for them, and re-layouts  2.63 us (4%)
  between operations  0.82 us (1%)
    ppermute x12, waiting for transfers between devices, exchange(): lax.ppermute(piece, 'ctx', [(i, i ^ m) for i in range(count)])  17.4 us
    ppermute x12, starting transfers between devices, exchange(): lax.ppermute(piece, 'ctx', [(i, i ^ m) for i in range(count)])  15.2 us
    pallas_call x10, Pallas kernels, call(): pl.pallas_call(kernel, name=name, out_shape=outs, in_specs=[SCALAR] * len...  15.1 us
    ppermute x2, waiting for transfers between devices, shift(): return lax.ppermute(x, 'ctx', pairs)  8.84 us
    ppermute x2, starting transfers between devices, shift(): return lax.ppermute(x, 'ctx', pairs)  4.92 us
    unnamed x18, local copies, waits for them, and re-layouts  2.62 us
  transfers between devices with their start and end apart: 15, of which 11 were waited for; matrix products, arithmetic and copies ran while one was open for 0% of the time, Pallas kernels for 10%

profile of v1, /device:TPU:0, one launch (start us, length us, event | category | flops | bytes accessed | tf_op | source)
XLA Modules:
  0.0 66.3 jit_solution(177585352805364083)
XLA Ops:
  3.3 1.6 %exit_states.1 = (f32[304,128]{1,0:T(8,128)S(1)}, f32[304,128]{1,0:T(8,128)S(1)}, f32[304,128]{1,0:T(8,128)S(1)}, f32[304,128]{1,0:T(8,128)S(1)}, bf16[128,1536]{1,0:T(8,128)(2,1)S(1)}) custom-call(s32[2]{0:T(128)S(1)} %pad_add_fusion.place_ref, s32[16]{0:T(128)S(1)} %copy-done.6, f32[16,128]{1,0:T(8,128)S(1)} %copy-done.5, bf16[128,1536]{1,0:T(8,128)(2,1)S(1)} %copy-done.1, ...), custom_call_target="tpu_custom_call" | custom-call | flops 100000000 | bytes 1810432 | tf_op jit(solution)/shard_map/exit_states/pallas_call | solution.py:353
  4.9 3.0 %collective-permute-start = (f32[304,128]{1,0:T(8,128)S(1)}, f32[304,128]{1,0:T(8,128)S(1)}, u32[]{:S(2)}, u32[]{:S(2)}) collective-permute-start(f32[304,128]{1,0:T(8,128)S(1)} %get-tuple-element.39), channel_id=1, source_target_pairs={{0,2},{2,0},{4,6},{6,4},{8,10},{10,8},{12,14},{14,12},{16,18},{18,... | collective-permute-start | bytes 466952 | tf_op jit(solution)/shard_map/ppermute | solution.py:371
  7.9 1.5 %collective-permute-start.1 = (f32[304,128]{1,0:T(8,128)S(1)}, f32[304,128]{1,0:T(8,128)S(1)}, u32[]{:S(2)}, u32[]{:S(2)}) collective-permute-start(f32[304,128]{1,0:T(8,128)S(1)} %get-tuple-element.40), channel_id=1, source_target_pairs={{0,4},{2,6},{4,0},{6,2},{8,12},{10,14},{12,8},{14,10},{16,20},{18,... | collective-permute-start | bytes 466952 | tf_op jit(solution)/shard_map/ppermute | solution.py:371
  9.5 3.1 %collective-permute-done.refs_1_.refs_5_ = f32[304,128]{1,0:T(8,128)S(1)} collective-permute-done((f32[304,128]{1,0:T(8,128)S(1)}, f32[304,128]{1,0:T(8,128)S(1)}, u32[]{:S(2)}, u32[]{:S(2)}) %collective-permute-start) | collective-permute-done | bytes 155680 | tf_op jit(solution)/shard_map/ppermute | solution.py:371
  12.6 4.2 %collective-permute-done.1.refs_2_.refs_6_ = f32[304,128]{1,0:T(8,128)S(1)} collective-permute-done((f32[304,128]{1,0:T(8,128)S(1)}, f32[304,128]{1,0:T(8,128)S(1)}, u32[]{:S(2)}, u32[]{:S(2)}) %collective-permute-start.1) | collective-permute-done | bytes 155680 | tf_op jit(solution)/shard_map/ppermute | solution.py:371
  17.4 3.6 %collective-permute-start.3 = (f32[288,128]{1,0:T(8,128)S(1)}, f32[288,128]{1,0:T(8,128)S(1)}, u32[]{:S(2)}, u32[]{:S(2)}) collective-permute-start(f32[288,128]{1,0:T(8,128)S(1)} %total_state.2), channel_id=1, source_target_pairs={{0,8},{2,10},{4,12},{6,14},{8,16},{10,18},{12,20},{14,22},{16,24},... | collective-permute-start | bytes 442376 | tf_op jit(solution)/shard_map/ppermute | solution.py:379
  21.0 2.6 %collective-permute-done.3.refs_8_ = f32[288,128]{1,0:T(8,128)S(1)} collective-permute-done((f32[288,128]{1,0:T(8,128)S(1)}, f32[288,128]{1,0:T(8,128)S(1)}, u32[]{:S(2)}, u32[]{:S(2)}) %collective-permute-start.3) | collective-permute-done | bytes 147488 | tf_op jit(solution)/shard_map/ppermute | solution.py:379
  24.4 1.3 %collective-permute-start.4 = (f32[288,128]{1,0:T(8,128)S(1)}, f32[288,128]{1,0:T(8,128)S(1)}, u32[]{:S(2)}, u32[]{:S(2)}) collective-permute-start(f32[288,128]{1,0:T(8,128)S(1)} %get-tuple-element.43), channel_id=1, source_target_pairs={{0,2},{2,0},{4,6},{6,4},{8,10},{10,8},{12,14},{14,12},{16,18},{18,... | collective-permute-start | bytes 442376 | tf_op jit(solution)/shard_map/ppermute | solution.py:371
  26.5 1.4 %collective-permute-start.6 = (f32[288,128]{1,0:T(8,128)S(1)}, f32[288,128]{1,0:T(8,128)S(1)}, u32[]{:S(2)}, u32[]{:S(2)}) collective-permute-start(f32[288,128]{1,0:T(8,128)S(1)} %get-tuple-element.45), channel_id=1, source_target_pairs={{0,6},{2,4},{4,2},{6,0},{8,14},{10,12},{12,10},{14,8},{16,22},{18,... | collective-permute-start | bytes 442376 | tf_op jit(solution)/shard_map/ppermute | solution.py:371
  28.0 2.2 %local_attention.1 = (bf16[128,2048]{1,0:T(8,128)(2,1)S(1)}, f32[128,1536]{1,0:T(8,128)S(1)}, bf16[128,1536]{1,0:T(8,128)(2,1)S(1)}) custom-call(s32[2]{0:T(128)S(1)} %pad_add_fusion.place_ref, s32[16]{0:T(128)S(1)} %copy-done.6, f32[16,128]{1,0:T(8,128)S(1)} %copy-done.5, bf16[128,1536]{1,0:T(8,128)(2,1)S(1)} %copy-done.7, bf16[128,1536]{1,0:T(8,128)(2,1)S(1)} %copy-done.2, ...), custom_call_target="tpu_custom_call" | custom-call | flops 1000000000 | bytes 2891776 | tf_op jit(solution)/shard_map/local_attention/pallas_call | solution.py:353
  30.8 1.7 %collective-permute-done.6.refs_3_ = f32[288,128]{1,0:T(8,128)S(1)} collective-permute-done((f32[288,128]{1,0:T(8,128)S(1)}, f32[288,128]{1,0:T(8,128)S(1)}, u32[]{:S(2)}, u32[]{:S(2)}) %collective-permute-start.6) | collective-permute-done | bytes 147488 | tf_op jit(solution)/shard_map/ppermute | solution.py:371
  32.5 1.1 %attended.1 = (f32[128,1536]{1,0:T(8,128)S(1)}, f32[128,128]{1,0:T(8,128)S(1)}, bf16[96,1536]{1,0:T(8,128)(2,1)S(1)}) custom-call(s32[2]{0:T(128)S(1)} %pad_add_fusion.place_ref, f32[128,1536]{1,0:T(8,128)S(1)} %get-tuple-element.36.local_ref, bf16[128,1536]{1,0:T(8,128)(2,1)S(1)} %get-tuple-element.37.reached_ref, bf16[128,1536]{1,0:T(8,128)(2,1)S(1)} %copy-done, ...), custom_call_target="tpu_custom_call" | custom-call | bytes 3315712 | tf_op jit(solution)/shard_map/attended/pallas_call | solution.py:353
  33.7 1.2 %collective-permute-done.7.other_ref = f32[128,128]{1,0:T(8,128)S(1)} collective-permute-done((f32[128,128]{1,0:T(8,128)S(1)}, f32[128,128]{1,0:T(8,128)S(1)}, u32[]{:S(2)}, u32[]{:S(2)}) %collective-permute-start.7) | collective-permute-done | bytes 65568 | tf_op jit(solution)/shard_map/ppermute | solution.py:465
  35.0 1.2 %attended_grad.1 = (f32[288,128]{1,0:T(8,128)S(1)}, f32[288,128]{1,0:T(8,128)S(1)}, f32[288,128]{1,0:T(8,128)S(1)}, f32[288,128]{1,0:T(8,128)S(1)}, bf16[128,153...) custom-call(s32[2]{0:T(128)S(1)} %pad_add_fusion.place_ref, f32[128,1536]{1,0:T(8,128)S(1)} %get-tuple-element.46.attended_ref, ...), custom_call_target="tpu_custom_call" | custom-call | bytes 2758656 | tf_op jit(solution)/shard_map/attended_grad/pallas_call | solution.py:353
  36.2 1.6 %collective-permute-start.8 = (f32[288,128]{1,0:T(8,128)S(1)}, f32[288,128]{1,0:T(8,128)S(1)}, u32[]{:S(2)}, u32[]{:S(2)}) collective-permute-start(f32[288,128]{1,0:T(8,128)S(1)} %get-tuple-element.59), channel_id=1, source_target_pairs={{0,2},{2,0},{4,6},{6,4},{8,10},{10,8},{12,14},{14,12},{16,18},{18,... | collective-permute-start | bytes 442376 | tf_op jit(solution)/shard_map/ppermute | solution.py:371
  38.5 1.3 %collective-permute-start.10 = (f32[288,128]{1,0:T(8,128)S(1)}, f32[288,128]{1,0:T(8,128)S(1)}, u32[]{:S(2)}, u32[]{:S(2)}) collective-permute-start(f32[288,128]{1,0:T(8,128)S(1)} %get-tuple-element.61), channel_id=1, source_target_pairs={{0,6},{2,4},{4,2},{6,0},{8,14},{10,12},{12,10},{14,8},{16,22},{18,... | collective-permute-start | bytes 442376 | tf_op jit(solution)/shard_map/ppermute | solution.py:371
  39.8 3.1 %collective-permute-done.8.refs_1_ = f32[288,128]{1,0:T(8,128)S(1)} collective-permute-done((f32[288,128]{1,0:T(8,128)S(1)}, f32[288,128]{1,0:T(8,128)S(1)}, u32[]{:S(2)}, u32[]{:S(2)}) %collective-permute-start.8) | collective-permute-done | bytes 147488 | tf_op jit(solution)/shard_map/ppermute | solution.py:371
  42.9 3.7 %collective-permute-done.9.refs_2_ = f32[288,128]{1,0:T(8,128)S(1)} collective-permute-done((f32[288,128]{1,0:T(8,128)S(1)}, f32[288,128]{1,0:T(8,128)S(1)}, u32[]{:S(2)}, u32[]{:S(2)}) %collective-permute-start.9) | collective-permute-done | bytes 147488 | tf_op jit(solution)/shard_map/ppermute | solution.py:371
  47.2 1.3 %collective-permute-start.11 = (f32[288,128]{1,0:T(8,128)S(1)}, f32[288,128]{1,0:T(8,128)S(1)}, u32[]{:S(2)}, u32[]{:S(2)}) collective-permute-start(f32[288,128]{1,0:T(8,128)S(1)} %total_state.3), channel_id=1, source_target_pairs={{8,0},{10,2},{12,4},{14,6},{16,8},{18,10},{20,12},{22,14},{24,16},... | collective-permute-start | bytes 442376 | tf_op jit(solution)/shard_map/ppermute | solution.py:379
  48.5 6.2 %collective-permute-done.11.refs_8_ = f32[288,128]{1,0:T(8,128)S(1)} collective-permute-done((f32[288,128]{1,0:T(8,128)S(1)}, f32[288,128]{1,0:T(8,128)S(1)}, u32[]{:S(2)}, u32[]{:S(2)}) %collective-permute-start.11) | collective-permute-done | bytes 147488 | tf_op jit(solution)/shard_map/ppermute | solution.py:379
  56.1 1.3 %collective-permute-start.13 = (f32[288,128]{1,0:T(8,128)S(1)}, f32[288,128]{1,0:T(8,128)S(1)}, u32[]{:S(2)}, u32[]{:S(2)}) collective-permute-start(f32[288,128]{1,0:T(8,128)S(1)} %get-tuple-element.64), channel_id=1, source_target_pairs={{0,4},{2,6},{4,0},{6,2},{8,12},{10,14},{12,8},{14,10},{16,20},{18,... | collective-permute-start | bytes 442376 | tf_op jit(solution)/shard_map/ppermute | solution.py:371
  57.4 1.5 %collective-permute-start.14 = (f32[288,128]{1,0:T(8,128)S(1)}, f32[288,128]{1,0:T(8,128)S(1)}, u32[]{:S(2)}, u32[]{:S(2)}) collective-permute-start(f32[288,128]{1,0:T(8,128)S(1)} %get-tuple-element.65), channel_id=1, source_target_pairs={{0,6},{2,4},{4,2},{6,0},{8,14},{10,12},{12,10},{14,8},{16,22},{18,... | collective-permute-start | bytes 442376 | tf_op jit(solution)/shard_map/ppermute | solution.py:371
  58.9 4.1 %local_grads.1 = (bf16[128,1536]{1,0:T(8,128)(2,1)}, bf16[128,1536]{1,0:T(8,128)(2,1)}, f32[128,1536]{1,0:T(8,128)S(1)}, f32[128,1536]{1,0:T(8,128)S(1)}, bf16[128,1536]{1,0:T(8,128)(2,1)S(1)}) custom-call(s32[2]{0:T(128)S(1)} %pad_add_fusion.place_ref, s32[16]{0:T(128)S(1)} %copy-done.6, f32[16,128]{1,0:T(8,128)S(1)} %copy-done.5, ...), custom_call_target="tpu_custom_call" | custom-call | flops 1000000000 | bytes 6010880 | tf_op jit(solution)/shard_map/local_grads/pallas_call | solution.py:353
  64.0 2.2 %key_value_grads.1 = (bf16[128,1536]{1,0:T(8,128)(2,1)}, bf16[128,1536]{1,0:T(8,128)(2,1)}) custom-call(s32[2]{0:T(128)S(1)} %pad_add_fusion.place_ref, f32[128,1536]{1,0:T(8,128)S(1)} %get-tuple-element.54.key_local_ref, f32[128,1536]{1,0:T(8,128)S(1)} %get-tuple-element.55.value_local_ref, bf16[128,1536]{1,0:T(8,128)(2,1)S(1)} %get-tuple-element.56.weighted_values_ref, ...), custom_call_target="tpu_custom_call" | custom-call | bytes 3735552 | tf_op jit(solution)/shard_map/key_value_grads/pallas_call | solution.py:353
  (36 shorter events, 9.2 us)
Async XLA Ops:
  0.6 0.7 %copy-start.5 = (f32[16,128]{1,0:T(8,128)S(1)}, f32[16,128]{1,0:T(8,128)}, u32[]{:S(2)}) copy-start(f32[16,128]{1,0:T(8,128)} %decay_ref.5) | copy-start | bytes 24580
  0.7 0.7 %copy-start.6 = (s32[16]{0:T(128)S(1)}, s32[16]{0:T(128)}, u32[]{:S(2)}) copy-start(s32[16]{0:T(128)} %lengths_ref.5) | copy-start | bytes 196
  1.3 1.0 %copy-start.1 = (bf16[128,1536]{1,0:T(8,128)(2,1)S(1)}, bf16[128,1536]{1,0:T(8,128)(2,1)}, u32[]{:S(2)}) copy-start(bf16[128,1536]{1,0:T(8,128)(2,1)} %keys_ref.5) | copy-start | bytes 1179652
  2.3 1.0 %copy-start.3 = (bf16[128,1536]{1,0:T(8,128)(2,1)S(1)}, bf16[128,1536]{1,0:T(8,128)(2,1)}, u32[]{:S(2)}) copy-start(bf16[128,1536]{1,0:T(8,128)(2,1)} %values_ref.5) | copy-start | bytes 1179652
  4.9 7.7 %collective-permute-start = (f32[304,128]{1,0:T(8,128)S(1)}, f32[304,128]{1,0:T(8,128)S(1)}, u32[]{:S(2)}, u32[]{:S(2)}) collective-permute-start(f32[304,128]{1,0:T(8,128)S(1)} %get-tuple-element.39), channel_id=1, source_target_pairs={{0,2},{2,0},{4,6},{6,4},{8,10},{10,8},{12,14},{14,12},{16,18},{18,... | collective-permute-start | bytes 466952 | tf_op jit(solution)/shard_map/ppermute | solution.py:371
  7.9 8.8 %collective-permute-start.1 = (f32[304,128]{1,0:T(8,128)S(1)}, f32[304,128]{1,0:T(8,128)S(1)}, u32[]{:S(2)}, u32[]{:S(2)}) collective-permute-start(f32[304,128]{1,0:T(8,128)S(1)} %get-tuple-element.40), channel_id=1, source_target_pairs={{0,4},{2,6},{4,0},{6,2},{8,12},{10,14},{12,8},{14,10},{16,20},{18,... | collective-permute-start | bytes 466952 | tf_op jit(solution)/shard_map/ppermute | solution.py:371
  9.4 7.3 %collective-permute-start.2 = (f32[304,128]{1,0:T(8,128)S(1)}, f32[304,128]{1,0:T(8,128)S(1)}, u32[]{:S(2)}, u32[]{:S(2)}) collective-permute-start(f32[304,128]{1,0:T(8,128)S(1)} %get-tuple-element.41), channel_id=1, source_target_pairs={{0,6},{2,4},{4,2},{6,0},{8,14},{10,12},{12,10},{14,8},{16,22},{18,... | collective-permute-start | bytes 466952 | tf_op jit(solution)/shard_map/ppermute | solution.py:371
  17.4 10.6 %copy-start.2 = (bf16[128,1536]{1,0:T(8,128)(2,1)S(1)}, bf16[128,1536]{1,0:T(8,128)(2,1)}, u32[]{:S(2)}) copy-start(bf16[128,1536]{1,0:T(8,128)(2,1)} %keys_ref.5) | copy-start | bytes 1179652
  17.4 10.6 %copy-start.4 = (bf16[128,1536]{1,0:T(8,128)(2,1)S(1)}, bf16[128,1536]{1,0:T(8,128)(2,1)}, u32[]{:S(2)}) copy-start(bf16[128,1536]{1,0:T(8,128)(2,1)} %values_ref.5) | copy-start | bytes 1179652
  17.4 10.6 %copy-start.7 = (bf16[128,1536]{1,0:T(8,128)(2,1)S(1)}, bf16[128,1536]{1,0:T(8,128)(2,1)}, u32[]{:S(2)}) copy-start(bf16[128,1536]{1,0:T(8,128)(2,1)} %queries_ref.3) | copy-start | bytes 1179652
  17.4 6.3 %collective-permute-start.3 = (f32[288,128]{1,0:T(8,128)S(1)}, f32[288,128]{1,0:T(8,128)S(1)}, u32[]{:S(2)}, u32[]{:S(2)}) collective-permute-start(f32[288,128]{1,0:T(8,128)S(1)} %total_state.2), channel_id=1, source_target_pairs={{0,8},{2,10},{4,12},{6,14},{8,16},{10,18},{12,20},{14,22},{16,24},... | collective-permute-start | bytes 442376 | tf_op jit(solution)/shard_map/ppermute | solution.py:379
  23.7 4.2 %copy-start.8 = (f32[1536]{0:T(1024)S(1)}, f32[1536]{0:T(1024)}, u32[]{:S(2)}) copy-start(f32[1536]{0:T(1024)} %param.11) | copy-start | bytes 18436
  24.4 6.1 %collective-permute-start.4 = (f32[288,128]{1,0:T(8,128)S(1)}, f32[288,128]{1,0:T(8,128)S(1)}, u32[]{:S(2)}, u32[]{:S(2)}) collective-permute-start(f32[288,128]{1,0:T(8,128)S(1)} %get-tuple-element.43), channel_id=1, source_target_pairs={{0,2},{2,0},{4,6},{6,4},{8,10},{10,8},{12,14},{14,12},{16,18},{18,... | collective-permute-start | bytes 442376 | tf_op jit(solution)/shard_map/ppermute | solution.py:371
  25.7 5.2 %collective-permute-start.5 = (f32[288,128]{1,0:T(8,128)S(1)}, f32[288,128]{1,0:T(8,128)S(1)}, u32[]{:S(2)}, u32[]{:S(2)}) collective-permute-start(f32[288,128]{1,0:T(8,128)S(1)} %get-tuple-element.44), channel_id=1, source_target_pairs={{0,4},{2,6},{4,0},{6,2},{8,12},{10,14},{12,8},{14,10},{16,20},{18,... | collective-permute-start | bytes 442376 | tf_op jit(solution)/shard_map/ppermute | solution.py:371
  26.5 6.0 %collective-permute-start.6 = (f32[288,128]{1,0:T(8,128)S(1)}, f32[288,128]{1,0:T(8,128)S(1)}, u32[]{:S(2)}, u32[]{:S(2)}) collective-permute-start(f32[288,128]{1,0:T(8,128)S(1)} %get-tuple-element.45), channel_id=1, source_target_pairs={{0,6},{2,4},{4,2},{6,0},{8,14},{10,12},{12,10},{14,8},{16,22},{18,... | collective-permute-start | bytes 442376 | tf_op jit(solution)/shard_map/ppermute | solution.py:371
  28.0 4.6 %copy-start = (bf16[128,1536]{1,0:T(8,128)(2,1)S(1)}, bf16[128,1536]{1,0:T(8,128)(2,1)}, u32[]{:S(2)}) copy-start(bf16[128,1536]{1,0:T(8,128)(2,1)} %out_grad_ref.3) | copy-start | bytes 1179652
  33.6 1.3 %collective-permute-start.7 = (f32[128,128]{1,0:T(8,128)S(1)}, f32[128,128]{1,0:T(8,128)S(1)}, u32[]{:S(2)}, u32[]{:S(2)}) collective-permute-start(f32[128,128]{1,0:T(8,128)S(1)} %get-tuple-element.47.sums_ref), channel_id=1, source_target_pairs={{0,1},{1,0},{2,3},{3,2},{4,5},{5,4},{6,7},{7,6},{8,9},{9,8},{10,11... | collective-permute-start | bytes 196616 | tf_op jit(solution)/shard_map/ppermute | solution.py:465
  36.2 6.7 %collective-permute-start.8 = (f32[288,128]{1,0:T(8,128)S(1)}, f32[288,128]{1,0:T(8,128)S(1)}, u32[]{:S(2)}, u32[]{:S(2)}) collective-permute-start(f32[288,128]{1,0:T(8,128)S(1)} %get-tuple-element.59), channel_id=1, source_target_pairs={{0,2},{2,0},{4,6},{6,4},{8,10},{10,8},{12,14},{14,12},{16,18},{18,... | collective-permute-start | bytes 442376 | tf_op jit(solution)/shard_map/ppermute | solution.py:371
  37.8 8.8 %collective-permute-start.9 = (f32[288,128]{1,0:T(8,128)S(1)}, f32[288,128]{1,0:T(8,128)S(1)}, u32[]{:S(2)}, u32[]{:S(2)}) collective-permute-start(f32[288,128]{1,0:T(8,128)S(1)} %get-tuple-element.60), channel_id=1, source_target_pairs={{0,4},{2,6},{4,0},{6,2},{8,12},{10,14},{12,8},{14,10},{16,20},{18,... | collective-permute-start | bytes 442376 | tf_op jit(solution)/shard_map/ppermute | solution.py:371
  38.5 8.1 %collective-permute-start.10 = (f32[288,128]{1,0:T(8,128)S(1)}, f32[288,128]{1,0:T(8,128)S(1)}, u32[]{:S(2)}, u32[]{:S(2)}) collective-permute-start(f32[288,128]{1,0:T(8,128)S(1)} %get-tuple-element.61), channel_id=1, source_target_pairs={{0,6},{2,4},{4,2},{6,0},{8,14},{10,12},{12,10},{14,8},{16,22},{18,... | collective-permute-start | bytes 442376 | tf_op jit(solution)/shard_map/ppermute | solution.py:371
  47.2 7.5 %collective-permute-start.11 = (f32[288,128]{1,0:T(8,128)S(1)}, f32[288,128]{1,0:T(8,128)S(1)}, u32[]{:S(2)}, u32[]{:S(2)}) collective-permute-start(f32[288,128]{1,0:T(8,128)S(1)} %total_state.3), channel_id=1, source_target_pairs={{8,0},{10,2},{12,4},{14,6},{16,8},{18,10},{20,12},{22,14},{24,16},... | collective-permute-start | bytes 442376 | tf_op jit(solution)/shard_map/ppermute | solution.py:379
  55.4 7.7 %collective-permute-start.12 = (f32[288,128]{1,0:T(8,128)S(1)}, f32[288,128]{1,0:T(8,128)S(1)}, u32[]{:S(2)}, u32[]{:S(2)}) collective-permute-start(f32[288,128]{1,0:T(8,128)S(1)} %get-tuple-element.63), channel_id=1, source_target_pairs={{0,2},{2,0},{4,6},{6,4},{8,10},{10,8},{12,14},{14,12},{16,18},{18,... | collective-permute-start | bytes 442376 | tf_op jit(solution)/shard_map/ppermute | solution.py:371
  56.1 7.9 %collective-permute-start.13 = (f32[288,128]{1,0:T(8,128)S(1)}, f32[288,128]{1,0:T(8,128)S(1)}, u32[]{:S(2)}, u32[]{:S(2)}) collective-permute-start(f32[288,128]{1,0:T(8,128)S(1)} %get-tuple-element.64), channel_id=1, source_target_pairs={{0,4},{2,6},{4,0},{6,2},{8,12},{10,14},{12,8},{14,10},{16,20},{18,... | collective-permute-start | bytes 442376 | tf_op jit(solution)/shard_map/ppermute | solution.py:371
  57.4 6.6 %collective-permute-start.14 = (f32[288,128]{1,0:T(8,128)S(1)}, f32[288,128]{1,0:T(8,128)S(1)}, u32[]{:S(2)}, u32[]{:S(2)}) collective-permute-start(f32[288,128]{1,0:T(8,128)S(1)} %get-tuple-element.65), channel_id=1, source_target_pairs={{0,6},{2,4},{4,2},{6,0},{8,14},{10,12},{12,10},{14,8},{16,22},{18,... | collective-permute-start | bytes 442376 | tf_op jit(solution)/shard_map/ppermute | solution.py:371

commit v2 on v1

--- a/solution.py
+++ b/solution.py
@@ -51,6 +51,11 @@
         self.factor_rows = -(-self.tiles // 8) * 8
 
 
+def place(plan):
+    index = lax.axis_index("ctx")
+    return index * plan.tokens, lax.rem(index, plan.pieces)
+
+
 def iota(shape, dim):
     return lax.broadcasted_iota(jnp.int32, shape, dim)
 
@@ -150,18 +155,36 @@
             ]
 
 
-def exit_kernel(plan, place_ref, lengths_ref, decay_ref, keys_ref, values_ref, *refs):
-    pieces, (weighted_ref, state_ref) = refs[: plan.pieces], refs[plan.pieces :]
-    block_start, mine = place_ref[0], place_ref[1]
+def row_copies(source, target, sems):
+    count = sems.shape[0]
+    rows = source.shape[0] // count
+    return [
+        pltpu.make_async_copy(
+            source.at[i * rows : (i + 1) * rows], target.at[i * rows : (i + 1) * rows], sems.at[i]
+        )
+        for i in range(count)
+    ]
+
+
+def exit_kernel(plan, lengths_hbm, decay_hbm, keys_hbm, values_hbm, *refs):
+    pieces = refs[: plan.pieces]
+    weighted_ref, lengths_ref, decay_ref, keys_ref, values_ref, state_ref, small_sems, key_sems, value_sems = refs[
+        plan.pieces :
+    ]
+    lengths_copy = pltpu.make_async_copy(lengths_hbm, lengths_ref, small_sems.at[0])
+    decay_copy = pltpu.make_async_copy(decay_hbm, decay_ref, small_sems.at[1])
+    lengths_copy.start()
+    decay_copy.start()
+    keys_copies = row_copies(keys_hbm, keys_ref, key_sems)
+    values_copies = row_copies(values_hbm, values_ref, value_sems)
+    for copy in keys_copies + values_copies:
+        copy.start()
+    block_start, mine = place(plan)
+    lengths_copy.wait()
     last, first = doc_edges(plan, lengths_ref, block_start)
+    decay_copy.wait()
     decay = decay_ref[...]
     weights = spread(plan, exit_columns(plan, decay, last, block_start))
-    for g in range(plan.groups):
-        at = lanes_of(plan, g)
-        weighted = (keys_ref[:, at].astype(F32) * weights[:, at]).astype(BF16)
-        weighted_ref[:, at] = weighted
-        state_ref[:, at] = own_heads(plan, dot(weighted, values_ref[:, at], TN), plan.dim)
-    store_pieces(plan, mine, state_ref, pieces)
     whole = jnp.exp(jnp.sum(decay, axis=1, keepdims=True))
     whole = jnp.where(first >= block_start + plan.tokens, whole, 0.0)
     head = iota((plan.heads, 128), 0)
@@ -174,50 +197,48 @@
     rows = jnp.concatenate(rows, axis=0)
     for piece in pieces:
         piece[plan.piece_rows :, :] = rows
-
-
-def chain_kernel(plan, reverse, with_carry, place_ref, *refs):
-    n = plan.pieces
+    for copy in keys_copies:
+        copy.wait()
+    weighted_ref[...] = (keys_ref[...].astype(F32) * weights).astype(BF16)
+    for copy in values_copies:
+        copy.wait()
+    for g in range(plan.groups):
+        at = lanes_of(plan, g)
+        state_ref[:, at] = own_heads(plan, dot(weighted_ref[:, at], values_ref[:, at], TN), plan.dim)
+    store_pieces(plan, mine, state_ref, pieces)
+
+
+def chain_kernel(plan, reverse, with_carry, *refs):
+    n, rows = plan.pieces, plan.rows
     pieces, factors = refs[:n], refs[n : 2 * n]
-    mine = place_ref[1]
-    rows = plan.rows
+    carry_ref = refs[2 * n] if with_carry else None
+    outs = refs[2 * n + 1 :] if with_carry else refs[2 * n :]
     order = range(n - 1, -1, -1) if reverse else range(n)
-    slot = [mine ^ j for j in range(n)]
-    state_scratch, factor_scratch = refs[-2], refs[-1]
-    for m in range(n):
-        state_scratch[mine ^ m] = pieces[m][: plan.piece_rows, :]
-        factor_scratch[mine ^ m] = factors[m][-plan.factor_rows :, :]
-    if with_carry:
-        held = refs[2 * n][...]
-        outs_ref = refs[-3]
-    else:
-        held = jnp.zeros((plan.piece_rows, 128), F32)
-        outs_ref = None
-    tiles = [held[j * rows : (j + 1) * rows] for j in range(plan.tiles)]
-    for step, b in enumerate(order):
-        if with_carry:
-            for j in range(plan.tiles):
-                outs_ref[b, j * rows : (j + 1) * rows, :] = tiles[j]
-            if step == n - 1:
-                break
+
+    def at_place(mine):
         for j in range(plan.tiles):
-            tiles[j] = (
-                tiles[j] * factor_scratch[b, j : j + 1, :]
-                + state_scratch[b, j * rows : (j + 1) * rows, :]
-            )
-    if with_carry:
-        outs = refs[2 * n + 1 : 3 * n + 1]
-        for m in range(n):
-            outs[m][...] = outs_ref[mine ^ m]
-    else:
-        for j in range(plan.tiles):
-            refs[2 * n][j * rows : (j + 1) * rows, :] = tiles[j]
+            at = slice(j * rows, (j + 1) * rows)
+            tile = carry_ref[at] if with_carry else None
+            for step, b in enumerate(order):
+                m = mine ^ b
+                if with_carry:
+                    outs[m][at] = tile
+                    if step == n - 1:
+                        break
+                rate = factors[m][plan.piece_rows + j : plan.piece_rows + j + 1, :]
+                tile = pieces[m][at] if tile is None else tile * rate + pieces[m][at]
+            if not with_carry:
+                outs[0][at] = tile
+
+    own = place(plan)[1]
+    for mine in range(n):
+        pl.when(own == mine)(functools.partial(at_place, mine))
 
 
 def local_kernel(
-    plan, place_ref, lengths_ref, decay_ref, queries_ref, keys_ref, values_ref, probs_ref, local_ref, reached_ref
+    plan, lengths_ref, decay_ref, queries_ref, keys_ref, values_ref, probs_ref, local_ref, reached_ref
 ):
-    block_start = place_ref[0]
+    block_start = place(plan)[0]
     decay = decay_ref[...]
     last, first = doc_edges(plan, lengths_ref, block_start)
     columns, rows = log_sums(plan, decay)
@@ -240,10 +261,10 @@
         local_ref[:, at] = dot(probs, stack_heads(plan, values))
 
 
-def attend_kernel(plan, place_ref, local_ref, reached_ref, out_grad_ref, gain_ref, *refs):
+def attend_kernel(plan, local_ref, reached_ref, out_grad_ref, gain_ref, *refs):
     pieces = refs[: plan.pieces]
     attended_ref, sums_ref, incoming_ref, state_ref = refs[plan.pieces :]
-    load_pieces(plan, place_ref[1], pieces, state_ref)
+    load_pieces(plan, place(plan)[1], pieces, state_ref)
     squares = inner = None
     for g in range(plan.groups):
         at = lanes_of(plan, g)
@@ -263,7 +284,7 @@
 
 
 def grad_kernel(
-    plan, features, place_ref, attended_ref, out_grad_ref, gain_ref, sums_ref, other_ref, reached_ref, *refs
+    plan, features, attended_ref, out_grad_ref, gain_ref, sums_ref, other_ref, reached_ref, *refs
 ):
     pieces, (attended_grad_ref, norm_ref, state_ref) = refs[: plan.pieces], refs[plan.pieces :]
     sums = sums_ref[...] + other_ref[...]
@@ -276,12 +297,11 @@
         attended_grad = (grad * inverse - attended_ref[:, at] * slope).astype(BF16)
         attended_grad_ref[:, at] = attended_grad
         state_ref[:, at] = own_heads(plan, dot(reached_ref[:, at], attended_grad, TN), plan.dim)
-    store_pieces(plan, place_ref[1], state_ref, pieces)
+    store_pieces(plan, place(plan)[1], state_ref, pieces)
 
 
 def inner_kernel(
     plan,
-    place_ref,
     lengths_ref,
     decay_ref,
     queries_ref,
@@ -299,7 +319,7 @@
     value_local_ref,
     weighted_ref,
 ):
-    block_start = place_ref[0]
+    block_start = place(plan)[0]
     decay = decay_ref[...]
     last, first = doc_edges(plan, lengths_ref, block_start)
     columns, rows = log_sums(plan, decay)
@@ -331,31 +351,50 @@
 
 
 def finish_kernel(
-    plan, place_ref, key_local_ref, value_local_ref, weighted_values_ref, weighted_keys_ref, *refs
+    plan, key_local_ref, value_local_ref, weighted_values_ref, weighted_keys_ref, *refs
 ):
-    pieces, (key_grad_ref, value_grad_ref, state_ref) = refs[: plan.pieces], refs[plan.pieces :]
-    load_pieces(plan, place_ref[1], pieces, state_ref)
+    pieces = refs[: plan.pieces]
+    key_grad_hbm, value_grad_hbm, state_ref, key_grad_ref, value_grad_ref, key_sems, value_sems = refs[
+        plan.pieces :
+    ]
+    load_pieces(plan, place(plan)[1], pieces, state_ref)
+    copies = []
     for g in range(plan.groups):
         at = lanes_of(plan, g)
         later = stack_heads(plan, state_ref[:, at].astype(BF16))
         key_grad = key_local_ref[:, at] + dot(weighted_values_ref[:, at], later, NT)
         key_grad_ref[:, at] = key_grad.astype(BF16)
+        copies.append(
+            pltpu.make_async_copy(key_grad_ref.at[:, at], key_grad_hbm.at[:, at], key_sems.at[g])
+        )
+        copies[-1].start()
         value_grad = value_local_ref[:, at] + dot(weighted_keys_ref[:, at], later)
         value_grad_ref[:, at] = value_grad.astype(BF16)
+        copies.append(
+            pltpu.make_async_copy(value_grad_ref.at[:, at], value_grad_hbm.at[:, at], value_sems.at[g])
+        )
+        copies[-1].start()
+    for copy in copies:
+        copy.wait()
 
 
 SCALAR = pl.BlockSpec(memory_space=pltpu.SMEM)
 WHOLE = pl.BlockSpec(memory_space=pltpu.VMEM)
-
-
-def call(kernel, name, scalars, arrays, outs, scratch=(), flops=0):
+FAR = pl.BlockSpec(memory_space=pltpu.HBM)
+
+
+def call(kernel, name, scalars, arrays, outs, scratch=(), flops=0, far_in=0, far_out=False):
+    scalars = [pltpu.with_memory_space_constraint(a, pltpu.HBM) for a in scalars]
+    arrays = [
+        pltpu.with_memory_space_constraint(a, pltpu.HBM) if i < far_in else a for i, a in enumerate(arrays)
+    ]
     moved = sum(a.size * a.dtype.itemsize for a in (*arrays, *outs))
     return pl.pallas_call(
         kernel,
         name=name,
         out_shape=outs,
-        in_specs=[SCALAR] * len(scalars) + [WHOLE] * len(arrays),
-        out_specs=[WHOLE] * len(outs),
+        in_specs=[SCALAR] * len(scalars) + [FAR] * far_in + [WHOLE] * (len(arrays) - far_in),
+        out_specs=[FAR if far_out else WHOLE] * len(outs),
         scratch_shapes=list(scratch),
         compiler_params=pltpu.CompilerParams(vmem_limit_bytes=40 * 2**20),
         cost_estimate=pl.CostEstimate(flops=flops, bytes_accessed=moved, transcendentals=0),
@@ -399,8 +438,6 @@
     even = reach & (reach - 1) == 0 and (width // heads) % (8 * reach) == 0
     plan = Plan(tokens, width, heads, reach if even else 1)
     n = plan.pieces
-    index = lax.axis_index("ctx")
-    place = jnp.stack([index * tokens, index % n]).astype(jnp.int32)
     gain = norm_gain.reshape(1, width)
     like = array(tokens, width, dtype=BF16)
     wide = array(tokens, width)
@@ -411,11 +448,21 @@
     *pieces, weighted_keys = call(
         functools.partial(exit_kernel, plan),
         "exit_states",
-        (place, doc_lengths),
-        (decay_log, keys, values),
+        (),
+        (doc_lengths, decay_log, keys, values),
         [framed] * n + [like],
-        [state],
+        [
+            pltpu.SMEM(doc_lengths.shape, jnp.int32),
+            pltpu.VMEM(decay_log.shape, F32),
+            pltpu.VMEM((tokens, width), BF16),
+            pltpu.VMEM((tokens, width), BF16),
+            state,
+            pltpu.SemaphoreType.DMA((2,)),
+            pltpu.SemaphoreType.DMA((1,)),
+            pltpu.SemaphoreType.DMA((1,)),
+        ],
         flops=10**8,
+        far_in=4,
     )
     if even:
         pieces = exchange(pieces, count)
@@ -423,16 +470,12 @@
 
     def chain(pieces, reverse, carry=None):
         with_carry = carry is not None
-        scratch = [pltpu.VMEM((n, plan.piece_rows, 128), F32), pltpu.VMEM((n, plan.factor_rows, 128), F32)]
-        if with_carry:
-            scratch = [pltpu.VMEM((n, plan.piece_rows, 128), F32)] + scratch
         return call(
             functools.partial(chain_kernel, plan, reverse, with_carry),
             "prefix_states" if with_carry else "total_state",
-            (place,),
+            (),
             (*pieces, *frames, carry) if with_carry else (*pieces, *frames),
             [piece] * n if with_carry else [piece],
-            scratch,
         )
 
     def entering(pieces, reverse):
@@ -449,7 +492,7 @@
     probs, local, reached = call(
         functools.partial(local_kernel, plan),
         "local_attention",
-        (place, doc_lengths),
+        (doc_lengths,),
         (decay_log, queries, keys, values),
         [array(tokens, heads * tokens, dtype=BF16), wide, like],
         flops=10**9,
@@ -457,7 +500,7 @@
     attended, sums, incoming_state = call(
         functools.partial(attend_kernel, plan),
         "attended",
-        (place,),
+        (),
         (local, reached, out_grad, gain, *incoming),
         [wide, array(tokens, 128), array(plan.dim, width, dtype=BF16)],
         [state],
@@ -466,7 +509,7 @@
     *pieces, attended_grad, norm = call(
         functools.partial(grad_kernel, plan, features),
         "attended_grad",
-        (place,),
+        (),
         (attended, out_grad, gain, sums, other, reached),
         [piece] * n + [like, array(tokens, 128)],
         [state],
@@ -477,7 +520,7 @@
     output, query_grad, key_local, value_local, weighted_values = call(
         functools.partial(inner_kernel, plan),
         "local_grads",
-        (place, doc_lengths),
+        (doc_lengths,),
         (
             decay_log,
             queries,
@@ -496,10 +539,17 @@
     key_grad, value_grad = call(
         functools.partial(finish_kernel, plan),
         "key_value_grads",
-        (place,),
+        (),
         (key_local, value_local, weighted_values, weighted_keys, *later),
         [like, like],
-        [state],
+        [
+            state,
+            pltpu.VMEM((tokens, width), BF16),
+            pltpu.VMEM((tokens, width), BF16),
+            pltpu.SemaphoreType.DMA((plan.groups,)),
+            pltpu.SemaphoreType.DMA((plan.groups,)),
+        ],
+        far_out=True,
     )
     return (output, query_grad, key_grad, value_grad)
 

time: 66.5 us -> 60.1 us (0.904)
  Pallas kernels: 15.1 us -> 11.8 us
  local copies, waits for them, and re-layouts: 2.63 us -> 0.04 us
    pallas_call x10, Pallas kernels: 15.1 us -> 11.8 us  [call(): pl.pallas_call(kernel, name=name, out_shape=outs, in_specs=[SCALAR] * len...]
    unnamed x18 -> x12, local copies, waits for them, and re-layouts: 2.62 us -> 0.03 us
  transfers between devices with their start and end apart: 15 -> 15, of which waited for: 11 -> 10; matrix products, arithmetic and copies ran while one was open for 0% -> 0% of each run, Pallas kernels for 10% -> 11%
where the time goes in v2:
time: 60.1 us; the launch traced here: 59.9 us
  waiting for transfers between devices  27.1 us (45%)
  starting transfers between devices  20.2 us (34%)
  Pallas kernels  11.8 us (20%)
  between operations  0.81 us (1%)
    ppermute x12, waiting for transfers between devices, exchange(): lax.ppermute(piece, 'ctx', [(i, i ^ m) for i in range(count)])  17 us
    ppermute x12, starting transfers between devices, exchange(): lax.ppermute(piece, 'ctx', [(i, i ^ m) for i in range(count)])  15.2 us
    pallas_call x10, Pallas kernels, call(): pl.pallas_call(kernel, name=name, out_shape=outs, in_specs=[SCALAR] * len...  11.8 us
    ppermute x2, waiting for transfers between devices, shift(): return lax.ppermute(x, 'ctx', pairs)  8.84 us
    ppermute x2, starting transfers between devices, shift(): return lax.ppermute(x, 'ctx', pairs)  4.91 us
    ppermute x1, waiting for transfers between devices, on_device(): other = lax.ppermute(sums, 'head', [(0, 1), (1, 0)])  1.24 us
  transfers between devices with their start and end apart: 15, of which 10 were waited for; matrix products, arithmetic and copies ran while one was open for 0% of the time, Pallas kernels for 11%

profile of v2, /device:TPU:0, one launch (start us, length us, event | category | flops | bytes accessed | tf_op | source)
XLA Modules:
  0.0 59.9 jit_solution(7710404567461992521)
XLA Ops:
  0.6 2.0 %exit_states.1 = (f32[304,128]{1,0:T(8,128)S(1)}, f32[304,128]{1,0:T(8,128)S(1)}, f32[304,128]{1,0:T(8,128)S(1)}, f32[304,128]{1,0:T(8,128)S(1)}, bf16[128,1536]{1,0:T(8,128)(2,1)S(1)}) custom-call(s32[16]{0:T(128)} %lengths_ref.3, f32[16,128]{1,0:T(8,128)} %decay_ref.3, bf16[128,1536]{1,0:T(8,128)(2,1)} %keys_ref.3, bf16[128,1536]{1,0:T(8,128)(2,1)} %values_ref.3), custom_call_target="tpu_custom_call" | custom-call | flops 100000000 | bytes 1810496 | tf_op jit(solution)/shard_map/exit_states/pallas_call | solution.py:392
  2.6 3.0 %collective-permute-start = (f32[304,128]{1,0:T(8,128)S(1)}, f32[304,128]{1,0:T(8,128)S(1)}, u32[]{:S(2)}, u32[]{:S(2)}) collective-permute-start(f32[304,128]{1,0:T(8,128)S(1)} %get-tuple-element.39), channel_id=1, source_target_pairs={{0,2},{2,0},{4,6},{6,4},{8,10},{10,8},{12,14},{14,12},{16,18},{18,... | collective-permute-start | bytes 466952 | tf_op jit(solution)/shard_map/ppermute | solution.py:410
  5.6 1.5 %collective-permute-start.1 = (f32[304,128]{1,0:T(8,128)S(1)}, f32[304,128]{1,0:T(8,128)S(1)}, u32[]{:S(2)}, u32[]{:S(2)}) collective-permute-start(f32[304,128]{1,0:T(8,128)S(1)} %get-tuple-element.40), channel_id=1, source_target_pairs={{0,4},{2,6},{4,0},{6,2},{8,12},{10,14},{12,8},{14,10},{16,20},{18,... | collective-permute-start | bytes 466952 | tf_op jit(solution)/shard_map/ppermute | solution.py:410
  7.2 3.1 %collective-permute-done.refs_1_.refs_5_ = f32[304,128]{1,0:T(8,128)S(1)} collective-permute-done((f32[304,128]{1,0:T(8,128)S(1)}, f32[304,128]{1,0:T(8,128)S(1)}, u32[]{:S(2)}, u32[]{:S(2)}) %collective-permute-start) | collective-permute-done | bytes 155680 | tf_op jit(solution)/shard_map/ppermute | solution.py:410
  10.3 4.2 %collective-permute-done.1.refs_2_.refs_6_ = f32[304,128]{1,0:T(8,128)S(1)} collective-permute-done((f32[304,128]{1,0:T(8,128)S(1)}, f32[304,128]{1,0:T(8,128)S(1)}, u32[]{:S(2)}, u32[]{:S(2)}) %collective-permute-start.1) | collective-permute-done | bytes 155680 | tf_op jit(solution)/shard_map/ppermute | solution.py:410
  14.5 3.6 %collective-permute-start.3 = (f32[288,128]{1,0:T(8,128)S(1)}, f32[288,128]{1,0:T(8,128)S(1)}, u32[]{:S(2)}, u32[]{:S(2)}) collective-permute-start(f32[288,128]{1,0:T(8,128)S(1)} %total_state.2), channel_id=1, source_target_pairs={{0,8},{2,10},{4,12},{6,14},{8,16},{10,18},{12,20},{14,22},{16,24},... | collective-permute-start | bytes 442376 | tf_op jit(solution)/shard_map/ppermute | solution.py:418
  18.2 2.6 %collective-permute-done.3.refs_8_ = f32[288,128]{1,0:T(8,128)S(1)} collective-permute-done((f32[288,128]{1,0:T(8,128)S(1)}, f32[288,128]{1,0:T(8,128)S(1)}, u32[]{:S(2)}, u32[]{:S(2)}) %collective-permute-start.3) | collective-permute-done | bytes 147488 | tf_op jit(solution)/shard_map/ppermute | solution.py:418
  20.9 1.3 %collective-permute-start.4 = (f32[288,128]{1,0:T(8,128)S(1)}, f32[288,128]{1,0:T(8,128)S(1)}, u32[]{:S(2)}, u32[]{:S(2)}) collective-permute-start(f32[288,128]{1,0:T(8,128)S(1)} %get-tuple-element.43), channel_id=1, source_target_pairs={{0,2},{2,0},{4,6},{6,4},{8,10},{10,8},{12,14},{14,12},{16,18},{18,... | collective-permute-start | bytes 442376 | tf_op jit(solution)/shard_map/ppermute | solution.py:410
  22.2 0.8 %collective-permute-start.5 = (f32[288,128]{1,0:T(8,128)S(1)}, f32[288,128]{1,0:T(8,128)S(1)}, u32[]{:S(2)}, u32[]{:S(2)}) collective-permute-start(f32[288,128]{1,0:T(8,128)S(1)} %get-tuple-element.44), channel_id=1, source_target_pairs={{0,4},{2,6},{4,0},{6,2},{8,12},{10,14},{12,8},{14,10},{16,20},{18,... | collective-permute-start | bytes 442376 | tf_op jit(solution)/shard_map/ppermute | solution.py:410
  23.0 1.5 %collective-permute-start.6 = (f32[288,128]{1,0:T(8,128)S(1)}, f32[288,128]{1,0:T(8,128)S(1)}, u32[]{:S(2)}, u32[]{:S(2)}) collective-permute-start(f32[288,128]{1,0:T(8,128)S(1)} %get-tuple-element.45), channel_id=1, source_target_pairs={{0,6},{2,4},{4,2},{6,0},{8,14},{10,12},{12,10},{14,8},{16,22},{18,... | collective-permute-start | bytes 442376 | tf_op jit(solution)/shard_map/ppermute | solution.py:410
  24.5 2.5 %local_attention.1 = (bf16[128,2048]{1,0:T(8,128)(2,1)S(1)}, f32[128,1536]{1,0:T(8,128)S(1)}, bf16[128,1536]{1,0:T(8,128)(2,1)S(1)}) custom-call(s32[16]{0:T(128)} %lengths_ref.3, f32[16,128]{1,0:T(8,128)S(1)} %copy-done.3, bf16[128,1536]{1,0:T(8,128)(2,1)S(1)} %copy-done.4, bf16[128,1536]{1,0:T(8,128)(2,1)S(1)} %copy-done.1, bf16[128,1536]{1,0:T(8,128)(2,1)S(1)} %copy-done.2), custom_call_target="tpu_custom_call" | custom-call | flops 1000000000 | bytes 2891776 | tf_op jit(solution)/shard_map/local_attention/pallas_call | solution.py:392
  27.3 1.7 %collective-permute-done.6.refs_3_ = f32[288,128]{1,0:T(8,128)S(1)} collective-permute-done((f32[288,128]{1,0:T(8,128)S(1)}, f32[288,128]{1,0:T(8,128)S(1)}, u32[]{:S(2)}, u32[]{:S(2)}) %collective-permute-start.6) | collective-permute-done | bytes 147488 | tf_op jit(solution)/shard_map/ppermute | solution.py:410
  29.7 1.2 %collective-permute-done.7.other_ref = f32[128,128]{1,0:T(8,128)S(1)} collective-permute-done((f32[128,128]{1,0:T(8,128)S(1)}, f32[128,128]{1,0:T(8,128)S(1)}, u32[]{:S(2)}, u32[]{:S(2)}) %collective-permute-start.7) | collective-permute-done | bytes 65568 | tf_op jit(solution)/shard_map/ppermute | solution.py:508
  31.6 1.6 %collective-permute-start.8 = (f32[288,128]{1,0:T(8,128)S(1)}, f32[288,128]{1,0:T(8,128)S(1)}, u32[]{:S(2)}, u32[]{:S(2)}) collective-permute-start(f32[288,128]{1,0:T(8,128)S(1)} %get-tuple-element.59), channel_id=1, source_target_pairs={{0,2},{2,0},{4,6},{6,4},{8,10},{10,8},{12,14},{14,12},{16,18},{18,... | collective-permute-start | bytes 442376 | tf_op jit(solution)/shard_map/ppermute | solution.py:410
  33.9 1.3 %collective-permute-start.10 = (f32[288,128]{1,0:T(8,128)S(1)}, f32[288,128]{1,0:T(8,128)S(1)}, u32[]{:S(2)}, u32[]{:S(2)}) collective-permute-start(f32[288,128]{1,0:T(8,128)S(1)} %get-tuple-element.61), channel_id=1, source_target_pairs={{0,6},{2,4},{4,2},{6,0},{8,14},{10,12},{12,10},{14,8},{16,22},{18,... | collective-permute-start | bytes 442376 | tf_op jit(solution)/shard_map/ppermute | solution.py:410
  35.2 3.1 %collective-permute-done.8.refs_1_ = f32[288,128]{1,0:T(8,128)S(1)} collective-permute-done((f32[288,128]{1,0:T(8,128)S(1)}, f32[288,128]{1,0:T(8,128)S(1)}, u32[]{:S(2)}, u32[]{:S(2)}) %collective-permute-start.8) | collective-permute-done | bytes 147488 | tf_op jit(solution)/shard_map/ppermute | solution.py:410
  38.3 3.7 %collective-permute-done.9.refs_2_ = f32[288,128]{1,0:T(8,128)S(1)} collective-permute-done((f32[288,128]{1,0:T(8,128)S(1)}, f32[288,128]{1,0:T(8,128)S(1)}, u32[]{:S(2)}, u32[]{:S(2)}) %collective-permute-start.9) | collective-permute-done | bytes 147488 | tf_op jit(solution)/shard_map/ppermute | solution.py:410
  42.1 1.3 %collective-permute-start.11 = (f32[288,128]{1,0:T(8,128)S(1)}, f32[288,128]{1,0:T(8,128)S(1)}, u32[]{:S(2)}, u32[]{:S(2)}) collective-permute-start(f32[288,128]{1,0:T(8,128)S(1)} %total_state.3), channel_id=1, source_target_pairs={{8,0},{10,2},{12,4},{14,6},{16,8},{18,10},{20,12},{22,14},{24,16},... | collective-permute-start | bytes 442376 | tf_op jit(solution)/shard_map/ppermute | solution.py:418
  43.4 6.2 %collective-permute-done.11.refs_8_ = f32[288,128]{1,0:T(8,128)S(1)} collective-permute-done((f32[288,128]{1,0:T(8,128)S(1)}, f32[288,128]{1,0:T(8,128)S(1)}, u32[]{:S(2)}, u32[]{:S(2)}) %collective-permute-start.11) | collective-permute-done | bytes 147488 | tf_op jit(solution)/shard_map/ppermute | solution.py:418
  50.3 1.3 %collective-permute-start.13 = (f32[288,128]{1,0:T(8,128)S(1)}, f32[288,128]{1,0:T(8,128)S(1)}, u32[]{:S(2)}, u32[]{:S(2)}) collective-permute-start(f32[288,128]{1,0:T(8,128)S(1)} %get-tuple-element.64), channel_id=1, source_target_pairs={{0,4},{2,6},{4,0},{6,2},{8,12},{10,14},{12,8},{14,10},{16,20},{18,... | collective-permute-start | bytes 442376 | tf_op jit(solution)/shard_map/ppermute | solution.py:410
  51.6 1.6 %collective-permute-start.14 = (f32[288,128]{1,0:T(8,128)S(1)}, f32[288,128]{1,0:T(8,128)S(1)}, u32[]{:S(2)}, u32[]{:S(2)}) collective-permute-start(f32[288,128]{1,0:T(8,128)S(1)} %get-tuple-element.65), channel_id=1, source_target_pairs={{0,6},{2,4},{4,2},{6,0},{8,14},{10,12},{12,10},{14,8},{16,22},{18,... | collective-permute-start | bytes 442376 | tf_op jit(solution)/shard_map/ppermute | solution.py:410
  53.2 4.2 %local_grads.1 = (bf16[128,1536]{1,0:T(8,128)(2,1)}, bf16[128,1536]{1,0:T(8,128)(2,1)}, f32[128,1536]{1,0:T(8,128)S(1)}, f32[128,1536]{1,0:T(8,128)S(1)}, bf16[128,1536]{1,0:T(8,128)(2,1)S(1)}) custom-call(s32[16]{0:T(128)} %lengths_ref.3, f32[16,128]{1,0:T(8,128)S(1)} %copy-done.3, bf16[128,1536]{1,0:T(8,128)(2,1)S(1)} %copy-done.4, ...), custom_call_target="tpu_custom_call" | custom-call | flops 1000000000 | bytes 6010880 | tf_op jit(solution)/shard_map/local_grads/pallas_call | solution.py:392
  57.4 0.9 %collective-permute-done.13.refs_2_ = f32[288,128]{1,0:T(8,128)S(1)} collective-permute-done((f32[288,128]{1,0:T(8,128)S(1)}, f32[288,128]{1,0:T(8,128)S(1)}, u32[]{:S(2)}, u32[]{:S(2)}) %collective-permute-start.13) | collective-permute-done | bytes 147488 | tf_op jit(solution)/shard_map/ppermute | solution.py:410
  58.2 1.6 %key_value_grads.1 = (bf16[128,1536]{1,0:T(8,128)(2,1)}, bf16[128,1536]{1,0:T(8,128)(2,1)}) custom-call(f32[128,1536]{1,0:T(8,128)S(1)} %get-tuple-element.54.key_local_ref, f32[128,1536]{1,0:T(8,128)S(1)} %get-tuple-element.55.value_local_ref, bf16[128,1536]{1,0:T(8,128)(2,1)S(1)} %get-tuple-element.56.weighted_values_ref, ...), custom_call_target="tpu_custom_call" | custom-call | bytes 3735552 | tf_op jit(solution)/shard_map/key_value_grads/pallas_call | solution.py:392
  (29 shorter events, 3.4 us)
Async XLA Ops:
  2.6 7.7 %collective-permute-start = (f32[304,128]{1,0:T(8,128)S(1)}, f32[304,128]{1,0:T(8,128)S(1)}, u32[]{:S(2)}, u32[]{:S(2)}) collective-permute-start(f32[304,128]{1,0:T(8,128)S(1)} %get-tuple-element.39), channel_id=1, source_target_pairs={{0,2},{2,0},{4,6},{6,4},{8,10},{10,8},{12,14},{14,12},{16,18},{18,... | collective-permute-start | bytes 466952 | tf_op jit(solution)/shard_map/ppermute | solution.py:410
  5.6 8.8 %collective-permute-start.1 = (f32[304,128]{1,0:T(8,128)S(1)}, f32[304,128]{1,0:T(8,128)S(1)}, u32[]{:S(2)}, u32[]{:S(2)}) collective-permute-start(f32[304,128]{1,0:T(8,128)S(1)} %get-tuple-element.40), channel_id=1, source_target_pairs={{0,4},{2,6},{4,0},{6,2},{8,12},{10,14},{12,8},{14,10},{16,20},{18,... | collective-permute-start | bytes 466952 | tf_op jit(solution)/shard_map/ppermute | solution.py:410
  7.1 7.3 %collective-permute-start.2 = (f32[304,128]{1,0:T(8,128)S(1)}, f32[304,128]{1,0:T(8,128)S(1)}, u32[]{:S(2)}, u32[]{:S(2)}) collective-permute-start(f32[304,128]{1,0:T(8,128)S(1)} %get-tuple-element.41), channel_id=1, source_target_pairs={{0,6},{2,4},{4,2},{6,0},{8,14},{10,12},{12,10},{14,8},{16,22},{18,... | collective-permute-start | bytes 466952 | tf_op jit(solution)/shard_map/ppermute | solution.py:410
  14.5 10.0 %copy-start.1 = (bf16[128,1536]{1,0:T(8,128)(2,1)S(1)}, bf16[128,1536]{1,0:T(8,128)(2,1)}, u32[]{:S(2)}) copy-start(bf16[128,1536]{1,0:T(8,128)(2,1)} %keys_ref.3) | copy-start | bytes 1179652
  14.5 10.0 %copy-start.2 = (bf16[128,1536]{1,0:T(8,128)(2,1)S(1)}, bf16[128,1536]{1,0:T(8,128)(2,1)}, u32[]{:S(2)}) copy-start(bf16[128,1536]{1,0:T(8,128)(2,1)} %values_ref.3) | copy-start | bytes 1179652
  14.5 10.0 %copy-start.4 = (bf16[128,1536]{1,0:T(8,128)(2,1)S(1)}, bf16[128,1536]{1,0:T(8,128)(2,1)}, u32[]{:S(2)}) copy-start(bf16[128,1536]{1,0:T(8,128)(2,1)} %queries_ref.3) | copy-start | bytes 1179652
  14.5 6.3 %collective-permute-start.3 = (f32[288,128]{1,0:T(8,128)S(1)}, f32[288,128]{1,0:T(8,128)S(1)}, u32[]{:S(2)}, u32[]{:S(2)}) collective-permute-start(f32[288,128]{1,0:T(8,128)S(1)} %total_state.2), channel_id=1, source_target_pairs={{0,8},{2,10},{4,12},{6,14},{8,16},{10,18},{12,20},{14,22},{16,24},... | collective-permute-start | bytes 442376 | tf_op jit(solution)/shard_map/ppermute | solution.py:418
  20.8 3.6 %copy-start.5 = (f32[1536]{0:T(1024)S(1)}, f32[1536]{0:T(1024)}, u32[]{:S(2)}) copy-start(f32[1536]{0:T(1024)} %param.11) | copy-start | bytes 18436
  20.9 6.1 %collective-permute-start.4 = (f32[288,128]{1,0:T(8,128)S(1)}, f32[288,128]{1,0:T(8,128)S(1)}, u32[]{:S(2)}, u32[]{:S(2)}) collective-permute-start(f32[288,128]{1,0:T(8,128)S(1)} %get-tuple-element.43), channel_id=1, source_target_pairs={{0,2},{2,0},{4,6},{6,4},{8,10},{10,8},{12,14},{14,12},{16,18},{18,... | collective-permute-start | bytes 442376 | tf_op jit(solution)/shard_map/ppermute | solution.py:410
  22.2 2.3 %copy-start.3 = (f32[16,128]{1,0:T(8,128)S(1)}, f32[16,128]{1,0:T(8,128)}, u32[]{:S(2)}) copy-start(f32[16,128]{1,0:T(8,128)} %decay_ref.3) | copy-start | bytes 24580
  22.2 5.2 %collective-permute-start.5 = (f32[288,128]{1,0:T(8,128)S(1)}, f32[288,128]{1,0:T(8,128)S(1)}, u32[]{:S(2)}, u32[]{:S(2)}) collective-permute-start(f32[288,128]{1,0:T(8,128)S(1)} %get-tuple-element.44), channel_id=1, source_target_pairs={{0,4},{2,6},{4,0},{6,2},{8,12},{10,14},{12,8},{14,10},{16,20},{18,... | collective-permute-start | bytes 442376 | tf_op jit(solution)/shard_map/ppermute | solution.py:410
  23.0 6.0 %collective-permute-start.6 = (f32[288,128]{1,0:T(8,128)S(1)}, f32[288,128]{1,0:T(8,128)S(1)}, u32[]{:S(2)}, u32[]{:S(2)}) collective-permute-start(f32[288,128]{1,0:T(8,128)S(1)} %get-tuple-element.45), channel_id=1, source_target_pairs={{0,6},{2,4},{4,2},{6,0},{8,14},{10,12},{12,10},{14,8},{16,22},{18,... | collective-permute-start | bytes 442376 | tf_op jit(solution)/shard_map/ppermute | solution.py:410
  24.5 4.5 %copy-start = (bf16[128,1536]{1,0:T(8,128)(2,1)S(1)}, bf16[128,1536]{1,0:T(8,128)(2,1)}, u32[]{:S(2)}) copy-start(bf16[128,1536]{1,0:T(8,128)(2,1)} %out_grad_ref.3) | copy-start | bytes 1179652
  29.6 1.3 %collective-permute-start.7 = (f32[128,128]{1,0:T(8,128)S(1)}, f32[128,128]{1,0:T(8,128)S(1)}, u32[]{:S(2)}, u32[]{:S(2)}) collective-permute-start(f32[128,128]{1,0:T(8,128)S(1)} %get-tuple-element.47.sums_ref), channel_id=1, source_target_pairs={{0,1},{1,0},{2,3},{3,2},{4,5},{5,4},{6,7},{7,6},{8,9},{9,8},{10,11... | collective-permute-start | bytes 196616 | tf_op jit(solution)/shard_map/ppermute | solution.py:508
  31.6 6.7 %collective-permute-start.8 = (f32[288,128]{1,0:T(8,128)S(1)}, f32[288,128]{1,0:T(8,128)S(1)}, u32[]{:S(2)}, u32[]{:S(2)}) collective-permute-start(f32[288,128]{1,0:T(8,128)S(1)} %get-tuple-element.59), channel_id=1, source_target_pairs={{0,2},{2,0},{4,6},{6,4},{8,10},{10,8},{12,14},{14,12},{16,18},{18,... | collective-permute-start | bytes 442376 | tf_op jit(solution)/shard_map/ppermute | solution.py:410
  33.2 8.8 %collective-permute-start.9 = (f32[288,128]{1,0:T(8,128)S(1)}, f32[288,128]{1,0:T(8,128)S(1)}, u32[]{:S(2)}, u32[]{:S(2)}) collective-permute-start(f32[288,128]{1,0:T(8,128)S(1)} %get-tuple-element.60), channel_id=1, source_target_pairs={{0,4},{2,6},{4,0},{6,2},{8,12},{10,14},{12,8},{14,10},{16,20},{18,... | collective-permute-start | bytes 442376 | tf_op jit(solution)/shard_map/ppermute | solution.py:410
  33.9 8.1 %collective-permute-start.10 = (f32[288,128]{1,0:T(8,128)S(1)}, f32[288,128]{1,0:T(8,128)S(1)}, u32[]{:S(2)}, u32[]{:S(2)}) collective-permute-start(f32[288,128]{1,0:T(8,128)S(1)} %get-tuple-element.61), channel_id=1, source_target_pairs={{0,6},{2,4},{4,2},{6,0},{8,14},{10,12},{12,10},{14,8},{16,22},{18,... | collective-permute-start | bytes 442376 | tf_op jit(solution)/shard_map/ppermute | solution.py:410
  42.1 7.5 %collective-permute-start.11 = (f32[288,128]{1,0:T(8,128)S(1)}, f32[288,128]{1,0:T(8,128)S(1)}, u32[]{:S(2)}, u32[]{:S(2)}) collective-permute-start(f32[288,128]{1,0:T(8,128)S(1)} %total_state.3), channel_id=1, source_target_pairs={{8,0},{10,2},{12,4},{14,6},{16,8},{18,10},{20,12},{22,14},{24,16},... | collective-permute-start | bytes 442376 | tf_op jit(solution)/shard_map/ppermute | solution.py:418
  49.6 7.8 %collective-permute-start.12 = (f32[288,128]{1,0:T(8,128)S(1)}, f32[288,128]{1,0:T(8,128)S(1)}, u32[]{:S(2)}, u32[]{:S(2)}) collective-permute-start(f32[288,128]{1,0:T(8,128)S(1)} %get-tuple-element.63), channel_id=1, source_target_pairs={{0,2},{2,0},{4,6},{6,4},{8,10},{10,8},{12,14},{14,12},{16,18},{18,... | collective-permute-start | bytes 442376 | tf_op jit(solution)/shard_map/ppermute | solution.py:410
  50.3 7.9 %collective-permute-start.13 = (f32[288,128]{1,0:T(8,128)S(1)}, f32[288,128]{1,0:T(8,128)S(1)}, u32[]{:S(2)}, u32[]{:S(2)}) collective-permute-start(f32[288,128]{1,0:T(8,128)S(1)} %get-tuple-element.64), channel_id=1, source_target_pairs={{0,4},{2,6},{4,0},{6,2},{8,12},{10,14},{12,8},{14,10},{16,20},{18,... | collective-permute-start | bytes 442376 | tf_op jit(solution)/shard_map/ppermute | solution.py:410
  51.6 6.6 %collective-permute-start.14 = (f32[288,128]{1,0:T(8,128)S(1)}, f32[288,128]{1,0:T(8,128)S(1)}, u32[]{:S(2)}, u32[]{:S(2)}) collective-permute-start(f32[288,128]{1,0:T(8,128)S(1)} %get-tuple-element.65), channel_id=1, source_target_pairs={{0,6},{2,4},{4,2},{6,0},{8,14},{10,12},{12,10},{14,8},{16,22},{18,... | collective-permute-start | bytes 442376 | tf_op jit(solution)/shard_map/ppermute | solution.py:410

commit v3 on v2

--- a/solution.py
+++ b/solution.py
@@ -131,6 +131,57 @@
     return jnp.concatenate(
         [jnp.where(head_mask(plan, k), x, jnp.zeros_like(x)) for k in range(plan.group)], axis=0
     )
+
+
+def windows(plan):
+    for h in range(0, plan.group, 2):
+        heads = range(h, min(h + 2, plan.group))
+        start = heads[0] * plan.dim // 128 * 128
+        yield heads, start, -(-(heads[-1] + 1) * plan.dim // 128) * 128
+
+
+def block_diagonal(plan, x, heads, start, stop):
+    zeros = lambda rows: [jnp.zeros((rows, stop - start), x.dtype)] if rows else []
+    x = x[:, start:stop]
+    lane = iota((1, stop - start), 1) + start
+    parts = zeros(heads[0] * plan.dim - start)
+    for h in heads:
+        on = (lane >= h * plan.dim) & (lane < (h + 1) * plan.dim)
+        parts.append(jnp.where(on, x, jnp.zeros_like(x)))
+    parts += zeros(stop - (heads[-1] + 1) * plan.dim)
+    return jnp.concatenate(parts, axis=0)
+
+
+def sum_windows(plan, terms):
+    tiles = [None] * (plan.lanes // 128)
+    for start, stop, term in terms:
+        for j in range(start // 128, stop // 128):
+            tile = term[:, j * 128 - start : (j + 1) * 128 - start]
+            tiles[j] = tile if tiles[j] is None else tiles[j] + tile
+    return jnp.concatenate(tiles, axis=1)
+
+
+def through_states(plan, x, state, dims):
+    return sum_windows(
+        plan,
+        [
+            (start, stop, dot(x[:, start:stop], block_diagonal(plan, state, heads, start, stop), dims))
+            for heads, start, stop in windows(plan)
+        ],
+    )
+
+
+def outer_states(plan, x, y):
+    terms = []
+    for heads, start, stop in windows(plan):
+        product = dot(x[:, start:stop], y[:, start:stop], TN)
+        lane = iota((1, stop - start), 1) + start
+        out = jnp.zeros((plan.dim, stop - start), F32)
+        for h in heads:
+            on = (lane >= h * plan.dim) & (lane < (h + 1) * plan.dim)
+            out = jnp.where(on, product[h * plan.dim - start : (h + 1) * plan.dim - start], out)
+        terms.append((start, stop, out))
+    return sum_windows(plan, terms)
 
 
 def lanes_of(plan, g):
@@ -204,21 +255,26 @@
         copy.wait()
     for g in range(plan.groups):
         at = lanes_of(plan, g)
-        state_ref[:, at] = own_heads(plan, dot(weighted_ref[:, at], values_ref[:, at], TN), plan.dim)
+        state_ref[:, at] = outer_states(plan, weighted_ref[:, at], values_ref[:, at])
     store_pieces(plan, mine, state_ref, pieces)
 
 
-def chain_kernel(plan, reverse, with_carry, *refs):
+def chain_kernel(plan, reverse, with_carry, groups, *refs):
     n, rows = plan.pieces, plan.rows
     pieces, factors = refs[:n], refs[n : 2 * n]
-    carry_ref = refs[2 * n] if with_carry else None
-    outs = refs[2 * n + 1 :] if with_carry else refs[2 * n :]
+    hops = refs[2 * n : 2 * n + 2]
+    outs = refs[2 * n + 2 :] if with_carry else refs[2 * n :]
+    group = lax.axis_index("ctx") // n
+    end = groups - 1 if reverse else 0
+    by_first = lax.rem(group, 2) == (0 if reverse else 1)
     order = range(n - 1, -1, -1) if reverse else range(n)
 
     def at_place(mine):
         for j in range(plan.tiles):
             at = slice(j * rows, (j + 1) * rows)
-            tile = carry_ref[at] if with_carry else None
+            tile = None
+            if with_carry:
+                tile = jnp.where(group == end, 0.0, jnp.where(by_first, hops[0][at], hops[1][at]))
             for step, b in enumerate(order):
                 m = mine ^ b
                 if with_carry:
@@ -270,7 +326,7 @@
         at = lanes_of(plan, g)
         incoming = state_ref[:, at].astype(BF16)
         incoming_ref[:, at] = incoming
-        attended = local_ref[:, at] + dot(reached_ref[:, at], stack_heads(plan, incoming))
+        attended = local_ref[:, at] + through_states(plan, reached_ref[:, at], incoming, NN)
         attended_ref[:, at] = attended
         grad = out_grad_ref[:, at].astype(F32) * gain_ref[:, at]
         square, product = attended * attended, grad * attended
@@ -296,7 +352,7 @@
         grad = out_grad_ref[:, at].astype(F32) * gain_ref[:, at]
         attended_grad = (grad * inverse - attended_ref[:, at] * slope).astype(BF16)
         attended_grad_ref[:, at] = attended_grad
-        state_ref[:, at] = own_heads(plan, dot(reached_ref[:, at], attended_grad, TN), plan.dim)
+        state_ref[:, at] = outer_states(plan, reached_ref[:, at], attended_grad)
     store_pieces(plan, place(plan)[1], state_ref, pieces)
 
 
@@ -344,7 +400,7 @@
         score_grads = jnp.concatenate(score_grads, axis=1)
         probs = probs_ref[:, g * plan.group * n : (g + 1) * plan.group * n]
         query_grad = dot(score_grads, stack_heads(plan, keys))
-        query_grad += reach[:, at] * dot(grads, stack_heads(plan, incoming_ref[:, at]), NT)
+        query_grad += reach[:, at] * through_states(plan, grads, incoming_ref[:, at], NT)
         query_grad_ref[:, at] = query_grad.astype(BF16)
         key_local_ref[:, at] = own_heads(plan, dot(score_grads, queries, TN), n)
         value_local_ref[:, at] = own_heads(plan, dot(probs, grads, TN), n)
@@ -361,14 +417,14 @@
     copies = []
     for g in range(plan.groups):
         at = lanes_of(plan, g)
-        later = stack_heads(plan, state_ref[:, at].astype(BF16))
-        key_grad = key_local_ref[:, at] + dot(weighted_values_ref[:, at], later, NT)
+        later = state_ref[:, at].astype(BF16)
+        key_grad = key_local_ref[:, at] + through_states(plan, weighted_values_ref[:, at], later, NT)
         key_grad_ref[:, at] = key_grad.astype(BF16)
         copies.append(
             pltpu.make_async_copy(key_grad_ref.at[:, at], key_grad_hbm.at[:, at], key_sems.at[g])
         )
         copies[-1].start()
-        value_grad = value_local_ref[:, at] + dot(weighted_keys_ref[:, at], later)
+        value_grad = value_local_ref[:, at] + through_states(plan, weighted_keys_ref[:, at], later, NN)
         value_grad_ref[:, at] = value_grad.astype(BF16)
         copies.append(
             pltpu.make_async_copy(value_grad_ref.at[:, at], value_grad_hbm.at[:, at], value_sems.at[g])
@@ -418,6 +474,12 @@
     return lax.ppermute(x, "ctx", pairs)
 
 
+def group_swaps(n, count):
+    first = [(i, i ^ n) for i in range(count)]
+    second = [(i, i ^ 1 if i < n or i >= count - n else (((i // n - 1) ^ 1) + 1) * n + i % n) for i in range(count)]
+    return first, second
+
+
 def scan_whole(plan, state, factor, count, reach, sign):
     held = shift(state, count, sign)
     rates = shift(factor, count, sign)
@@ -435,7 +497,7 @@
     count = lax.axis_size("ctx")
     features = width * lax.axis_size("head")
     reach = count // 4
-    even = reach & (reach - 1) == 0 and (width // heads) % (8 * reach) == 0
+    even = reach > 1 and reach & (reach - 1) == 0 and (width // heads) % (8 * reach) == 0
     plan = Plan(tokens, width, heads, reach if even else 1)
     n = plan.pieces
     gain = norm_gain.reshape(1, width)
@@ -471,10 +533,10 @@
     def chain(pieces, reverse, carry=None):
         with_carry = carry is not None
         return call(
-            functools.partial(chain_kernel, plan, reverse, with_carry),
+            functools.partial(chain_kernel, plan, reverse, with_carry, count // n),
             "prefix_states" if with_carry else "total_state",
             (),
-            (*pieces, *frames, carry) if with_carry else (*pieces, *frames),
+            (*pieces, *frames, *carry) if with_carry else (*pieces, *frames),
             [piece] * n if with_carry else [piece],
         )
 
@@ -485,7 +547,7 @@
             factor = frames[0][plan.piece_rows : plan.piece_rows + plan.tiles, None, :]
             return [scan_whole(plan, whole, factor, count, reach, sign).reshape(piece.shape)]
         (total,) = chain(pieces, reverse)
-        carry = shift(total, count, sign * n)
+        carry = [lax.ppermute(total, "ctx", pairs) for pairs in group_swaps(n, count)]
         return exchange(chain(pieces, reverse, carry), count)
 
     incoming = entering(pieces, False)

time: 60.1 us -> 57.7 us (0.960)
  waiting for transfers between devices: 27.1 us -> 24.3 us
  starting transfers between devices: 20.2 us -> 21 us
    ppermute x2 -> x4, waiting for transfers between devices: 8.84 us -> 6.78 us  [entering(): lax.ppermute(total, 'ctx', pairs)]
    ppermute x2 -> x4, starting transfers between devices: 4.91 us -> 5.75 us  [entering(): lax.ppermute(total, 'ctx', pairs)]
    ppermute x12, waiting for transfers between devices: 17 us -> 16.3 us  [exchange(): lax.ppermute(piece, 'ctx', [(i, i ^ m) for i in range(count)])]
  transfers between devices with their start and end apart: 15 -> 17, of which waited for: 10 -> 12; matrix products, arithmetic and copies ran while one was open for 0% -> 0% of each run, Pallas kernels for 11% -> 12%
where the time goes in v3:
time: 57.7 us; the launch traced here: 57.5 us
  waiting for transfers between devices  24.3 us (42%)
  starting transfers between devices  21 us (36%)
  Pallas kernels  11.4 us (20%)
  between operations  0.8 us (1%)
    ppermute x12, waiting for transfers between devices, exchange(): lax.ppermute(piece, 'ctx', [(i, i ^ m) for i in range(count)])  16.3 us
    ppermute x12, starting transfers between devices, exchange(): lax.ppermute(piece, 'ctx', [(i, i ^ m) for i in range(count)])  15.2 us
    pallas_call x10, Pallas kernels, call(): pl.pallas_call(kernel, name=name, out_shape=outs, in_specs=[SCALAR] * len...  11.4 us
    ppermute x4, waiting for transfers between devices, entering(): lax.ppermute(total, 'ctx', pairs)  6.78 us
    ppermute x4, starting transfers between devices, entering(): lax.ppermute(total, 'ctx', pairs)  5.75 us
    ppermute x1, waiting for transfers between devices, on_device(): other = lax.ppermute(sums, 'head', [(0, 1), (1, 0)])  1.24 us
  transfers between devices with their start and end apart: 17, of which 12 were waited for; matrix products, arithmetic and copies ran while one was open for 0% of the time, Pallas kernels for 12%

profile of v3, /device:TPU:0, one launch (start us, length us, event | category | flops | bytes accessed | tf_op | source)
XLA Modules:
  0.0 57.5 jit_solution(2705464759013103677)
XLA Ops:
  0.6 2.0 %exit_states.1 = (f32[304,128]{1,0:T(8,128)S(1)}, f32[304,128]{1,0:T(8,128)S(1)}, f32[304,128]{1,0:T(8,128)S(1)}, f32[304,128]{1,0:T(8,128)S(1)}, bf16[128,1536]{1,0:T(8,128)(2,1)S(1)}) custom-call(s32[16]{0:T(128)} %lengths_ref.3, f32[16,128]{1,0:T(8,128)} %decay_ref.3, bf16[128,1536]{1,0:T(8,128)(2,1)} %keys_ref.3, bf16[128,1536]{1,0:T(8,128)(2,1)} %values_ref.3), custom_call_target="tpu_custom_call" | custom-call | flops 100000000 | bytes 1810496 | tf_op jit(solution)/shard_map/exit_states/pallas_call | solution.py:448
  2.6 3.0 %collective-permute-start = (f32[304,128]{1,0:T(8,128)S(1)}, f32[304,128]{1,0:T(8,128)S(1)}, u32[]{:S(2)}, u32[]{:S(2)}) collective-permute-start(f32[304,128]{1,0:T(8,128)S(1)} %get-tuple-element.39), channel_id=1, source_target_pairs={{0,2},{2,0},{4,6},{6,4},{8,10},{10,8},{12,14},{14,12},{16,18},{18,... | collective-permute-start | bytes 466952 | tf_op jit(solution)/shard_map/ppermute | solution.py:466
  5.6 1.5 %collective-permute-start.1 = (f32[304,128]{1,0:T(8,128)S(1)}, f32[304,128]{1,0:T(8,128)S(1)}, u32[]{:S(2)}, u32[]{:S(2)}) collective-permute-start(f32[304,128]{1,0:T(8,128)S(1)} %get-tuple-element.40), channel_id=1, source_target_pairs={{0,4},{2,6},{4,0},{6,2},{8,12},{10,14},{12,8},{14,10},{16,20},{18,... | collective-permute-start | bytes 466952 | tf_op jit(solution)/shard_map/ppermute | solution.py:466
  7.1 3.1 %collective-permute-done.refs_1_.refs_5_ = f32[304,128]{1,0:T(8,128)S(1)} collective-permute-done((f32[304,128]{1,0:T(8,128)S(1)}, f32[304,128]{1,0:T(8,128)S(1)}, u32[]{:S(2)}, u32[]{:S(2)}) %collective-permute-start) | collective-permute-done | bytes 155680 | tf_op jit(solution)/shard_map/ppermute | solution.py:466
  10.3 4.2 %collective-permute-done.1.refs_2_.refs_6_ = f32[304,128]{1,0:T(8,128)S(1)} collective-permute-done((f32[304,128]{1,0:T(8,128)S(1)}, f32[304,128]{1,0:T(8,128)S(1)}, u32[]{:S(2)}, u32[]{:S(2)}) %collective-permute-start.1) | collective-permute-done | bytes 155680 | tf_op jit(solution)/shard_map/ppermute | solution.py:466
  14.5 1.3 %collective-permute-start.4 = (f32[288,128]{1,0:T(8,128)S(1)}, f32[288,128]{1,0:T(8,128)S(1)}, u32[]{:S(2)}, u32[]{:S(2)}) collective-permute-start(f32[288,128]{1,0:T(8,128)S(1)} %total_state.2), channel_id=1, source_target_pairs={{0,2},{2,0},{4,6},{6,4},{8,16},{10,18},{12,20},{14,22},{16,8},{18,... | collective-permute-start | bytes 442376 | tf_op jit(solution)/shard_map/ppermute | solution.py:550
  15.8 1.9 %collective-permute-start.3 = (f32[288,128]{1,0:T(8,128)S(1)}, f32[288,128]{1,0:T(8,128)S(1)}, u32[]{:S(2)}, u32[]{:S(2)}) collective-permute-start(f32[288,128]{1,0:T(8,128)S(1)} %total_state.2), channel_id=1, source_target_pairs={{0,8},{2,10},{4,12},{6,14},{8,0},{10,2},{12,4},{14,6},{16,24},{18,... | collective-permute-start | bytes 442376 | tf_op jit(solution)/shard_map/ppermute | solution.py:550
  17.8 2.0 %collective-permute-done.4.refs_9_ = f32[288,128]{1,0:T(8,128)S(1)} collective-permute-done((f32[288,128]{1,0:T(8,128)S(1)}, f32[288,128]{1,0:T(8,128)S(1)}, u32[]{:S(2)}, u32[]{:S(2)}) %collective-permute-start.4) | collective-permute-done | bytes 147488 | tf_op jit(solution)/shard_map/ppermute | solution.py:550
  19.7 1.2 %collective-permute-done.3.refs_8_ = f32[288,128]{1,0:T(8,128)S(1)} collective-permute-done((f32[288,128]{1,0:T(8,128)S(1)}, f32[288,128]{1,0:T(8,128)S(1)}, u32[]{:S(2)}, u32[]{:S(2)}) %collective-permute-start.3) | collective-permute-done | bytes 147488 | tf_op jit(solution)/shard_map/ppermute | solution.py:550
  21.1 1.2 %collective-permute-start.5 = (f32[288,128]{1,0:T(8,128)S(1)}, f32[288,128]{1,0:T(8,128)S(1)}, u32[]{:S(2)}, u32[]{:S(2)}) collective-permute-start(f32[288,128]{1,0:T(8,128)S(1)} %get-tuple-element.43), channel_id=1, source_target_pairs={{0,2},{2,0},{4,6},{6,4},{8,10},{10,8},{12,14},{14,12},{16,18},{18,... | collective-permute-start | bytes 442376 | tf_op jit(solution)/shard_map/ppermute | solution.py:466
  23.4 1.2 %collective-permute-start.7 = (f32[288,128]{1,0:T(8,128)S(1)}, f32[288,128]{1,0:T(8,128)S(1)}, u32[]{:S(2)}, u32[]{:S(2)}) collective-permute-start(f32[288,128]{1,0:T(8,128)S(1)} %get-tuple-element.45), channel_id=1, source_target_pairs={{0,6},{2,4},{4,2},{6,0},{8,14},{10,12},{12,10},{14,8},{16,22},{18,... | collective-permute-start | bytes 442376 | tf_op jit(solution)/shard_map/ppermute | solution.py:466
  24.7 2.5 %local_attention.1 = (bf16[128,2048]{1,0:T(8,128)(2,1)S(1)}, f32[128,1536]{1,0:T(8,128)S(1)}, bf16[128,1536]{1,0:T(8,128)(2,1)S(1)}) custom-call(s32[16]{0:T(128)} %lengths_ref.3, f32[16,128]{1,0:T(8,128)S(1)} %copy-done.3, bf16[128,1536]{1,0:T(8,128)(2,1)S(1)} %copy-done.4, bf16[128,1536]{1,0:T(8,128)(2,1)S(1)} %copy-done.1, bf16[128,1536]{1,0:T(8,128)(2,1)S(1)} %copy-done.2), custom_call_target="tpu_custom_call" | custom-call | flops 1000000000 | bytes 2891776 | tf_op jit(solution)/shard_map/local_attention/pallas_call | solution.py:448
  27.4 2.1 %collective-permute-done.7.refs_3_ = f32[288,128]{1,0:T(8,128)S(1)} collective-permute-done((f32[288,128]{1,0:T(8,128)S(1)}, f32[288,128]{1,0:T(8,128)S(1)}, u32[]{:S(2)}, u32[]{:S(2)}) %collective-permute-start.7) | collective-permute-done | bytes 147488 | tf_op jit(solution)/shard_map/ppermute | solution.py:466
  30.0 1.2 %collective-permute-done.8.other_ref = f32[128,128]{1,0:T(8,128)S(1)} collective-permute-done((f32[128,128]{1,0:T(8,128)S(1)}, f32[128,128]{1,0:T(8,128)S(1)}, u32[]{:S(2)}, u32[]{:S(2)}) %collective-permute-start.8) | collective-permute-done | bytes 65568 | tf_op jit(solution)/shard_map/ppermute | solution.py:570
  31.9 1.2 %collective-permute-start.9 = (f32[288,128]{1,0:T(8,128)S(1)}, f32[288,128]{1,0:T(8,128)S(1)}, u32[]{:S(2)}, u32[]{:S(2)}) collective-permute-start(f32[288,128]{1,0:T(8,128)S(1)} %get-tuple-element.59), channel_id=1, source_target_pairs={{0,2},{2,0},{4,6},{6,4},{8,10},{10,8},{12,14},{14,12},{16,18},{18,... | collective-permute-start | bytes 442376 | tf_op jit(solution)/shard_map/ppermute | solution.py:466
  33.8 1.6 %collective-permute-start.11 = (f32[288,128]{1,0:T(8,128)S(1)}, f32[288,128]{1,0:T(8,128)S(1)}, u32[]{:S(2)}, u32[]{:S(2)}) collective-permute-start(f32[288,128]{1,0:T(8,128)S(1)} %get-tuple-element.61), channel_id=1, source_target_pairs={{0,6},{2,4},{4,2},{6,0},{8,14},{10,12},{12,10},{14,8},{16,22},{18,... | collective-permute-start | bytes 442376 | tf_op jit(solution)/shard_map/ppermute | solution.py:466
  35.5 3.2 %collective-permute-done.9.refs_1_ = f32[288,128]{1,0:T(8,128)S(1)} collective-permute-done((f32[288,128]{1,0:T(8,128)S(1)}, f32[288,128]{1,0:T(8,128)S(1)}, u32[]{:S(2)}, u32[]{:S(2)}) %collective-permute-start.9) | collective-permute-done | bytes 147488 | tf_op jit(solution)/shard_map/ppermute | solution.py:466
  38.7 3.2 %collective-permute-done.10.refs_2_ = f32[288,128]{1,0:T(8,128)S(1)} collective-permute-done((f32[288,128]{1,0:T(8,128)S(1)}, f32[288,128]{1,0:T(8,128)S(1)}, u32[]{:S(2)}, u32[]{:S(2)}) %collective-permute-start.10) | collective-permute-done | bytes 147488 | tf_op jit(solution)/shard_map/ppermute | solution.py:466
  42.9 1.6 %collective-permute-start.12 = (f32[288,128]{1,0:T(8,128)S(1)}, f32[288,128]{1,0:T(8,128)S(1)}, u32[]{:S(2)}, u32[]{:S(2)}) collective-permute-start(f32[288,128]{1,0:T(8,128)S(1)} %total_state.3), channel_id=1, source_target_pairs={{0,8},{2,10},{4,12},{6,14},{8,0},{10,2},{12,4},{14,6},{16,24},{18,... | collective-permute-start | bytes 442376 | tf_op jit(solution)/shard_map/ppermute | solution.py:550
  44.5 2.7 %collective-permute-done.13.refs_9_ = f32[288,128]{1,0:T(8,128)S(1)} collective-permute-done((f32[288,128]{1,0:T(8,128)S(1)}, f32[288,128]{1,0:T(8,128)S(1)}, u32[]{:S(2)}, u32[]{:S(2)}) %collective-permute-start.13) | collective-permute-done | bytes 147488 | tf_op jit(solution)/shard_map/ppermute | solution.py:550
  48.2 1.2 %collective-permute-start.14 = (f32[288,128]{1,0:T(8,128)S(1)}, f32[288,128]{1,0:T(8,128)S(1)}, u32[]{:S(2)}, u32[]{:S(2)}) collective-permute-start(f32[288,128]{1,0:T(8,128)S(1)} %get-tuple-element.63), channel_id=1, source_target_pairs={{0,2},{2,0},{4,6},{6,4},{8,10},{10,8},{12,14},{14,12},{16,18},{18,... | collective-permute-start | bytes 442376 | tf_op jit(solution)/shard_map/ppermute | solution.py:466
  50.1 1.6 %collective-permute-start.16 = (f32[288,128]{1,0:T(8,128)S(1)}, f32[288,128]{1,0:T(8,128)S(1)}, u32[]{:S(2)}, u32[]{:S(2)}) collective-permute-start(f32[288,128]{1,0:T(8,128)S(1)} %get-tuple-element.65), channel_id=1, source_target_pairs={{0,6},{2,4},{4,2},{6,0},{8,14},{10,12},{12,10},{14,8},{16,22},{18,... | collective-permute-start | bytes 442376 | tf_op jit(solution)/shard_map/ppermute | solution.py:466
  51.7 4.2 %local_grads.1 = (bf16[128,1536]{1,0:T(8,128)(2,1)}, bf16[128,1536]{1,0:T(8,128)(2,1)}, f32[128,1536]{1,0:T(8,128)S(1)}, f32[128,1536]{1,0:T(8,128)S(1)}, bf16[128,1536]{1,0:T(8,128)(2,1)S(1)}) custom-call(s32[16]{0:T(128)} %lengths_ref.3, f32[16,128]{1,0:T(8,128)S(1)} %copy-done.3, bf16[128,1536]{1,0:T(8,128)(2,1)S(1)} %copy-done.4, ...), custom_call_target="tpu_custom_call" | custom-call | flops 1000000000 | bytes 6010880 | tf_op jit(solution)/shard_map/local_grads/pallas_call | solution.py:448
  56.2 1.3 %key_value_grads.1 = (bf16[128,1536]{1,0:T(8,128)(2,1)}, bf16[128,1536]{1,0:T(8,128)(2,1)}) custom-call(f32[128,1536]{1,0:T(8,128)S(1)} %get-tuple-element.54.key_local_ref, f32[128,1536]{1,0:T(8,128)S(1)} %get-tuple-element.55.value_local_ref, bf16[128,1536]{1,0:T(8,128)(2,1)S(1)} %get-tuple-element.56.weighted_values_ref, ...), custom_call_target="tpu_custom_call" | custom-call | bytes 3735552 | tf_op jit(solution)/shard_map/key_value_grads/pallas_call | solution.py:448
  (33 shorter events, 6.5 us)
Async XLA Ops:
  2.6 7.7 %collective-permute-start = (f32[304,128]{1,0:T(8,128)S(1)}, f32[304,128]{1,0:T(8,128)S(1)}, u32[]{:S(2)}, u32[]{:S(2)}) collective-permute-start(f32[304,128]{1,0:T(8,128)S(1)} %get-tuple-element.39), channel_id=1, source_target_pairs={{0,2},{2,0},{4,6},{6,4},{8,10},{10,8},{12,14},{14,12},{16,18},{18,... | collective-permute-start | bytes 466952 | tf_op jit(solution)/shard_map/ppermute | solution.py:466
  5.6 8.8 %collective-permute-start.1 = (f32[304,128]{1,0:T(8,128)S(1)}, f32[304,128]{1,0:T(8,128)S(1)}, u32[]{:S(2)}, u32[]{:S(2)}) collective-permute-start(f32[304,128]{1,0:T(8,128)S(1)} %get-tuple-element.40), channel_id=1, source_target_pairs={{0,4},{2,6},{4,0},{6,2},{8,12},{10,14},{12,8},{14,10},{16,20},{18,... | collective-permute-start | bytes 466952 | tf_op jit(solution)/shard_map/ppermute | solution.py:466
  7.1 7.3 %collective-permute-start.2 = (f32[304,128]{1,0:T(8,128)S(1)}, f32[304,128]{1,0:T(8,128)S(1)}, u32[]{:S(2)}, u32[]{:S(2)}) collective-permute-start(f32[304,128]{1,0:T(8,128)S(1)} %get-tuple-element.41), channel_id=1, source_target_pairs={{0,6},{2,4},{4,2},{6,0},{8,14},{10,12},{12,10},{14,8},{16,22},{18,... | collective-permute-start | bytes 466952 | tf_op jit(solution)/shard_map/ppermute | solution.py:466
  14.5 10.1 %copy-start.1 = (bf16[128,1536]{1,0:T(8,128)(2,1)S(1)}, bf16[128,1536]{1,0:T(8,128)(2,1)}, u32[]{:S(2)}) copy-start(bf16[128,1536]{1,0:T(8,128)(2,1)} %keys_ref.3) | copy-start | bytes 1179652
  14.5 10.1 %copy-start.2 = (bf16[128,1536]{1,0:T(8,128)(2,1)S(1)}, bf16[128,1536]{1,0:T(8,128)(2,1)}, u32[]{:S(2)}) copy-start(bf16[128,1536]{1,0:T(8,128)(2,1)} %values_ref.3) | copy-start | bytes 1179652
  14.5 10.1 %copy-start.4 = (bf16[128,1536]{1,0:T(8,128)(2,1)S(1)}, bf16[128,1536]{1,0:T(8,128)(2,1)}, u32[]{:S(2)}) copy-start(bf16[128,1536]{1,0:T(8,128)(2,1)} %queries_ref.3) | copy-start | bytes 1179652
  14.5 5.2 %collective-permute-start.4 = (f32[288,128]{1,0:T(8,128)S(1)}, f32[288,128]{1,0:T(8,128)S(1)}, u32[]{:S(2)}, u32[]{:S(2)}) collective-permute-start(f32[288,128]{1,0:T(8,128)S(1)} %total_state.2), channel_id=1, source_target_pairs={{0,2},{2,0},{4,6},{6,4},{8,16},{10,18},{12,20},{14,22},{16,8},{18,... | collective-permute-start | bytes 442376 | tf_op jit(solution)/shard_map/ppermute | solution.py:550
  15.8 5.1 %collective-permute-start.3 = (f32[288,128]{1,0:T(8,128)S(1)}, f32[288,128]{1,0:T(8,128)S(1)}, u32[]{:S(2)}, u32[]{:S(2)}) collective-permute-start(f32[288,128]{1,0:T(8,128)S(1)} %total_state.2), channel_id=1, source_target_pairs={{0,8},{2,10},{4,12},{6,14},{8,0},{10,2},{12,4},{14,6},{16,24},{18,... | collective-permute-start | bytes 442376 | tf_op jit(solution)/shard_map/ppermute | solution.py:550
  21.0 3.6 %copy-start.5 = (f32[1536]{0:T(1024)S(1)}, f32[1536]{0:T(1024)}, u32[]{:S(2)}) copy-start(f32[1536]{0:T(1024)} %param.11) | copy-start | bytes 18436
  21.1 6.1 %collective-permute-start.5 = (f32[288,128]{1,0:T(8,128)S(1)}, f32[288,128]{1,0:T(8,128)S(1)}, u32[]{:S(2)}, u32[]{:S(2)}) collective-permute-start(f32[288,128]{1,0:T(8,128)S(1)} %get-tuple-element.43), channel_id=1, source_target_pairs={{0,2},{2,0},{4,6},{6,4},{8,10},{10,8},{12,14},{14,12},{16,18},{18,... | collective-permute-start | bytes 442376 | tf_op jit(solution)/shard_map/ppermute | solution.py:466
  22.3 2.4 %copy-start.3 = (f32[16,128]{1,0:T(8,128)S(1)}, f32[16,128]{1,0:T(8,128)}, u32[]{:S(2)}) copy-start(f32[16,128]{1,0:T(8,128)} %decay_ref.3) | copy-start | bytes 24580
  22.3 5.2 %collective-permute-start.6 = (f32[288,128]{1,0:T(8,128)S(1)}, f32[288,128]{1,0:T(8,128)S(1)}, u32[]{:S(2)}, u32[]{:S(2)}) collective-permute-start(f32[288,128]{1,0:T(8,128)S(1)} %get-tuple-element.44), channel_id=1, source_target_pairs={{0,4},{2,6},{4,0},{6,2},{8,12},{10,14},{12,8},{14,10},{16,20},{18,... | collective-permute-start | bytes 442376 | tf_op jit(solution)/shard_map/ppermute | solution.py:466
  23.4 6.0 %collective-permute-start.7 = (f32[288,128]{1,0:T(8,128)S(1)}, f32[288,128]{1,0:T(8,128)S(1)}, u32[]{:S(2)}, u32[]{:S(2)}) collective-permute-start(f32[288,128]{1,0:T(8,128)S(1)} %get-tuple-element.45), channel_id=1, source_target_pairs={{0,6},{2,4},{4,2},{6,0},{8,14},{10,12},{12,10},{14,8},{16,22},{18,... | collective-permute-start | bytes 442376 | tf_op jit(solution)/shard_map/ppermute | solution.py:466
  24.7 4.8 %copy-start = (bf16[128,1536]{1,0:T(8,128)(2,1)S(1)}, bf16[128,1536]{1,0:T(8,128)(2,1)}, u32[]{:S(2)}) copy-start(bf16[128,1536]{1,0:T(8,128)(2,1)} %out_grad_ref.3) | copy-start | bytes 1179652
  30.0 1.3 %collective-permute-start.8 = (f32[128,128]{1,0:T(8,128)S(1)}, f32[128,128]{1,0:T(8,128)S(1)}, u32[]{:S(2)}, u32[]{:S(2)}) collective-permute-start(f32[128,128]{1,0:T(8,128)S(1)} %get-tuple-element.47.sums_ref), channel_id=1, source_target_pairs={{0,1},{1,0},{2,3},{3,2},{4,5},{5,4},{6,7},{7,6},{8,9},{9,8},{10,11... | collective-permute-start | bytes 196616 | tf_op jit(solution)/shard_map/ppermute | solution.py:570
  31.9 6.8 %collective-permute-start.9 = (f32[288,128]{1,0:T(8,128)S(1)}, f32[288,128]{1,0:T(8,128)S(1)}, u32[]{:S(2)}, u32[]{:S(2)}) collective-permute-start(f32[288,128]{1,0:T(8,128)S(1)} %get-tuple-element.59), channel_id=1, source_target_pairs={{0,2},{2,0},{4,6},{6,4},{8,10},{10,8},{12,14},{14,12},{16,18},{18,... | collective-permute-start | bytes 442376 | tf_op jit(solution)/shard_map/ppermute | solution.py:466
  33.1 8.8 %collective-permute-start.10 = (f32[288,128]{1,0:T(8,128)S(1)}, f32[288,128]{1,0:T(8,128)S(1)}, u32[]{:S(2)}, u32[]{:S(2)}) collective-permute-start(f32[288,128]{1,0:T(8,128)S(1)} %get-tuple-element.60), channel_id=1, source_target_pairs={{0,4},{2,6},{4,0},{6,2},{8,12},{10,14},{12,8},{14,10},{16,20},{18,... | collective-permute-start | bytes 442376 | tf_op jit(solution)/shard_map/ppermute | solution.py:466
  33.8 8.1 %collective-permute-start.11 = (f32[288,128]{1,0:T(8,128)S(1)}, f32[288,128]{1,0:T(8,128)S(1)}, u32[]{:S(2)}, u32[]{:S(2)}) collective-permute-start(f32[288,128]{1,0:T(8,128)S(1)} %get-tuple-element.61), channel_id=1, source_target_pairs={{0,6},{2,4},{4,2},{6,0},{8,14},{10,12},{12,10},{14,8},{16,22},{18,... | collective-permute-start | bytes 442376 | tf_op jit(solution)/shard_map/ppermute | solution.py:466
  42.0 5.2 %collective-permute-start.13 = (f32[288,128]{1,0:T(8,128)S(1)}, f32[288,128]{1,0:T(8,128)S(1)}, u32[]{:S(2)}, u32[]{:S(2)}) collective-permute-start(f32[288,128]{1,0:T(8,128)S(1)} %total_state.3), channel_id=1, source_target_pairs={{0,2},{2,0},{4,6},{6,4},{8,16},{10,18},{12,20},{14,22},{16,8},{18,... | collective-permute-start | bytes 442376 | tf_op jit(solution)/shard_map/ppermute | solution.py:550
  42.9 5.1 %collective-permute-start.12 = (f32[288,128]{1,0:T(8,128)S(1)}, f32[288,128]{1,0:T(8,128)S(1)}, u32[]{:S(2)}, u32[]{:S(2)}) collective-permute-start(f32[288,128]{1,0:T(8,128)S(1)} %total_state.3), channel_id=1, source_target_pairs={{0,8},{2,10},{4,12},{6,14},{8,0},{10,2},{12,4},{14,6},{16,24},{18,... | collective-permute-start | bytes 442376 | tf_op jit(solution)/shard_map/ppermute | solution.py:550
  48.2 7.7 %collective-permute-start.14 = (f32[288,128]{1,0:T(8,128)S(1)}, f32[288,128]{1,0:T(8,128)S(1)}, u32[]{:S(2)}, u32[]{:S(2)}) collective-permute-start(f32[288,128]{1,0:T(8,128)S(1)} %get-tuple-element.63), channel_id=1, source_target_pairs={{0,2},{2,0},{4,6},{6,4},{8,10},{10,8},{12,14},{14,12},{16,18},{18,... | collective-permute-start | bytes 442376 | tf_op jit(solution)/shard_map/ppermute | solution.py:466
  49.4 6.5 %collective-permute-start.15 = (f32[288,128]{1,0:T(8,128)S(1)}, f32[288,128]{1,0:T(8,128)S(1)}, u32[]{:S(2)}, u32[]{:S(2)}) collective-permute-start(f32[288,128]{1,0:T(8,128)S(1)} %get-tuple-element.64), channel_id=1, source_target_pairs={{0,4},{2,6},{4,0},{6,2},{8,12},{10,14},{12,8},{14,10},{16,20},{18,... | collective-permute-start | bytes 442376 | tf_op jit(solution)/shard_map/ppermute | solution.py:466
  50.1 6.1 %collective-permute-start.16 = (f32[288,128]{1,0:T(8,128)S(1)}, f32[288,128]{1,0:T(8,128)S(1)}, u32[]{:S(2)}, u32[]{:S(2)}) collective-permute-start(f32[288,128]{1,0:T(8,128)S(1)} %get-tuple-element.65), channel_id=1, source_target_pairs={{0,6},{2,4},{4,2},{6,0},{8,14},{10,12},{12,10},{14,8},{16,22},{18,... | collective-permute-start | bytes 442376 | tf_op jit(solution)/shard_map/ppermute | solution.py:466

commit v4 on v3

--- a/solution.py
+++ b/solution.py
@@ -44,6 +44,8 @@
         self.lanes = self.group * self.dim
         self.groups = heads // self.group
         self.pieces = pieces
+        self.out_masks = tuple(range(pieces))
+        self.back_masks = (0, *range(pieces - 1, 0, -1)) if pieces != 4 else (0, 3, 1, 2)
         self.rows = self.dim // pieces
         self.tiles = width // 128
         self.scale = 1.0 / math.sqrt(self.dim)
@@ -189,7 +191,7 @@
 
 
 def store_pieces(plan, mine, state_ref, piece_refs):
-    for m, piece in enumerate(piece_refs):
+    for m, piece in zip(plan.out_masks, piece_refs):
         start = pl.multiple_of((mine ^ m) * plan.rows, plan.rows)
         for j in range(plan.tiles):
             piece[j * plan.rows : (j + 1) * plan.rows, :] = state_ref[
@@ -198,7 +200,7 @@
 
 
 def load_pieces(plan, mine, piece_refs, state_ref):
-    for m, piece in enumerate(piece_refs):
+    for m, piece in zip(plan.back_masks, piece_refs):
         start = pl.multiple_of((mine ^ m) * plan.rows, plan.rows)
         for j in range(plan.tiles):
             state_ref[pl.ds(start, plan.rows), j * 128 : (j + 1) * 128] = piece[
@@ -276,9 +278,9 @@
             if with_carry:
                 tile = jnp.where(group == end, 0.0, jnp.where(by_first, hops[0][at], hops[1][at]))
             for step, b in enumerate(order):
-                m = mine ^ b
+                m = plan.out_masks.index(mine ^ b)
                 if with_carry:
-                    outs[m][at] = tile
+                    outs[plan.back_masks.index(mine ^ b)][at] = tile
                     if step == n - 1:
                         break
                 rate = factors[m][plan.piece_rows + j : plan.piece_rows + j + 1, :]
@@ -461,11 +463,10 @@
     return jax.ShapeDtypeStruct(shape, dtype)
 
 
-def exchange(pieces, count):
-    return [pieces[0]] + [
-        lax.ppermute(piece, "ctx", [(i, i ^ m) for i in range(count)])
-        for m, piece in enumerate(pieces)
-        if m
+def exchange(pieces, count, masks):
+    return [
+        lax.ppermute(piece, "ctx", [(i, i ^ m) for i in range(count)]) if m else piece
+        for m, piece in zip(masks, pieces)
     ]
 
 
@@ -527,7 +528,7 @@
         far_in=4,
     )
     if even:
-        pieces = exchange(pieces, count)
+        pieces = exchange(pieces, count, plan.out_masks)
     frames = pieces
 
     def chain(pieces, reverse, carry=None):
@@ -548,7 +549,7 @@
             return [scan_whole(plan, whole, factor, count, reach, sign).reshape(piece.shape)]
         (total,) = chain(pieces, reverse)
         carry = [lax.ppermute(total, "ctx", pairs) for pairs in group_swaps(n, count)]
-        return exchange(chain(pieces, reverse, carry), count)
+        return exchange(chain(pieces, reverse, carry), count, plan.back_masks)
 
     incoming = entering(pieces, False)
     probs, local, reached = call(
@@ -577,7 +578,7 @@
         [state],
     )
     if even:
-        pieces = exchange(pieces, count)
+        pieces = exchange(pieces, count, plan.out_masks)
     later = entering(pieces, True)
     output, query_grad, key_local, value_local, weighted_values = call(
         functools.partial(inner_kernel, plan),

time: 57.7 us -> 57.1 us (0.990)
  waiting for transfers between devices: 24.3 us -> 23.6 us
    ppermute x12, waiting for transfers between devices: 16.3 us -> 15.6 us  [exchange(): lax.ppermute(piece, 'ctx', [(i, i ^ m) for i in range(count)])]
where the time goes in v4:
time: 57.1 us; the launch traced here: 56.9 us
  waiting for transfers between devices  23.6 us (41%)
  starting transfers between devices  21.1 us (37%)
  Pallas kernels  11.3 us (20%)
  between operations  0.8 us (1%)
    ppermute x12, waiting for transfers between devices, exchange(): lax.ppermute(piece, 'ctx', [(i, i ^ m) for i in range(count)])  15.6 us
    ppermute x12, starting transfers between devices, exchange(): lax.ppermute(piece, 'ctx', [(i, i ^ m) for i in range(count)])  15.2 us
    pallas_call x10, Pallas kernels, call(): pl.pallas_call(kernel, name=name, out_shape=outs, in_specs=[SCALAR] * len...  11.3 us
    ppermute x4, waiting for transfers between devices, entering(): lax.ppermute(total, 'ctx', pairs)  6.8 us
    ppermute x4, starting transfers between devices, entering(): lax.ppermute(total, 'ctx', pairs)  5.84 us
    ppermute x1, waiting for transfers between devices, on_device(): other = lax.ppermute(sums, 'head', [(0, 1), (1, 0)])  1.24 us
  transfers between devices with their start and end apart: 17, of which 12 were waited for; matrix products, arithmetic and copies ran while one was open for 0% of the time, Pallas kernels for 12%

profile of v4, /device:TPU:0, one launch (start us, length us, event | category | flops | bytes accessed | tf_op | source)
XLA Modules:
  0.0 56.9 jit_solution(10123024353711283903)
XLA Ops:
  0.6 2.0 %exit_states.1 = (f32[304,128]{1,0:T(8,128)S(1)}, f32[304,128]{1,0:T(8,128)S(1)}, f32[304,128]{1,0:T(8,128)S(1)}, f32[304,128]{1,0:T(8,128)S(1)}, bf16[128,1536]{1,0:T(8,128)(2,1)S(1)}) custom-call(s32[16]{0:T(128)} %lengths_ref.3, f32[16,128]{1,0:T(8,128)} %decay_ref.3, bf16[128,1536]{1,0:T(8,128)(2,1)} %keys_ref.3, bf16[128,1536]{1,0:T(8,128)(2,1)} %values_ref.3), custom_call_target="tpu_custom_call" | custom-call | flops 100000000 | bytes 1810496 | tf_op jit(solution)/shard_map/exit_states/pallas_call | solution.py:450
  2.6 3.0 %collective-permute-start = (f32[304,128]{1,0:T(8,128)S(1)}, f32[304,128]{1,0:T(8,128)S(1)}, u32[]{:S(2)}, u32[]{:S(2)}) collective-permute-start(f32[304,128]{1,0:T(8,128)S(1)} %get-tuple-element.39), channel_id=1, source_target_pairs={{0,2},{2,0},{4,6},{6,4},{8,10},{10,8},{12,14},{14,12},{16,18},{18,... | collective-permute-start | bytes 466952 | tf_op jit(solution)/shard_map/ppermute | solution.py:468
  5.6 1.5 %collective-permute-start.1 = (f32[304,128]{1,0:T(8,128)S(1)}, f32[304,128]{1,0:T(8,128)S(1)}, u32[]{:S(2)}, u32[]{:S(2)}) collective-permute-start(f32[304,128]{1,0:T(8,128)S(1)} %get-tuple-element.40), channel_id=1, source_target_pairs={{0,4},{2,6},{4,0},{6,2},{8,12},{10,14},{12,8},{14,10},{16,20},{18,... | collective-permute-start | bytes 466952 | tf_op jit(solution)/shard_map/ppermute | solution.py:468
  7.1 3.1 %collective-permute-done.refs_1_.refs_5_ = f32[304,128]{1,0:T(8,128)S(1)} collective-permute-done((f32[304,128]{1,0:T(8,128)S(1)}, f32[304,128]{1,0:T(8,128)S(1)}, u32[]{:S(2)}, u32[]{:S(2)}) %collective-permute-start) | collective-permute-done | bytes 155680 | tf_op jit(solution)/shard_map/ppermute | solution.py:468
  10.3 4.2 %collective-permute-done.1.refs_2_.refs_6_ = f32[304,128]{1,0:T(8,128)S(1)} collective-permute-done((f32[304,128]{1,0:T(8,128)S(1)}, f32[304,128]{1,0:T(8,128)S(1)}, u32[]{:S(2)}, u32[]{:S(2)}) %collective-permute-start.1) | collective-permute-done | bytes 155680 | tf_op jit(solution)/shard_map/ppermute | solution.py:468
  14.5 1.3 %collective-permute-start.4 = (f32[288,128]{1,0:T(8,128)S(1)}, f32[288,128]{1,0:T(8,128)S(1)}, u32[]{:S(2)}, u32[]{:S(2)}) collective-permute-start(f32[288,128]{1,0:T(8,128)S(1)} %total_state.2), channel_id=1, source_target_pairs={{0,2},{2,0},{4,6},{6,4},{8,16},{10,18},{12,20},{14,22},{16,8},{18,... | collective-permute-start | bytes 442376 | tf_op jit(solution)/shard_map/ppermute | solution.py:551
  15.8 1.9 %collective-permute-start.3 = (f32[288,128]{1,0:T(8,128)S(1)}, f32[288,128]{1,0:T(8,128)S(1)}, u32[]{:S(2)}, u32[]{:S(2)}) collective-permute-start(f32[288,128]{1,0:T(8,128)S(1)} %total_state.2), channel_id=1, source_target_pairs={{0,8},{2,10},{4,12},{6,14},{8,0},{10,2},{12,4},{14,6},{16,24},{18,... | collective-permute-start | bytes 442376 | tf_op jit(solution)/shard_map/ppermute | solution.py:551
  17.8 2.0 %collective-permute-done.4.refs_9_ = f32[288,128]{1,0:T(8,128)S(1)} collective-permute-done((f32[288,128]{1,0:T(8,128)S(1)}, f32[288,128]{1,0:T(8,128)S(1)}, u32[]{:S(2)}, u32[]{:S(2)}) %collective-permute-start.4) | collective-permute-done | bytes 147488 | tf_op jit(solution)/shard_map/ppermute | solution.py:551
  19.7 1.2 %collective-permute-done.3.refs_8_ = f32[288,128]{1,0:T(8,128)S(1)} collective-permute-done((f32[288,128]{1,0:T(8,128)S(1)}, f32[288,128]{1,0:T(8,128)S(1)}, u32[]{:S(2)}, u32[]{:S(2)}) %collective-permute-start.3) | collective-permute-done | bytes 147488 | tf_op jit(solution)/shard_map/ppermute | solution.py:551
  21.1 1.8 %collective-permute-start.5 = (f32[288,128]{1,0:T(8,128)S(1)}, f32[288,128]{1,0:T(8,128)S(1)}, u32[]{:S(2)}, u32[]{:S(2)}) collective-permute-start(f32[288,128]{1,0:T(8,128)S(1)} %get-tuple-element.43), channel_id=1, source_target_pairs={{0,6},{2,4},{4,2},{6,0},{8,14},{10,12},{12,10},{14,8},{16,22},{18,... | collective-permute-start | bytes 442376 | tf_op jit(solution)/shard_map/ppermute | solution.py:468
  22.9 1.1 %collective-permute-start.6 = (f32[288,128]{1,0:T(8,128)S(1)}, f32[288,128]{1,0:T(8,128)S(1)}, u32[]{:S(2)}, u32[]{:S(2)}) collective-permute-start(f32[288,128]{1,0:T(8,128)S(1)} %get-tuple-element.44), channel_id=1, source_target_pairs={{0,2},{2,0},{4,6},{6,4},{8,10},{10,8},{12,14},{14,12},{16,18},{18,... | collective-permute-start | bytes 442376 | tf_op jit(solution)/shard_map/ppermute | solution.py:468
  24.7 2.5 %local_attention.1 = (bf16[128,2048]{1,0:T(8,128)(2,1)S(1)}, f32[128,1536]{1,0:T(8,128)S(1)}, bf16[128,1536]{1,0:T(8,128)(2,1)S(1)}) custom-call(s32[16]{0:T(128)} %lengths_ref.3, f32[16,128]{1,0:T(8,128)S(1)} %copy-done.3, bf16[128,1536]{1,0:T(8,128)(2,1)S(1)} %copy-done.4, bf16[128,1536]{1,0:T(8,128)(2,1)S(1)} %copy-done.1, bf16[128,1536]{1,0:T(8,128)(2,1)S(1)} %copy-done.2), custom_call_target="tpu_custom_call" | custom-call | flops 1000000000 | bytes 2891776 | tf_op jit(solution)/shard_map/local_attention/pallas_call | solution.py:450
  27.4 1.3 %collective-permute-done.6.refs_2_ = f32[288,128]{1,0:T(8,128)S(1)} collective-permute-done((f32[288,128]{1,0:T(8,128)S(1)}, f32[288,128]{1,0:T(8,128)S(1)}, u32[]{:S(2)}, u32[]{:S(2)}) %collective-permute-start.6) | collective-permute-done | bytes 147488 | tf_op jit(solution)/shard_map/ppermute | solution.py:468
  29.7 1.2 %collective-permute-done.8.other_ref = f32[128,128]{1,0:T(8,128)S(1)} collective-permute-done((f32[128,128]{1,0:T(8,128)S(1)}, f32[128,128]{1,0:T(8,128)S(1)}, u32[]{:S(2)}, u32[]{:S(2)}) %collective-permute-start.8) | collective-permute-done | bytes 65568 | tf_op jit(solution)/shard_map/ppermute | solution.py:571
  31.6 1.1 %collective-permute-start.9 = (f32[288,128]{1,0:T(8,128)S(1)}, f32[288,128]{1,0:T(8,128)S(1)}, u32[]{:S(2)}, u32[]{:S(2)}) collective-permute-start(f32[288,128]{1,0:T(8,128)S(1)} %get-tuple-element.59), channel_id=1, source_target_pairs={{0,2},{2,0},{4,6},{6,4},{8,10},{10,8},{12,14},{14,12},{16,18},{18,... | collective-permute-start | bytes 442376 | tf_op jit(solution)/shard_map/ppermute | solution.py:468
  33.6 1.6 %collective-permute-start.11 = (f32[288,128]{1,0:T(8,128)S(1)}, f32[288,128]{1,0:T(8,128)S(1)}, u32[]{:S(2)}, u32[]{:S(2)}) collective-permute-start(f32[288,128]{1,0:T(8,128)S(1)} %get-tuple-element.61), channel_id=1, source_target_pairs={{0,6},{2,4},{4,2},{6,0},{8,14},{10,12},{12,10},{14,8},{16,22},{18,... | collective-permute-start | bytes 442376 | tf_op jit(solution)/shard_map/ppermute | solution.py:468
  35.2 3.2 %collective-permute-done.9.refs_1_ = f32[288,128]{1,0:T(8,128)S(1)} collective-permute-done((f32[288,128]{1,0:T(8,128)S(1)}, f32[288,128]{1,0:T(8,128)S(1)}, u32[]{:S(2)}, u32[]{:S(2)}) %collective-permute-start.9) | collective-permute-done | bytes 147488 | tf_op jit(solution)/shard_map/ppermute | solution.py:468
  38.4 3.1 %collective-permute-done.10.refs_2_ = f32[288,128]{1,0:T(8,128)S(1)} collective-permute-done((f32[288,128]{1,0:T(8,128)S(1)}, f32[288,128]{1,0:T(8,128)S(1)}, u32[]{:S(2)}, u32[]{:S(2)}) %collective-permute-start.10) | collective-permute-done | bytes 147488 | tf_op jit(solution)/shard_map/ppermute | solution.py:468
  42.6 1.6 %collective-permute-start.12 = (f32[288,128]{1,0:T(8,128)S(1)}, f32[288,128]{1,0:T(8,128)S(1)}, u32[]{:S(2)}, u32[]{:S(2)}) collective-permute-start(f32[288,128]{1,0:T(8,128)S(1)} %total_state.3), channel_id=1, source_target_pairs={{0,8},{2,10},{4,12},{6,14},{8,0},{10,2},{12,4},{14,6},{16,24},{18,... | collective-permute-start | bytes 442376 | tf_op jit(solution)/shard_map/ppermute | solution.py:551
  44.2 2.6 %collective-permute-done.13.refs_9_ = f32[288,128]{1,0:T(8,128)S(1)} collective-permute-done((f32[288,128]{1,0:T(8,128)S(1)}, f32[288,128]{1,0:T(8,128)S(1)}, u32[]{:S(2)}, u32[]{:S(2)}) %collective-permute-start.13) | collective-permute-done | bytes 147488 | tf_op jit(solution)/shard_map/ppermute | solution.py:551
  47.8 1.4 %collective-permute-start.14 = (f32[288,128]{1,0:T(8,128)S(1)}, f32[288,128]{1,0:T(8,128)S(1)}, u32[]{:S(2)}, u32[]{:S(2)}) collective-permute-start(f32[288,128]{1,0:T(8,128)S(1)} %get-tuple-element.63), channel_id=1, source_target_pairs={{0,6},{2,4},{4,2},{6,0},{8,14},{10,12},{12,10},{14,8},{16,22},{18,... | collective-permute-start | bytes 442376 | tf_op jit(solution)/shard_map/ppermute | solution.py:468
  49.2 1.1 %collective-permute-start.15 = (f32[288,128]{1,0:T(8,128)S(1)}, f32[288,128]{1,0:T(8,128)S(1)}, u32[]{:S(2)}, u32[]{:S(2)}) collective-permute-start(f32[288,128]{1,0:T(8,128)S(1)} %get-tuple-element.64), channel_id=1, source_target_pairs={{0,2},{2,0},{4,6},{6,4},{8,10},{10,8},{12,14},{14,12},{16,18},{18,... | collective-permute-start | bytes 442376 | tf_op jit(solution)/shard_map/ppermute | solution.py:468
  51.4 4.2 %local_grads.1 = (bf16[128,1536]{1,0:T(8,128)(2,1)}, bf16[128,1536]{1,0:T(8,128)(2,1)}, f32[128,1536]{1,0:T(8,128)S(1)}, f32[128,1536]{1,0:T(8,128)S(1)}, bf16[128,1536]{1,0:T(8,128)(2,1)S(1)}) custom-call(s32[16]{0:T(128)} %lengths_ref.3, f32[16,128]{1,0:T(8,128)S(1)} %copy-done.3, bf16[128,1536]{1,0:T(8,128)(2,1)S(1)} %copy-done.4, ...), custom_call_target="tpu_custom_call" | custom-call | flops 1000000000 | bytes 6010880 | tf_op jit(solution)/shard_map/local_grads/pallas_call | solution.py:450
  55.6 1.3 %key_value_grads.1 = (bf16[128,1536]{1,0:T(8,128)(2,1)}, bf16[128,1536]{1,0:T(8,128)(2,1)}) custom-call(f32[128,1536]{1,0:T(8,128)S(1)} %get-tuple-element.54.key_local_ref, f32[128,1536]{1,0:T(8,128)S(1)} %get-tuple-element.55.value_local_ref, bf16[128,1536]{1,0:T(8,128)(2,1)S(1)} %get-tuple-element.56.weighted_values_ref, ...), custom_call_target="tpu_custom_call" | custom-call | bytes 3735552 | tf_op jit(solution)/shard_map/key_value_grads/pallas_call | solution.py:450
  (33 shorter events, 6.8 us)
Async XLA Ops:
  2.6 7.7 %collective-permute-start = (f32[304,128]{1,0:T(8,128)S(1)}, f32[304,128]{1,0:T(8,128)S(1)}, u32[]{:S(2)}, u32[]{:S(2)}) collective-permute-start(f32[304,128]{1,0:T(8,128)S(1)} %get-tuple-element.39), channel_id=1, source_target_pairs={{0,2},{2,0},{4,6},{6,4},{8,10},{10,8},{12,14},{14,12},{16,18},{18,... | collective-permute-start | bytes 466952 | tf_op jit(solution)/shard_map/ppermute | solution.py:468
  5.6 8.8 %collective-permute-start.1 = (f32[304,128]{1,0:T(8,128)S(1)}, f32[304,128]{1,0:T(8,128)S(1)}, u32[]{:S(2)}, u32[]{:S(2)}) collective-permute-start(f32[304,128]{1,0:T(8,128)S(1)} %get-tuple-element.40), channel_id=1, source_target_pairs={{0,4},{2,6},{4,0},{6,2},{8,12},{10,14},{12,8},{14,10},{16,20},{18,... | collective-permute-start | bytes 466952 | tf_op jit(solution)/shard_map/ppermute | solution.py:468
  7.1 7.3 %collective-permute-start.2 = (f32[304,128]{1,0:T(8,128)S(1)}, f32[304,128]{1,0:T(8,128)S(1)}, u32[]{:S(2)}, u32[]{:S(2)}) collective-permute-start(f32[304,128]{1,0:T(8,128)S(1)} %get-tuple-element.41), channel_id=1, source_target_pairs={{0,6},{2,4},{4,2},{6,0},{8,14},{10,12},{12,10},{14,8},{16,22},{18,... | collective-permute-start | bytes 466952 | tf_op jit(solution)/shard_map/ppermute | solution.py:468
  14.5 10.1 %copy-start.1 = (bf16[128,1536]{1,0:T(8,128)(2,1)S(1)}, bf16[128,1536]{1,0:T(8,128)(2,1)}, u32[]{:S(2)}) copy-start(bf16[128,1536]{1,0:T(8,128)(2,1)} %keys_ref.3) | copy-start | bytes 1179652
  14.5 10.1 %copy-start.2 = (bf16[128,1536]{1,0:T(8,128)(2,1)S(1)}, bf16[128,1536]{1,0:T(8,128)(2,1)}, u32[]{:S(2)}) copy-start(bf16[128,1536]{1,0:T(8,128)(2,1)} %values_ref.3) | copy-start | bytes 1179652
  14.5 10.1 %copy-start.4 = (bf16[128,1536]{1,0:T(8,128)(2,1)S(1)}, bf16[128,1536]{1,0:T(8,128)(2,1)}, u32[]{:S(2)}) copy-start(bf16[128,1536]{1,0:T(8,128)(2,1)} %queries_ref.3) | copy-start | bytes 1179652
  14.5 5.2 %collective-permute-start.4 = (f32[288,128]{1,0:T(8,128)S(1)}, f32[288,128]{1,0:T(8,128)S(1)}, u32[]{:S(2)}, u32[]{:S(2)}) collective-permute-start(f32[288,128]{1,0:T(8,128)S(1)} %total_state.2), channel_id=1, source_target_pairs={{0,2},{2,0},{4,6},{6,4},{8,16},{10,18},{12,20},{14,22},{16,8},{18,... | collective-permute-start | bytes 442376 | tf_op jit(solution)/shard_map/ppermute | solution.py:551
  15.8 5.1 %collective-permute-start.3 = (f32[288,128]{1,0:T(8,128)S(1)}, f32[288,128]{1,0:T(8,128)S(1)}, u32[]{:S(2)}, u32[]{:S(2)}) collective-permute-start(f32[288,128]{1,0:T(8,128)S(1)} %total_state.2), channel_id=1, source_target_pairs={{0,8},{2,10},{4,12},{6,14},{8,0},{10,2},{12,4},{14,6},{16,24},{18,... | collective-permute-start | bytes 442376 | tf_op jit(solution)/shard_map/ppermute | solution.py:551
  21.0 3.7 %copy-start.5 = (f32[1536]{0:T(1024)S(1)}, f32[1536]{0:T(1024)}, u32[]{:S(2)}) copy-start(f32[1536]{0:T(1024)} %param.11) | copy-start | bytes 18436
  21.1 6.3 %collective-permute-start.5 = (f32[288,128]{1,0:T(8,128)S(1)}, f32[288,128]{1,0:T(8,128)S(1)}, u32[]{:S(2)}, u32[]{:S(2)}) collective-permute-start(f32[288,128]{1,0:T(8,128)S(1)} %get-tuple-element.43), channel_id=1, source_target_pairs={{0,6},{2,4},{4,2},{6,0},{8,14},{10,12},{12,10},{14,8},{16,22},{18,... | collective-permute-start | bytes 442376 | tf_op jit(solution)/shard_map/ppermute | solution.py:468
  22.9 1.8 %copy-start.3 = (f32[16,128]{1,0:T(8,128)S(1)}, f32[16,128]{1,0:T(8,128)}, u32[]{:S(2)}) copy-start(f32[16,128]{1,0:T(8,128)} %decay_ref.3) | copy-start | bytes 24580
  22.9 5.8 %collective-permute-start.6 = (f32[288,128]{1,0:T(8,128)S(1)}, f32[288,128]{1,0:T(8,128)S(1)}, u32[]{:S(2)}, u32[]{:S(2)}) collective-permute-start(f32[288,128]{1,0:T(8,128)S(1)} %get-tuple-element.44), channel_id=1, source_target_pairs={{0,2},{2,0},{4,6},{6,4},{8,10},{10,8},{12,14},{14,12},{16,18},{18,... | collective-permute-start | bytes 442376 | tf_op jit(solution)/shard_map/ppermute | solution.py:468
  24.0 5.1 %collective-permute-start.7 = (f32[288,128]{1,0:T(8,128)S(1)}, f32[288,128]{1,0:T(8,128)S(1)}, u32[]{:S(2)}, u32[]{:S(2)}) collective-permute-start(f32[288,128]{1,0:T(8,128)S(1)} %get-tuple-element.45), channel_id=1, source_target_pairs={{0,4},{2,6},{4,0},{6,2},{8,12},{10,14},{12,8},{14,10},{16,20},{18,... | collective-permute-start | bytes 442376 | tf_op jit(solution)/shard_map/ppermute | solution.py:468
  24.7 4.5 %copy-start = (bf16[128,1536]{1,0:T(8,128)(2,1)S(1)}, bf16[128,1536]{1,0:T(8,128)(2,1)}, u32[]{:S(2)}) copy-start(bf16[128,1536]{1,0:T(8,128)(2,1)} %out_grad_ref.3) | copy-start | bytes 1179652
  29.6 1.3 %collective-permute-start.8 = (f32[128,128]{1,0:T(8,128)S(1)}, f32[128,128]{1,0:T(8,128)S(1)}, u32[]{:S(2)}, u32[]{:S(2)}) collective-permute-start(f32[128,128]{1,0:T(8,128)S(1)} %get-tuple-element.47.sums_ref), channel_id=1, source_target_pairs={{0,1},{1,0},{2,3},{3,2},{4,5},{5,4},{6,7},{7,6},{8,9},{9,8},{10,11... | collective-permute-start | bytes 196616 | tf_op jit(solution)/shard_map/ppermute | solution.py:571
  31.6 6.8 %collective-permute-start.9 = (f32[288,128]{1,0:T(8,128)S(1)}, f32[288,128]{1,0:T(8,128)S(1)}, u32[]{:S(2)}, u32[]{:S(2)}) collective-permute-start(f32[288,128]{1,0:T(8,128)S(1)} %get-tuple-element.59), channel_id=1, source_target_pairs={{0,2},{2,0},{4,6},{6,4},{8,10},{10,8},{12,14},{14,12},{16,18},{18,... | collective-permute-start | bytes 442376 | tf_op jit(solution)/shard_map/ppermute | solution.py:468
  32.7 8.8 %collective-permute-start.10 = (f32[288,128]{1,0:T(8,128)S(1)}, f32[288,128]{1,0:T(8,128)S(1)}, u32[]{:S(2)}, u32[]{:S(2)}) collective-permute-start(f32[288,128]{1,0:T(8,128)S(1)} %get-tuple-element.60), channel_id=1, source_target_pairs={{0,4},{2,6},{4,0},{6,2},{8,12},{10,14},{12,8},{14,10},{16,20},{18,... | collective-permute-start | bytes 442376 | tf_op jit(solution)/shard_map/ppermute | solution.py:468
  33.6 7.9 %collective-permute-start.11 = (f32[288,128]{1,0:T(8,128)S(1)}, f32[288,128]{1,0:T(8,128)S(1)}, u32[]{:S(2)}, u32[]{:S(2)}) collective-permute-start(f32[288,128]{1,0:T(8,128)S(1)} %get-tuple-element.61), channel_id=1, source_target_pairs={{0,6},{2,4},{4,2},{6,0},{8,14},{10,12},{12,10},{14,8},{16,22},{18,... | collective-permute-start | bytes 442376 | tf_op jit(solution)/shard_map/ppermute | solution.py:468
  41.6 5.2 %collective-permute-start.13 = (f32[288,128]{1,0:T(8,128)S(1)}, f32[288,128]{1,0:T(8,128)S(1)}, u32[]{:S(2)}, u32[]{:S(2)}) collective-permute-start(f32[288,128]{1,0:T(8,128)S(1)} %total_state.3), channel_id=1, source_target_pairs={{0,2},{2,0},{4,6},{6,4},{8,16},{10,18},{12,20},{14,22},{16,8},{18,... | collective-permute-start | bytes 442376 | tf_op jit(solution)/shard_map/ppermute | solution.py:551
  42.6 5.1 %collective-permute-start.12 = (f32[288,128]{1,0:T(8,128)S(1)}, f32[288,128]{1,0:T(8,128)S(1)}, u32[]{:S(2)}, u32[]{:S(2)}) collective-permute-start(f32[288,128]{1,0:T(8,128)S(1)} %total_state.3), channel_id=1, source_target_pairs={{0,8},{2,10},{4,12},{6,14},{8,0},{10,2},{12,4},{14,6},{16,24},{18,... | collective-permute-start | bytes 442376 | tf_op jit(solution)/shard_map/ppermute | solution.py:551
  47.8 7.7 %collective-permute-start.14 = (f32[288,128]{1,0:T(8,128)S(1)}, f32[288,128]{1,0:T(8,128)S(1)}, u32[]{:S(2)}, u32[]{:S(2)}) collective-permute-start(f32[288,128]{1,0:T(8,128)S(1)} %get-tuple-element.63), channel_id=1, source_target_pairs={{0,6},{2,4},{4,2},{6,0},{8,14},{10,12},{12,10},{14,8},{16,22},{18,... | collective-permute-start | bytes 442376 | tf_op jit(solution)/shard_map/ppermute | solution.py:468
  49.2 6.3 %collective-permute-start.15 = (f32[288,128]{1,0:T(8,128)S(1)}, f32[288,128]{1,0:T(8,128)S(1)}, u32[]{:S(2)}, u32[]{:S(2)}) collective-permute-start(f32[288,128]{1,0:T(8,128)S(1)} %get-tuple-element.64), channel_id=1, source_target_pairs={{0,2},{2,0},{4,6},{6,4},{8,10},{10,8},{12,14},{14,12},{16,18},{18,... | collective-permute-start | bytes 442376 | tf_op jit(solution)/shard_map/ppermute | solution.py:468
  50.4 5.2 %collective-permute-start.16 = (f32[288,128]{1,0:T(8,128)S(1)}, f32[288,128]{1,0:T(8,128)S(1)}, u32[]{:S(2)}, u32[]{:S(2)}) collective-permute-start(f32[288,128]{1,0:T(8,128)S(1)} %get-tuple-element.65), channel_id=1, source_target_pairs={{0,4},{2,6},{4,0},{6,2},{8,12},{10,14},{12,8},{14,10},{16,20},{18,... | collective-permute-start | bytes 442376 | tf_op jit(solution)/shard_map/ppermute | solution.py:468

commit v5 on v4

--- a/solution.py
+++ b/solution.py
@@ -199,13 +199,16 @@
             ]
 
 
-def load_pieces(plan, mine, piece_refs, state_ref):
-    for m, piece in zip(plan.back_masks, piece_refs):
-        start = pl.multiple_of((mine ^ m) * plan.rows, plan.rows)
+def load_pieces(plan, own, piece_refs, state_ref):
+    def at_place(mine):
+        order = [piece_refs[plan.back_masks.index(mine ^ b)] for b in range(plan.pieces)]
         for j in range(plan.tiles):
-            state_ref[pl.ds(start, plan.rows), j * 128 : (j + 1) * 128] = piece[
-                j * plan.rows : (j + 1) * plan.rows, :
-            ]
+            at = slice(j * plan.rows, (j + 1) * plan.rows)
+            rows = jnp.concatenate([piece[at, :] for piece in order], axis=0)
+            state_ref[:, j * 128 : (j + 1) * 128] = rows.astype(state_ref.dtype)
+
+    for mine in range(plan.pieces):
+        pl.when(own == mine)(functools.partial(at_place, mine))
 
 
 def row_copies(source, target, sems):
@@ -294,7 +297,18 @@
 
 
 def local_kernel(
-    plan, lengths_ref, decay_ref, queries_ref, keys_ref, values_ref, probs_ref, local_ref, reached_ref
+    plan,
+    lengths_ref,
+    decay_ref,
+    queries_ref,
+    keys_ref,
+    values_ref,
+    out_grad_ref,
+    gain_ref,
+    probs_ref,
+    local_ref,
+    reached_ref,
+    scaled_ref,
 ):
     block_start = place(plan)[0]
     decay = decay_ref[...]
@@ -306,6 +320,7 @@
     n = plan.tokens
     for g in range(plan.groups):
         at = lanes_of(plan, g)
+        scaled_ref[:, at] = out_grad_ref[:, at].astype(F32) * gain_ref[:, at]
         queries, keys, values = queries_ref[:, at], keys_ref[:, at], values_ref[:, at]
         reached_ref[:, at] = (queries.astype(F32) * reach[:, at]).astype(BF16)
         scores = dot(stack_heads(plan, queries), keys, NT)
@@ -319,19 +334,17 @@
         local_ref[:, at] = dot(probs, stack_heads(plan, values))
 
 
-def attend_kernel(plan, local_ref, reached_ref, out_grad_ref, gain_ref, *refs):
+def attend_kernel(plan, local_ref, reached_ref, scaled_ref, *refs):
     pieces = refs[: plan.pieces]
-    attended_ref, sums_ref, incoming_ref, state_ref = refs[plan.pieces :]
-    load_pieces(plan, place(plan)[1], pieces, state_ref)
+    attended_ref, sums_ref, incoming_ref = refs[plan.pieces :]
+    load_pieces(plan, place(plan)[1], pieces, incoming_ref)
     squares = inner = None
     for g in range(plan.groups):
         at = lanes_of(plan, g)
-        incoming = state_ref[:, at].astype(BF16)
-        incoming_ref[:, at] = incoming
+        incoming = incoming_ref[:, at]
         attended = local_ref[:, at] + through_states(plan, reached_ref[:, at], incoming, NN)
         attended_ref[:, at] = attended
-        grad = out_grad_ref[:, at].astype(F32) * gain_ref[:, at]
-        square, product = attended * attended, grad * attended
+        square, product = attended * attended, scaled_ref[:, at] * attended
         for j in range(0, plan.lanes, 128):
             squares = square[:, j : j + 128] if squares is None else squares + square[:, j : j + 128]
             inner = product[:, j : j + 128] if inner is None else inner + product[:, j : j + 128]
@@ -342,7 +355,7 @@
 
 
 def grad_kernel(
-    plan, features, attended_ref, out_grad_ref, gain_ref, sums_ref, other_ref, reached_ref, *refs
+    plan, features, attended_ref, scaled_ref, sums_ref, other_ref, reached_ref, *refs
 ):
     pieces, (attended_grad_ref, norm_ref, state_ref) = refs[: plan.pieces], refs[plan.pieces :]
     sums = sums_ref[...] + other_ref[...]
@@ -351,8 +364,7 @@
     slope = inverse * inverse * inverse * sums[:, 64:65] / features
     for g in range(plan.groups):
         at = lanes_of(plan, g)
-        grad = out_grad_ref[:, at].astype(F32) * gain_ref[:, at]
-        attended_grad = (grad * inverse - attended_ref[:, at] * slope).astype(BF16)
+        attended_grad = (scaled_ref[:, at] * inverse - attended_ref[:, at] * slope).astype(BF16)
         attended_grad_ref[:, at] = attended_grad
         state_ref[:, at] = outer_states(plan, reached_ref[:, at], attended_grad)
     store_pieces(plan, place(plan)[1], state_ref, pieces)
@@ -419,7 +431,7 @@
     copies = []
     for g in range(plan.groups):
         at = lanes_of(plan, g)
-        later = state_ref[:, at].astype(BF16)
+        later = state_ref[:, at]
         key_grad = key_local_ref[:, at] + through_states(plan, weighted_values_ref[:, at], later, NT)
         key_grad_ref[:, at] = key_grad.astype(BF16)
         copies.append(
@@ -552,28 +564,27 @@
         return exchange(chain(pieces, reverse, carry), count, plan.back_masks)
 
     incoming = entering(pieces, False)
-    probs, local, reached = call(
+    probs, local, reached, scaled = call(
         functools.partial(local_kernel, plan),
         "local_attention",
         (doc_lengths,),
-        (decay_log, queries, keys, values),
-        [array(tokens, heads * tokens, dtype=BF16), wide, like],
+        (decay_log, queries, keys, values, out_grad, gain),
+        [array(tokens, heads * tokens, dtype=BF16), wide, like, wide],
         flops=10**9,
     )
     attended, sums, incoming_state = call(
         functools.partial(attend_kernel, plan),
         "attended",
         (),
-        (local, reached, out_grad, gain, *incoming),
+        (local, reached, scaled, *incoming),
         [wide, array(tokens, 128), array(plan.dim, width, dtype=BF16)],
-        [state],
     )
     other = lax.ppermute(sums, "head", [(0, 1), (1, 0)])
     *pieces, attended_grad, norm = call(
         functools.partial(grad_kernel, plan, features),
         "attended_grad",
         (),
-        (attended, out_grad, gain, sums, other, reached),
+        (attended, scaled, sums, other, reached),
         [piece] * n + [like, array(tokens, 128)],
         [state],
     )
@@ -606,7 +617,7 @@
         (key_local, value_local, weighted_values, weighted_keys, *later),
         [like, like],
         [
-            state,
+            pltpu.VMEM((plan.dim, width), BF16),
             pltpu.VMEM((tokens, width), BF16),
             pltpu.VMEM((tokens, width), BF16),
             pltpu.SemaphoreType.DMA((plan.groups,)),

time: 57.1 us -> 57.1 us (level)
  transfers between devices with their start and end apart: 17 -> 17, of which waited for: 12 -> 12; matrix products, arithmetic and copies ran while one was open for 0% -> 0% of each run, Pallas kernels for 12% -> 11%
where the time goes in v5:
time: 57.1 us; the launch traced here: 56.9 us
  waiting for transfers between devices  23.8 us (42%)
  starting transfers between devices  21.1 us (37%)
  Pallas kernels  11.1 us (19%)
  between operations  0.8 us (1%)
    ppermute x12, waiting for transfers between devices, exchange(): lax.ppermute(piece, 'ctx', [(i, i ^ m) for i in range(count)])  15.7 us
    ppermute x12, starting transfers between devices, exchange(): lax.ppermute(piece, 'ctx', [(i, i ^ m) for i in range(count)])  15.2 us
    pallas_call x10, Pallas kernels, call(): pl.pallas_call(kernel, name=name, out_shape=outs, in_specs=[SCALAR] * len...  11.1 us
    ppermute x4, waiting for transfers between devices, entering(): lax.ppermute(total, 'ctx', pairs)  6.81 us
    ppermute x4, starting transfers between devices, entering(): lax.ppermute(total, 'ctx', pairs)  5.84 us
    ppermute x1, waiting for transfers between devices, on_device(): other = lax.ppermute(sums, 'head', [(0, 1), (1, 0)])  1.24 us
  transfers between devices with their start and end apart: 17, of which 12 were waited for; matrix products, arithmetic and copies ran while one was open for 0% of the time, Pallas kernels for 11%

profile of v5, /device:TPU:0, one launch (start us, length us, event | category | flops | bytes accessed | tf_op | source)
XLA Modules:
  0.0 56.9 jit_solution(10212095272637420167)
XLA Ops:
  0.6 2.0 %exit_states.1 = (f32[304,128]{1,0:T(8,128)S(1)}, f32[304,128]{1,0:T(8,128)S(1)}, f32[304,128]{1,0:T(8,128)S(1)}, f32[304,128]{1,0:T(8,128)S(1)}, bf16[128,1536]{1,0:T(8,128)(2,1)S(1)}) custom-call(s32[16]{0:T(128)} %lengths_ref.3, f32[16,128]{1,0:T(8,128)} %decay_ref.3, bf16[128,1536]{1,0:T(8,128)(2,1)} %keys_ref.3, bf16[128,1536]{1,0:T(8,128)(2,1)} %values_ref.3), custom_call_target="tpu_custom_call" | custom-call | flops 100000000 | bytes 1810496 | tf_op jit(solution)/shard_map/exit_states/pallas_call | solution.py:462
  2.6 3.0 %collective-permute-start = (f32[304,128]{1,0:T(8,128)S(1)}, f32[304,128]{1,0:T(8,128)S(1)}, u32[]{:S(2)}, u32[]{:S(2)}) collective-permute-start(f32[304,128]{1,0:T(8,128)S(1)} %get-tuple-element.41), channel_id=1, source_target_pairs={{0,2},{2,0},{4,6},{6,4},{8,10},{10,8},{12,14},{14,12},{16,18},{18,... | collective-permute-start | bytes 466952 | tf_op jit(solution)/shard_map/ppermute | solution.py:480
  5.6 1.5 %collective-permute-start.1 = (f32[304,128]{1,0:T(8,128)S(1)}, f32[304,128]{1,0:T(8,128)S(1)}, u32[]{:S(2)}, u32[]{:S(2)}) collective-permute-start(f32[304,128]{1,0:T(8,128)S(1)} %get-tuple-element.42), channel_id=1, source_target_pairs={{0,4},{2,6},{4,0},{6,2},{8,12},{10,14},{12,8},{14,10},{16,20},{18,... | collective-permute-start | bytes 466952 | tf_op jit(solution)/shard_map/ppermute | solution.py:480
  7.1 3.1 %collective-permute-done.refs_1_.refs_5_ = f32[304,128]{1,0:T(8,128)S(1)} collective-permute-done((f32[304,128]{1,0:T(8,128)S(1)}, f32[304,128]{1,0:T(8,128)S(1)}, u32[]{:S(2)}, u32[]{:S(2)}) %collective-permute-start) | collective-permute-done | bytes 155680 | tf_op jit(solution)/shard_map/ppermute | solution.py:480
  10.3 4.2 %collective-permute-done.1.refs_2_.refs_6_ = f32[304,128]{1,0:T(8,128)S(1)} collective-permute-done((f32[304,128]{1,0:T(8,128)S(1)}, f32[304,128]{1,0:T(8,128)S(1)}, u32[]{:S(2)}, u32[]{:S(2)}) %collective-permute-start.1) | collective-permute-done | bytes 155680 | tf_op jit(solution)/shard_map/ppermute | solution.py:480
  14.5 1.3 %collective-permute-start.4 = (f32[288,128]{1,0:T(8,128)S(1)}, f32[288,128]{1,0:T(8,128)S(1)}, u32[]{:S(2)}, u32[]{:S(2)}) collective-permute-start(f32[288,128]{1,0:T(8,128)S(1)} %total_state.2), channel_id=1, source_target_pairs={{0,2},{2,0},{4,6},{6,4},{8,16},{10,18},{12,20},{14,22},{16,8},{18,... | collective-permute-start | bytes 442376 | tf_op jit(solution)/shard_map/ppermute | solution.py:563
  15.8 1.9 %collective-permute-start.3 = (f32[288,128]{1,0:T(8,128)S(1)}, f32[288,128]{1,0:T(8,128)S(1)}, u32[]{:S(2)}, u32[]{:S(2)}) collective-permute-start(f32[288,128]{1,0:T(8,128)S(1)} %total_state.2), channel_id=1, source_target_pairs={{0,8},{2,10},{4,12},{6,14},{8,0},{10,2},{12,4},{14,6},{16,24},{18,... | collective-permute-start | bytes 442376 | tf_op jit(solution)/shard_map/ppermute | solution.py:563
  17.8 2.0 %collective-permute-done.4.refs_9_ = f32[288,128]{1,0:T(8,128)S(1)} collective-permute-done((f32[288,128]{1,0:T(8,128)S(1)}, f32[288,128]{1,0:T(8,128)S(1)}, u32[]{:S(2)}, u32[]{:S(2)}) %collective-permute-start.4) | collective-permute-done | bytes 147488 | tf_op jit(solution)/shard_map/ppermute | solution.py:563
  19.7 1.2 %collective-permute-done.3.refs_8_ = f32[288,128]{1,0:T(8,128)S(1)} collective-permute-done((f32[288,128]{1,0:T(8,128)S(1)}, f32[288,128]{1,0:T(8,128)S(1)}, u32[]{:S(2)}, u32[]{:S(2)}) %collective-permute-start.3) | collective-permute-done | bytes 147488 | tf_op jit(solution)/shard_map/ppermute | solution.py:563
  21.1 1.8 %collective-permute-start.5 = (f32[288,128]{1,0:T(8,128)S(1)}, f32[288,128]{1,0:T(8,128)S(1)}, u32[]{:S(2)}, u32[]{:S(2)}) collective-permute-start(f32[288,128]{1,0:T(8,128)S(1)} %get-tuple-element.45), channel_id=1, source_target_pairs={{0,6},{2,4},{4,2},{6,0},{8,14},{10,12},{12,10},{14,8},{16,22},{18,... | collective-permute-start | bytes 442376 | tf_op jit(solution)/shard_map/ppermute | solution.py:480
  22.9 1.1 %collective-permute-start.6 = (f32[288,128]{1,0:T(8,128)S(1)}, f32[288,128]{1,0:T(8,128)S(1)}, u32[]{:S(2)}, u32[]{:S(2)}) collective-permute-start(f32[288,128]{1,0:T(8,128)S(1)} %get-tuple-element.46), channel_id=1, source_target_pairs={{0,2},{2,0},{4,6},{6,4},{8,10},{10,8},{12,14},{14,12},{16,18},{18,... | collective-permute-start | bytes 442376 | tf_op jit(solution)/shard_map/ppermute | solution.py:480
  24.7 2.3 %local_attention.1 = (bf16[128,2048]{1,0:T(8,128)(2,1)S(1)}, f32[128,1536]{1,0:T(8,128)S(1)}, bf16[128,1536]{1,0:T(8,128)(2,1)S(1)}, f32[128,1536]{1,0:T(8,128)S(1)}) custom-call(s32[16]{0:T(128)} %lengths_ref.3, f32[16,128]{1,0:T(8,128)S(1)} %copy-done.2, bf16[128,1536]{1,0:T(8,128)(2,1)S(1)} %copy-done.4, bf16[128,1536]{1,0:T(8,128)(2,1)S(1)} %copy-done, ...), custom_call_target="tpu_custom_call" | custom-call | flops 1000000000 | bytes 4077568 | tf_op jit(solution)/shard_map/local_attention/pallas_call | solution.py:462
  27.4 1.3 %collective-permute-done.6.refs_2_ = f32[288,128]{1,0:T(8,128)S(1)} collective-permute-done((f32[288,128]{1,0:T(8,128)S(1)}, f32[288,128]{1,0:T(8,128)S(1)}, u32[]{:S(2)}, u32[]{:S(2)}) %collective-permute-start.6) | collective-permute-done | bytes 147488 | tf_op jit(solution)/shard_map/ppermute | solution.py:480
  29.7 1.2 %collective-permute-done.8.other_ref = f32[128,128]{1,0:T(8,128)S(1)} collective-permute-done((f32[128,128]{1,0:T(8,128)S(1)}, f32[128,128]{1,0:T(8,128)S(1)}, u32[]{:S(2)}, u32[]{:S(2)}) %collective-permute-start.8) | collective-permute-done | bytes 65568 | tf_op jit(solution)/shard_map/ppermute | solution.py:582
  31.6 1.1 %collective-permute-start.9 = (f32[288,128]{1,0:T(8,128)S(1)}, f32[288,128]{1,0:T(8,128)S(1)}, u32[]{:S(2)}, u32[]{:S(2)}) collective-permute-start(f32[288,128]{1,0:T(8,128)S(1)} %get-tuple-element.61), channel_id=1, source_target_pairs={{0,2},{2,0},{4,6},{6,4},{8,10},{10,8},{12,14},{14,12},{16,18},{18,... | collective-permute-start | bytes 442376 | tf_op jit(solution)/shard_map/ppermute | solution.py:480
  33.5 1.6 %collective-permute-start.11 = (f32[288,128]{1,0:T(8,128)S(1)}, f32[288,128]{1,0:T(8,128)S(1)}, u32[]{:S(2)}, u32[]{:S(2)}) collective-permute-start(f32[288,128]{1,0:T(8,128)S(1)} %get-tuple-element.63), channel_id=1, source_target_pairs={{0,6},{2,4},{4,2},{6,0},{8,14},{10,12},{12,10},{14,8},{16,22},{18,... | collective-permute-start | bytes 442376 | tf_op jit(solution)/shard_map/ppermute | solution.py:480
  35.1 3.2 %collective-permute-done.9.refs_1_ = f32[288,128]{1,0:T(8,128)S(1)} collective-permute-done((f32[288,128]{1,0:T(8,128)S(1)}, f32[288,128]{1,0:T(8,128)S(1)}, u32[]{:S(2)}, u32[]{:S(2)}) %collective-permute-start.9) | collective-permute-done | bytes 147488 | tf_op jit(solution)/shard_map/ppermute | solution.py:480
  38.3 3.1 %collective-permute-done.10.refs_2_ = f32[288,128]{1,0:T(8,128)S(1)} collective-permute-done((f32[288,128]{1,0:T(8,128)S(1)}, f32[288,128]{1,0:T(8,128)S(1)}, u32[]{:S(2)}, u32[]{:S(2)}) %collective-permute-start.10) | collective-permute-done | bytes 147488 | tf_op jit(solution)/shard_map/ppermute | solution.py:480
  42.6 1.6 %collective-permute-start.12 = (f32[288,128]{1,0:T(8,128)S(1)}, f32[288,128]{1,0:T(8,128)S(1)}, u32[]{:S(2)}, u32[]{:S(2)}) collective-permute-start(f32[288,128]{1,0:T(8,128)S(1)} %total_state.3), channel_id=1, source_target_pairs={{0,8},{2,10},{4,12},{6,14},{8,0},{10,2},{12,4},{14,6},{16,24},{18,... | collective-permute-start | bytes 442376 | tf_op jit(solution)/shard_map/ppermute | solution.py:563
  44.1 2.6 %collective-permute-done.13.refs_9_ = f32[288,128]{1,0:T(8,128)S(1)} collective-permute-done((f32[288,128]{1,0:T(8,128)S(1)}, f32[288,128]{1,0:T(8,128)S(1)}, u32[]{:S(2)}, u32[]{:S(2)}) %collective-permute-start.13) | collective-permute-done | bytes 147488 | tf_op jit(solution)/shard_map/ppermute | solution.py:563
  47.8 1.4 %collective-permute-start.14 = (f32[288,128]{1,0:T(8,128)S(1)}, f32[288,128]{1,0:T(8,128)S(1)}, u32[]{:S(2)}, u32[]{:S(2)}) collective-permute-start(f32[288,128]{1,0:T(8,128)S(1)} %get-tuple-element.65), channel_id=1, source_target_pairs={{0,6},{2,4},{4,2},{6,0},{8,14},{10,12},{12,10},{14,8},{16,22},{18,... | collective-permute-start | bytes 442376 | tf_op jit(solution)/shard_map/ppermute | solution.py:480
  49.2 1.1 %collective-permute-start.15 = (f32[288,128]{1,0:T(8,128)S(1)}, f32[288,128]{1,0:T(8,128)S(1)}, u32[]{:S(2)}, u32[]{:S(2)}) collective-permute-start(f32[288,128]{1,0:T(8,128)S(1)} %get-tuple-element.66), channel_id=1, source_target_pairs={{0,2},{2,0},{4,6},{6,4},{8,10},{10,8},{12,14},{14,12},{16,18},{18,... | collective-permute-start | bytes 442376 | tf_op jit(solution)/shard_map/ppermute | solution.py:480
  51.4 4.2 %local_grads.1 = (bf16[128,1536]{1,0:T(8,128)(2,1)}, bf16[128,1536]{1,0:T(8,128)(2,1)}, f32[128,1536]{1,0:T(8,128)S(1)}, f32[128,1536]{1,0:T(8,128)S(1)}, bf16[128,1536]{1,0:T(8,128)(2,1)S(1)}) custom-call(s32[16]{0:T(128)} %lengths_ref.3, f32[16,128]{1,0:T(8,128)S(1)} %copy-done.2, bf16[128,1536]{1,0:T(8,128)(2,1)S(1)} %copy-done.4, ...), custom_call_target="tpu_custom_call" | custom-call | flops 1000000000 | bytes 6010880 | tf_op jit(solution)/shard_map/local_grads/pallas_call | solution.py:462
  55.5 1.4 %key_value_grads.1 = (bf16[128,1536]{1,0:T(8,128)(2,1)}, bf16[128,1536]{1,0:T(8,128)(2,1)}) custom-call(f32[128,1536]{1,0:T(8,128)S(1)} %get-tuple-element.56.key_local_ref, f32[128,1536]{1,0:T(8,128)S(1)} %get-tuple-element.57.value_local_ref, bf16[128,1536]{1,0:T(8,128)(2,1)S(1)} %get-tuple-element.58.weighted_values_ref, ...), custom_call_target="tpu_custom_call" | custom-call | bytes 3735552 | tf_op jit(solution)/shard_map/key_value_grads/pallas_call | solution.py:462
  (33 shorter events, 7.0 us)
Async XLA Ops:
  2.6 7.7 %collective-permute-start = (f32[304,128]{1,0:T(8,128)S(1)}, f32[304,128]{1,0:T(8,128)S(1)}, u32[]{:S(2)}, u32[]{:S(2)}) collective-permute-start(f32[304,128]{1,0:T(8,128)S(1)} %get-tuple-element.41), channel_id=1, source_target_pairs={{0,2},{2,0},{4,6},{6,4},{8,10},{10,8},{12,14},{14,12},{16,18},{18,... | collective-permute-start | bytes 466952 | tf_op jit(solution)/shard_map/ppermute | solution.py:480
  5.6 8.8 %collective-permute-start.1 = (f32[304,128]{1,0:T(8,128)S(1)}, f32[304,128]{1,0:T(8,128)S(1)}, u32[]{:S(2)}, u32[]{:S(2)}) collective-permute-start(f32[304,128]{1,0:T(8,128)S(1)} %get-tuple-element.42), channel_id=1, source_target_pairs={{0,4},{2,6},{4,0},{6,2},{8,12},{10,14},{12,8},{14,10},{16,20},{18,... | collective-permute-start | bytes 466952 | tf_op jit(solution)/shard_map/ppermute | solution.py:480
  7.1 7.3 %collective-permute-start.2 = (f32[304,128]{1,0:T(8,128)S(1)}, f32[304,128]{1,0:T(8,128)S(1)}, u32[]{:S(2)}, u32[]{:S(2)}) collective-permute-start(f32[304,128]{1,0:T(8,128)S(1)} %get-tuple-element.43), channel_id=1, source_target_pairs={{0,6},{2,4},{4,2},{6,0},{8,14},{10,12},{12,10},{14,8},{16,22},{18,... | collective-permute-start | bytes 466952 | tf_op jit(solution)/shard_map/ppermute | solution.py:480
  14.4 10.2 %copy-start.4 = (bf16[128,1536]{1,0:T(8,128)(2,1)S(1)}, bf16[128,1536]{1,0:T(8,128)(2,1)}, u32[]{:S(2)}) copy-start(bf16[128,1536]{1,0:T(8,128)(2,1)} %queries_ref.3) | copy-start | bytes 1179652
  14.5 10.1 %copy-start = (bf16[128,1536]{1,0:T(8,128)(2,1)S(1)}, bf16[128,1536]{1,0:T(8,128)(2,1)}, u32[]{:S(2)}) copy-start(bf16[128,1536]{1,0:T(8,128)(2,1)} %keys_ref.3) | copy-start | bytes 1179652
  14.5 10.1 %copy-start.1 = (bf16[128,1536]{1,0:T(8,128)(2,1)S(1)}, bf16[128,1536]{1,0:T(8,128)(2,1)}, u32[]{:S(2)}) copy-start(bf16[128,1536]{1,0:T(8,128)(2,1)} %values_ref.3) | copy-start | bytes 1179652
  14.5 10.1 %copy-start.3 = (bf16[128,1536]{1,0:T(8,128)(2,1)S(1)}, bf16[128,1536]{1,0:T(8,128)(2,1)}, u32[]{:S(2)}) copy-start(bf16[128,1536]{1,0:T(8,128)(2,1)} %out_grad_ref.1) | copy-start | bytes 1179652
  14.5 5.2 %collective-permute-start.4 = (f32[288,128]{1,0:T(8,128)S(1)}, f32[288,128]{1,0:T(8,128)S(1)}, u32[]{:S(2)}, u32[]{:S(2)}) collective-permute-start(f32[288,128]{1,0:T(8,128)S(1)} %total_state.2), channel_id=1, source_target_pairs={{0,2},{2,0},{4,6},{6,4},{8,16},{10,18},{12,20},{14,22},{16,8},{18,... | collective-permute-start | bytes 442376 | tf_op jit(solution)/shard_map/ppermute | solution.py:563
  15.8 5.1 %collective-permute-start.3 = (f32[288,128]{1,0:T(8,128)S(1)}, f32[288,128]{1,0:T(8,128)S(1)}, u32[]{:S(2)}, u32[]{:S(2)}) collective-permute-start(f32[288,128]{1,0:T(8,128)S(1)} %total_state.2), channel_id=1, source_target_pairs={{0,8},{2,10},{4,12},{6,14},{8,0},{10,2},{12,4},{14,6},{16,24},{18,... | collective-permute-start | bytes 442376 | tf_op jit(solution)/shard_map/ppermute | solution.py:563
  21.0 3.6 %copy-start.5 = (f32[1536]{0:T(1024)S(1)}, f32[1536]{0:T(1024)}, u32[]{:S(2)}) copy-start(f32[1536]{0:T(1024)} %param.11) | copy-start | bytes 18436
  21.1 6.3 %collective-permute-start.5 = (f32[288,128]{1,0:T(8,128)S(1)}, f32[288,128]{1,0:T(8,128)S(1)}, u32[]{:S(2)}, u32[]{:S(2)}) collective-permute-start(f32[288,128]{1,0:T(8,128)S(1)} %get-tuple-element.45), channel_id=1, source_target_pairs={{0,6},{2,4},{4,2},{6,0},{8,14},{10,12},{12,10},{14,8},{16,22},{18,... | collective-permute-start | bytes 442376 | tf_op jit(solution)/shard_map/ppermute | solution.py:480
  22.9 1.8 %copy-start.2 = (f32[16,128]{1,0:T(8,128)S(1)}, f32[16,128]{1,0:T(8,128)}, u32[]{:S(2)}) copy-start(f32[16,128]{1,0:T(8,128)} %decay_ref.3) | copy-start | bytes 24580
  22.9 5.8 %collective-permute-start.6 = (f32[288,128]{1,0:T(8,128)S(1)}, f32[288,128]{1,0:T(8,128)S(1)}, u32[]{:S(2)}, u32[]{:S(2)}) collective-permute-start(f32[288,128]{1,0:T(8,128)S(1)} %get-tuple-element.46), channel_id=1, source_target_pairs={{0,2},{2,0},{4,6},{6,4},{8,10},{10,8},{12,14},{14,12},{16,18},{18,... | collective-permute-start | bytes 442376 | tf_op jit(solution)/shard_map/ppermute | solution.py:480
  24.0 5.1 %collective-permute-start.7 = (f32[288,128]{1,0:T(8,128)S(1)}, f32[288,128]{1,0:T(8,128)S(1)}, u32[]{:S(2)}, u32[]{:S(2)}) collective-permute-start(f32[288,128]{1,0:T(8,128)S(1)} %get-tuple-element.47), channel_id=1, source_target_pairs={{0,4},{2,6},{4,0},{6,2},{8,12},{10,14},{12,8},{14,10},{16,20},{18,... | collective-permute-start | bytes 442376 | tf_op jit(solution)/shard_map/ppermute | solution.py:480
  29.6 1.3 %collective-permute-start.8 = (f32[128,128]{1,0:T(8,128)S(1)}, f32[128,128]{1,0:T(8,128)S(1)}, u32[]{:S(2)}, u32[]{:S(2)}) collective-permute-start(f32[128,128]{1,0:T(8,128)S(1)} %get-tuple-element.49.sums_ref), channel_id=1, source_target_pairs={{0,1},{1,0},{2,3},{3,2},{4,5},{5,4},{6,7},{7,6},{8,9},{9,8},{10,11... | collective-permute-start | bytes 196616 | tf_op jit(solution)/shard_map/ppermute | solution.py:582
  31.6 6.8 %collective-permute-start.9 = (f32[288,128]{1,0:T(8,128)S(1)}, f32[288,128]{1,0:T(8,128)S(1)}, u32[]{:S(2)}, u32[]{:S(2)}) collective-permute-start(f32[288,128]{1,0:T(8,128)S(1)} %get-tuple-element.61), channel_id=1, source_target_pairs={{0,2},{2,0},{4,6},{6,4},{8,10},{10,8},{12,14},{14,12},{16,18},{18,... | collective-permute-start | bytes 442376 | tf_op jit(solution)/shard_map/ppermute | solution.py:480
  32.6 8.8 %collective-permute-start.10 = (f32[288,128]{1,0:T(8,128)S(1)}, f32[288,128]{1,0:T(8,128)S(1)}, u32[]{:S(2)}, u32[]{:S(2)}) collective-permute-start(f32[288,128]{1,0:T(8,128)S(1)} %get-tuple-element.62), channel_id=1, source_target_pairs={{0,4},{2,6},{4,0},{6,2},{8,12},{10,14},{12,8},{14,10},{16,20},{18,... | collective-permute-start | bytes 442376 | tf_op jit(solution)/shard_map/ppermute | solution.py:480
  33.5 7.9 %collective-permute-start.11 = (f32[288,128]{1,0:T(8,128)S(1)}, f32[288,128]{1,0:T(8,128)S(1)}, u32[]{:S(2)}, u32[]{:S(2)}) collective-permute-start(f32[288,128]{1,0:T(8,128)S(1)} %get-tuple-element.63), channel_id=1, source_target_pairs={{0,6},{2,4},{4,2},{6,0},{8,14},{10,12},{12,10},{14,8},{16,22},{18,... | collective-permute-start | bytes 442376 | tf_op jit(solution)/shard_map/ppermute | solution.py:480
  41.5 5.2 %collective-permute-start.13 = (f32[288,128]{1,0:T(8,128)S(1)}, f32[288,128]{1,0:T(8,128)S(1)}, u32[]{:S(2)}, u32[]{:S(2)}) collective-permute-start(f32[288,128]{1,0:T(8,128)S(1)} %total_state.3), channel_id=1, source_target_pairs={{0,2},{2,0},{4,6},{6,4},{8,16},{10,18},{12,20},{14,22},{16,8},{18,... | collective-permute-start | bytes 442376 | tf_op jit(solution)/shard_map/ppermute | solution.py:563
  42.6 5.1 %collective-permute-start.12 = (f32[288,128]{1,0:T(8,128)S(1)}, f32[288,128]{1,0:T(8,128)S(1)}, u32[]{:S(2)}, u32[]{:S(2)}) collective-permute-start(f32[288,128]{1,0:T(8,128)S(1)} %total_state.3), channel_id=1, source_target_pairs={{0,8},{2,10},{4,12},{6,14},{8,0},{10,2},{12,4},{14,6},{16,24},{18,... | collective-permute-start | bytes 442376 | tf_op jit(solution)/shard_map/ppermute | solution.py:563
  47.8 7.7 %collective-permute-start.14 = (f32[288,128]{1,0:T(8,128)S(1)}, f32[288,128]{1,0:T(8,128)S(1)}, u32[]{:S(2)}, u32[]{:S(2)}) collective-permute-start(f32[288,128]{1,0:T(8,128)S(1)} %get-tuple-element.65), channel_id=1, source_target_pairs={{0,6},{2,4},{4,2},{6,0},{8,14},{10,12},{12,10},{14,8},{16,22},{18,... | collective-permute-start | bytes 442376 | tf_op jit(solution)/shard_map/ppermute | solution.py:480
  49.2 6.3 %collective-permute-start.15 = (f32[288,128]{1,0:T(8,128)S(1)}, f32[288,128]{1,0:T(8,128)S(1)}, u32[]{:S(2)}, u32[]{:S(2)}) collective-permute-start(f32[288,128]{1,0:T(8,128)S(1)} %get-tuple-element.66), channel_id=1, source_target_pairs={{0,2},{2,0},{4,6},{6,4},{8,10},{10,8},{12,14},{14,12},{16,18},{18,... | collective-permute-start | bytes 442376 | tf_op jit(solution)/shard_map/ppermute | solution.py:480
  50.3 5.2 %collective-permute-start.16 = (f32[288,128]{1,0:T(8,128)S(1)}, f32[288,128]{1,0:T(8,128)S(1)}, u32[]{:S(2)}, u32[]{:S(2)}) collective-permute-start(f32[288,128]{1,0:T(8,128)S(1)} %get-tuple-element.67), channel_id=1, source_target_pairs={{0,4},{2,6},{4,0},{6,2},{8,12},{10,14},{12,8},{14,10},{16,20},{18,... | collective-permute-start | bytes 442376 | tf_op jit(solution)/shard_map/ppermute | solution.py:480

commit v6 on v4

--- a/solution.py
+++ b/solution.py
@@ -45,7 +45,7 @@
         self.groups = heads // self.group
         self.pieces = pieces
         self.out_masks = tuple(range(pieces))
-        self.back_masks = (0, *range(pieces - 1, 0, -1)) if pieces != 4 else (0, 3, 1, 2)
+        self.back_masks = (0, *range(pieces - 1, 0, -1))
         self.rows = self.dim // pieces
         self.tiles = width // 128
         self.scale = 1.0 / math.sqrt(self.dim)

time: 57.1 us -> 57.2 us (level)
  no operation moved by 1% of the time
where the time goes in v6:
time: 57.2 us; the launch traced here: 57 us
  waiting for transfers between devices  24.1 us (42%)
  starting transfers between devices  20.8 us (36%)
  Pallas kernels  11.3 us (20%)
  between operations  0.79 us (1%)
    ppermute x12, waiting for transfers between devices, exchange(): lax.ppermute(piece, 'ctx', [(i, i ^ m) for i in range(count)])  15.9 us
    ppermute x12, starting transfers between devices, exchange(): lax.ppermute(piece, 'ctx', [(i, i ^ m) for i in range(count)])  15.2 us
    pallas_call x10, Pallas kernels, call(): pl.pallas_call(kernel, name=name, out_shape=outs, in_specs=[SCALAR] * len...  11.3 us
    ppermute x4, waiting for transfers between devices, entering(): lax.ppermute(total, 'ctx', pairs)  6.91 us
    ppermute x4, starting transfers between devices, entering(): lax.ppermute(total, 'ctx', pairs)  5.53 us
    ppermute x1, waiting for transfers between devices, on_device(): other = lax.ppermute(sums, 'head', [(0, 1), (1, 0)])  1.24 us
  transfers between devices with their start and end apart: 17, of which 12 were waited for; matrix products, arithmetic and copies ran while one was open for 0% of the time, Pallas kernels for 12%

profile of v6, /device:TPU:0, one launch (start us, length us, event | category | flops | bytes accessed | tf_op | source)
XLA Modules:
  0.0 57.0 jit_solution(11643439941926513148)
XLA Ops:
  0.6 2.0 %exit_states.1 = (f32[304,128]{1,0:T(8,128)S(1)}, f32[304,128]{1,0:T(8,128)S(1)}, f32[304,128]{1,0:T(8,128)S(1)}, f32[304,128]{1,0:T(8,128)S(1)}, bf16[128,1536]{1,0:T(8,128)(2,1)S(1)}) custom-call(s32[16]{0:T(128)} %lengths_ref.3, f32[16,128]{1,0:T(8,128)} %decay_ref.3, bf16[128,1536]{1,0:T(8,128)(2,1)} %keys_ref.3, bf16[128,1536]{1,0:T(8,128)(2,1)} %values_ref.3), custom_call_target="tpu_custom_call" | custom-call | flops 100000000 | bytes 1810496 | tf_op jit(solution)/shard_map/exit_states/pallas_call | solution.py:450
  2.6 3.0 %collective-permute-start = (f32[304,128]{1,0:T(8,128)S(1)}, f32[304,128]{1,0:T(8,128)S(1)}, u32[]{:S(2)}, u32[]{:S(2)}) collective-permute-start(f32[304,128]{1,0:T(8,128)S(1)} %get-tuple-element.39), channel_id=1, source_target_pairs={{0,2},{2,0},{4,6},{6,4},{8,10},{10,8},{12,14},{14,12},{16,18},{18,... | collective-permute-start | bytes 466952 | tf_op jit(solution)/shard_map/ppermute | solution.py:468
  5.6 1.5 %collective-permute-start.1 = (f32[304,128]{1,0:T(8,128)S(1)}, f32[304,128]{1,0:T(8,128)S(1)}, u32[]{:S(2)}, u32[]{:S(2)}) collective-permute-start(f32[304,128]{1,0:T(8,128)S(1)} %get-tuple-element.40), channel_id=1, source_target_pairs={{0,4},{2,6},{4,0},{6,2},{8,12},{10,14},{12,8},{14,10},{16,20},{18,... | collective-permute-start | bytes 466952 | tf_op jit(solution)/shard_map/ppermute | solution.py:468
  7.1 3.1 %collective-permute-done.refs_1_.refs_5_ = f32[304,128]{1,0:T(8,128)S(1)} collective-permute-done((f32[304,128]{1,0:T(8,128)S(1)}, f32[304,128]{1,0:T(8,128)S(1)}, u32[]{:S(2)}, u32[]{:S(2)}) %collective-permute-start) | collective-permute-done | bytes 155680 | tf_op jit(solution)/shard_map/ppermute | solution.py:468
  10.3 4.2 %collective-permute-done.1.refs_2_.refs_6_ = f32[304,128]{1,0:T(8,128)S(1)} collective-permute-done((f32[304,128]{1,0:T(8,128)S(1)}, f32[304,128]{1,0:T(8,128)S(1)}, u32[]{:S(2)}, u32[]{:S(2)}) %collective-permute-start.1) | collective-permute-done | bytes 155680 | tf_op jit(solution)/shard_map/ppermute | solution.py:468
  14.5 1.3 %collective-permute-start.4 = (f32[288,128]{1,0:T(8,128)S(1)}, f32[288,128]{1,0:T(8,128)S(1)}, u32[]{:S(2)}, u32[]{:S(2)}) collective-permute-start(f32[288,128]{1,0:T(8,128)S(1)} %total_state.2), channel_id=1, source_target_pairs={{0,2},{2,0},{4,6},{6,4},{8,16},{10,18},{12,20},{14,22},{16,8},{18,... | collective-permute-start | bytes 442376 | tf_op jit(solution)/shard_map/ppermute | solution.py:551
  15.8 1.9 %collective-permute-start.3 = (f32[288,128]{1,0:T(8,128)S(1)}, f32[288,128]{1,0:T(8,128)S(1)}, u32[]{:S(2)}, u32[]{:S(2)}) collective-permute-start(f32[288,128]{1,0:T(8,128)S(1)} %total_state.2), channel_id=1, source_target_pairs={{0,8},{2,10},{4,12},{6,14},{8,0},{10,2},{12,4},{14,6},{16,24},{18,... | collective-permute-start | bytes 442376 | tf_op jit(solution)/shard_map/ppermute | solution.py:551
  17.8 2.0 %collective-permute-done.4.refs_9_ = f32[288,128]{1,0:T(8,128)S(1)} collective-permute-done((f32[288,128]{1,0:T(8,128)S(1)}, f32[288,128]{1,0:T(8,128)S(1)}, u32[]{:S(2)}, u32[]{:S(2)}) %collective-permute-start.4) | collective-permute-done | bytes 147488 | tf_op jit(solution)/shard_map/ppermute | solution.py:551
  19.7 1.2 %collective-permute-done.3.refs_8_ = f32[288,128]{1,0:T(8,128)S(1)} collective-permute-done((f32[288,128]{1,0:T(8,128)S(1)}, f32[288,128]{1,0:T(8,128)S(1)}, u32[]{:S(2)}, u32[]{:S(2)}) %collective-permute-start.3) | collective-permute-done | bytes 147488 | tf_op jit(solution)/shard_map/ppermute | solution.py:551
  21.1 1.8 %collective-permute-start.5 = (f32[288,128]{1,0:T(8,128)S(1)}, f32[288,128]{1,0:T(8,128)S(1)}, u32[]{:S(2)}, u32[]{:S(2)}) collective-permute-start(f32[288,128]{1,0:T(8,128)S(1)} %get-tuple-element.43), channel_id=1, source_target_pairs={{0,6},{2,4},{4,2},{6,0},{8,14},{10,12},{12,10},{14,8},{16,22},{18,... | collective-permute-start | bytes 442376 | tf_op jit(solution)/shard_map/ppermute | solution.py:468
  24.7 2.5 %local_attention.1 = (bf16[128,2048]{1,0:T(8,128)(2,1)S(1)}, f32[128,1536]{1,0:T(8,128)S(1)}, bf16[128,1536]{1,0:T(8,128)(2,1)S(1)}) custom-call(s32[16]{0:T(128)} %lengths_ref.3, f32[16,128]{1,0:T(8,128)S(1)} %copy-done.3, bf16[128,1536]{1,0:T(8,128)(2,1)S(1)} %copy-done.4, bf16[128,1536]{1,0:T(8,128)(2,1)S(1)} %copy-done.1, bf16[128,1536]{1,0:T(8,128)(2,1)S(1)} %copy-done.2), custom_call_target="tpu_custom_call" | custom-call | flops 1000000000 | bytes 2891776 | tf_op jit(solution)/shard_map/local_attention/pallas_call | solution.py:450
  27.5 1.5 %collective-permute-done.6.refs_2_ = f32[288,128]{1,0:T(8,128)S(1)} collective-permute-done((f32[288,128]{1,0:T(8,128)S(1)}, f32[288,128]{1,0:T(8,128)S(1)}, u32[]{:S(2)}, u32[]{:S(2)}) %collective-permute-start.6) | collective-permute-done | bytes 147488 | tf_op jit(solution)/shard_map/ppermute | solution.py:468
  29.5 1.2 %collective-permute-done.8.other_ref = f32[128,128]{1,0:T(8,128)S(1)} collective-permute-done((f32[128,128]{1,0:T(8,128)S(1)}, f32[128,128]{1,0:T(8,128)S(1)}, u32[]{:S(2)}, u32[]{:S(2)}) %collective-permute-start.8) | collective-permute-done | bytes 65568 | tf_op jit(solution)/shard_map/ppermute | solution.py:571
  31.4 1.3 %collective-permute-start.9 = (f32[288,128]{1,0:T(8,128)S(1)}, f32[288,128]{1,0:T(8,128)S(1)}, u32[]{:S(2)}, u32[]{:S(2)}) collective-permute-start(f32[288,128]{1,0:T(8,128)S(1)} %get-tuple-element.59), channel_id=1, source_target_pairs={{0,2},{2,0},{4,6},{6,4},{8,10},{10,8},{12,14},{14,12},{16,18},{18,... | collective-permute-start | bytes 442376 | tf_op jit(solution)/shard_map/ppermute | solution.py:468
  32.7 1.0 %collective-permute-start.10 = (f32[288,128]{1,0:T(8,128)S(1)}, f32[288,128]{1,0:T(8,128)S(1)}, u32[]{:S(2)}, u32[]{:S(2)}) collective-permute-start(f32[288,128]{1,0:T(8,128)S(1)} %get-tuple-element.60), channel_id=1, source_target_pairs={{0,4},{2,6},{4,0},{6,2},{8,12},{10,14},{12,8},{14,10},{16,20},{18,... | collective-permute-start | bytes 442376 | tf_op jit(solution)/shard_map/ppermute | solution.py:468
  33.7 1.3 %collective-permute-start.11 = (f32[288,128]{1,0:T(8,128)S(1)}, f32[288,128]{1,0:T(8,128)S(1)}, u32[]{:S(2)}, u32[]{:S(2)}) collective-permute-start(f32[288,128]{1,0:T(8,128)S(1)} %get-tuple-element.61), channel_id=1, source_target_pairs={{0,6},{2,4},{4,2},{6,0},{8,14},{10,12},{12,10},{14,8},{16,22},{18,... | collective-permute-start | bytes 442376 | tf_op jit(solution)/shard_map/ppermute | solution.py:468
  35.0 3.2 %collective-permute-done.9.refs_1_ = f32[288,128]{1,0:T(8,128)S(1)} collective-permute-done((f32[288,128]{1,0:T(8,128)S(1)}, f32[288,128]{1,0:T(8,128)S(1)}, u32[]{:S(2)}, u32[]{:S(2)}) %collective-permute-start.9) | collective-permute-done | bytes 147488 | tf_op jit(solution)/shard_map/ppermute | solution.py:468
  38.2 3.3 %collective-permute-done.10.refs_2_ = f32[288,128]{1,0:T(8,128)S(1)} collective-permute-done((f32[288,128]{1,0:T(8,128)S(1)}, f32[288,128]{1,0:T(8,128)S(1)}, u32[]{:S(2)}, u32[]{:S(2)}) %collective-permute-start.10) | collective-permute-done | bytes 147488 | tf_op jit(solution)/shard_map/ppermute | solution.py:468
  42.5 1.5 %collective-permute-start.12 = (f32[288,128]{1,0:T(8,128)S(1)}, f32[288,128]{1,0:T(8,128)S(1)}, u32[]{:S(2)}, u32[]{:S(2)}) collective-permute-start(f32[288,128]{1,0:T(8,128)S(1)} %total_state.3), channel_id=1, source_target_pairs={{0,8},{2,10},{4,12},{6,14},{8,0},{10,2},{12,4},{14,6},{16,24},{18,... | collective-permute-start | bytes 442376 | tf_op jit(solution)/shard_map/ppermute | solution.py:551
  43.9 2.9 %collective-permute-done.13.refs_9_ = f32[288,128]{1,0:T(8,128)S(1)} collective-permute-done((f32[288,128]{1,0:T(8,128)S(1)}, f32[288,128]{1,0:T(8,128)S(1)}, u32[]{:S(2)}, u32[]{:S(2)}) %collective-permute-start.13) | collective-permute-done | bytes 147488 | tf_op jit(solution)/shard_map/ppermute | solution.py:551
  47.7 1.7 %collective-permute-start.14 = (f32[288,128]{1,0:T(8,128)S(1)}, f32[288,128]{1,0:T(8,128)S(1)}, u32[]{:S(2)}, u32[]{:S(2)}) collective-permute-start(f32[288,128]{1,0:T(8,128)S(1)} %get-tuple-element.63), channel_id=1, source_target_pairs={{0,6},{2,4},{4,2},{6,0},{8,14},{10,12},{12,10},{14,8},{16,22},{18,... | collective-permute-start | bytes 442376 | tf_op jit(solution)/shard_map/ppermute | solution.py:468
  49.4 1.1 %collective-permute-start.15 = (f32[288,128]{1,0:T(8,128)S(1)}, f32[288,128]{1,0:T(8,128)S(1)}, u32[]{:S(2)}, u32[]{:S(2)}) collective-permute-start(f32[288,128]{1,0:T(8,128)S(1)} %get-tuple-element.64), channel_id=1, source_target_pairs={{0,4},{2,6},{4,0},{6,2},{8,12},{10,14},{12,8},{14,10},{16,20},{18,... | collective-permute-start | bytes 442376 | tf_op jit(solution)/shard_map/ppermute | solution.py:468
  51.2 4.2 %local_grads.1 = (bf16[128,1536]{1,0:T(8,128)(2,1)}, bf16[128,1536]{1,0:T(8,128)(2,1)}, f32[128,1536]{1,0:T(8,128)S(1)}, f32[128,1536]{1,0:T(8,128)S(1)}, bf16[128,1536]{1,0:T(8,128)(2,1)S(1)}) custom-call(s32[16]{0:T(128)} %lengths_ref.3, f32[16,128]{1,0:T(8,128)S(1)} %copy-done.3, bf16[128,1536]{1,0:T(8,128)(2,1)S(1)} %copy-done.4, ...), custom_call_target="tpu_custom_call" | custom-call | flops 1000000000 | bytes 6010880 | tf_op jit(solution)/shard_map/local_grads/pallas_call | solution.py:450
  55.7 1.3 %key_value_grads.1 = (bf16[128,1536]{1,0:T(8,128)(2,1)}, bf16[128,1536]{1,0:T(8,128)(2,1)}) custom-call(f32[128,1536]{1,0:T(8,128)S(1)} %get-tuple-element.54.key_local_ref, f32[128,1536]{1,0:T(8,128)S(1)} %get-tuple-element.55.value_local_ref, bf16[128,1536]{1,0:T(8,128)(2,1)S(1)} %get-tuple-element.56.weighted_values_ref, ...), custom_call_target="tpu_custom_call" | custom-call | bytes 3735552 | tf_op jit(solution)/shard_map/key_value_grads/pallas_call | solution.py:450
  (33 shorter events, 6.3 us)
Async XLA Ops:
  2.6 7.7 %collective-permute-start = (f32[304,128]{1,0:T(8,128)S(1)}, f32[304,128]{1,0:T(8,128)S(1)}, u32[]{:S(2)}, u32[]{:S(2)}) collective-permute-start(f32[304,128]{1,0:T(8,128)S(1)} %get-tuple-element.39), channel_id=1, source_target_pairs={{0,2},{2,0},{4,6},{6,4},{8,10},{10,8},{12,14},{14,12},{16,18},{18,... | collective-permute-start | bytes 466952 | tf_op jit(solution)/shard_map/ppermute | solution.py:468
  5.6 8.8 %collective-permute-start.1 = (f32[304,128]{1,0:T(8,128)S(1)}, f32[304,128]{1,0:T(8,128)S(1)}, u32[]{:S(2)}, u32[]{:S(2)}) collective-permute-start(f32[304,128]{1,0:T(8,128)S(1)} %get-tuple-element.40), channel_id=1, source_target_pairs={{0,4},{2,6},{4,0},{6,2},{8,12},{10,14},{12,8},{14,10},{16,20},{18,... | collective-permute-start | bytes 466952 | tf_op jit(solution)/shard_map/ppermute | solution.py:468
  7.1 7.3 %collective-permute-start.2 = (f32[304,128]{1,0:T(8,128)S(1)}, f32[304,128]{1,0:T(8,128)S(1)}, u32[]{:S(2)}, u32[]{:S(2)}) collective-permute-start(f32[304,128]{1,0:T(8,128)S(1)} %get-tuple-element.41), channel_id=1, source_target_pairs={{0,6},{2,4},{4,2},{6,0},{8,14},{10,12},{12,10},{14,8},{16,22},{18,... | collective-permute-start | bytes 466952 | tf_op jit(solution)/shard_map/ppermute | solution.py:468
  14.5 10.1 %copy-start.1 = (bf16[128,1536]{1,0:T(8,128)(2,1)S(1)}, bf16[128,1536]{1,0:T(8,128)(2,1)}, u32[]{:S(2)}) copy-start(bf16[128,1536]{1,0:T(8,128)(2,1)} %keys_ref.3) | copy-start | bytes 1179652
  14.5 10.1 %copy-start.2 = (bf16[128,1536]{1,0:T(8,128)(2,1)S(1)}, bf16[128,1536]{1,0:T(8,128)(2,1)}, u32[]{:S(2)}) copy-start(bf16[128,1536]{1,0:T(8,128)(2,1)} %values_ref.3) | copy-start | bytes 1179652
  14.5 10.1 %copy-start.4 = (bf16[128,1536]{1,0:T(8,128)(2,1)S(1)}, bf16[128,1536]{1,0:T(8,128)(2,1)}, u32[]{:S(2)}) copy-start(bf16[128,1536]{1,0:T(8,128)(2,1)} %queries_ref.3) | copy-start | bytes 1179652
  14.5 5.2 %collective-permute-start.4 = (f32[288,128]{1,0:T(8,128)S(1)}, f32[288,128]{1,0:T(8,128)S(1)}, u32[]{:S(2)}, u32[]{:S(2)}) collective-permute-start(f32[288,128]{1,0:T(8,128)S(1)} %total_state.2), channel_id=1, source_target_pairs={{0,2},{2,0},{4,6},{6,4},{8,16},{10,18},{12,20},{14,22},{16,8},{18,... | collective-permute-start | bytes 442376 | tf_op jit(solution)/shard_map/ppermute | solution.py:551
  15.8 5.1 %collective-permute-start.3 = (f32[288,128]{1,0:T(8,128)S(1)}, f32[288,128]{1,0:T(8,128)S(1)}, u32[]{:S(2)}, u32[]{:S(2)}) collective-permute-start(f32[288,128]{1,0:T(8,128)S(1)} %total_state.2), channel_id=1, source_target_pairs={{0,8},{2,10},{4,12},{6,14},{8,0},{10,2},{12,4},{14,6},{16,24},{18,... | collective-permute-start | bytes 442376 | tf_op jit(solution)/shard_map/ppermute | solution.py:551
  21.0 3.7 %copy-start.5 = (f32[1536]{0:T(1024)S(1)}, f32[1536]{0:T(1024)}, u32[]{:S(2)}) copy-start(f32[1536]{0:T(1024)} %param.11) | copy-start | bytes 18436
  21.1 6.4 %collective-permute-start.5 = (f32[288,128]{1,0:T(8,128)S(1)}, f32[288,128]{1,0:T(8,128)S(1)}, u32[]{:S(2)}, u32[]{:S(2)}) collective-permute-start(f32[288,128]{1,0:T(8,128)S(1)} %get-tuple-element.43), channel_id=1, source_target_pairs={{0,6},{2,4},{4,2},{6,0},{8,14},{10,12},{12,10},{14,8},{16,22},{18,... | collective-permute-start | bytes 442376 | tf_op jit(solution)/shard_map/ppermute | solution.py:468
  22.9 1.8 %copy-start.3 = (f32[16,128]{1,0:T(8,128)S(1)}, f32[16,128]{1,0:T(8,128)}, u32[]{:S(2)}) copy-start(f32[16,128]{1,0:T(8,128)} %decay_ref.3) | copy-start | bytes 24580
  22.9 6.1 %collective-permute-start.6 = (f32[288,128]{1,0:T(8,128)S(1)}, f32[288,128]{1,0:T(8,128)S(1)}, u32[]{:S(2)}, u32[]{:S(2)}) collective-permute-start(f32[288,128]{1,0:T(8,128)S(1)} %get-tuple-element.44), channel_id=1, source_target_pairs={{0,4},{2,6},{4,0},{6,2},{8,12},{10,14},{12,8},{14,10},{16,20},{18,... | collective-permute-start | bytes 442376 | tf_op jit(solution)/shard_map/ppermute | solution.py:468
  23.7 5.3 %collective-permute-start.7 = (f32[288,128]{1,0:T(8,128)S(1)}, f32[288,128]{1,0:T(8,128)S(1)}, u32[]{:S(2)}, u32[]{:S(2)}) collective-permute-start(f32[288,128]{1,0:T(8,128)S(1)} %get-tuple-element.45), channel_id=1, source_target_pairs={{0,2},{2,0},{4,6},{6,4},{8,10},{10,8},{12,14},{14,12},{16,18},{18,... | collective-permute-start | bytes 442376 | tf_op jit(solution)/shard_map/ppermute | solution.py:468
  24.7 4.3 %copy-start = (bf16[128,1536]{1,0:T(8,128)(2,1)S(1)}, bf16[128,1536]{1,0:T(8,128)(2,1)}, u32[]{:S(2)}) copy-start(bf16[128,1536]{1,0:T(8,128)(2,1)} %out_grad_ref.3) | copy-start | bytes 1179652
  29.5 1.3 %collective-permute-start.8 = (f32[128,128]{1,0:T(8,128)S(1)}, f32[128,128]{1,0:T(8,128)S(1)}, u32[]{:S(2)}, u32[]{:S(2)}) collective-permute-start(f32[128,128]{1,0:T(8,128)S(1)} %get-tuple-element.47.sums_ref), channel_id=1, source_target_pairs={{0,1},{1,0},{2,3},{3,2},{4,5},{5,4},{6,7},{7,6},{8,9},{9,8},{10,11... | collective-permute-start | bytes 196616 | tf_op jit(solution)/shard_map/ppermute | solution.py:571
  31.4 6.8 %collective-permute-start.9 = (f32[288,128]{1,0:T(8,128)S(1)}, f32[288,128]{1,0:T(8,128)S(1)}, u32[]{:S(2)}, u32[]{:S(2)}) collective-permute-start(f32[288,128]{1,0:T(8,128)S(1)} %get-tuple-element.59), channel_id=1, source_target_pairs={{0,2},{2,0},{4,6},{6,4},{8,10},{10,8},{12,14},{14,12},{16,18},{18,... | collective-permute-start | bytes 442376 | tf_op jit(solution)/shard_map/ppermute | solution.py:468
  32.7 8.8 %collective-permute-start.10 = (f32[288,128]{1,0:T(8,128)S(1)}, f32[288,128]{1,0:T(8,128)S(1)}, u32[]{:S(2)}, u32[]{:S(2)}) collective-permute-start(f32[288,128]{1,0:T(8,128)S(1)} %get-tuple-element.60), channel_id=1, source_target_pairs={{0,4},{2,6},{4,0},{6,2},{8,12},{10,14},{12,8},{14,10},{16,20},{18,... | collective-permute-start | bytes 442376 | tf_op jit(solution)/shard_map/ppermute | solution.py:468
  33.7 7.8 %collective-permute-start.11 = (f32[288,128]{1,0:T(8,128)S(1)}, f32[288,128]{1,0:T(8,128)S(1)}, u32[]{:S(2)}, u32[]{:S(2)}) collective-permute-start(f32[288,128]{1,0:T(8,128)S(1)} %get-tuple-element.61), channel_id=1, source_target_pairs={{0,6},{2,4},{4,2},{6,0},{8,14},{10,12},{12,10},{14,8},{16,22},{18,... | collective-permute-start | bytes 442376 | tf_op jit(solution)/shard_map/ppermute | solution.py:468
  41.6 5.2 %collective-permute-start.13 = (f32[288,128]{1,0:T(8,128)S(1)}, f32[288,128]{1,0:T(8,128)S(1)}, u32[]{:S(2)}, u32[]{:S(2)}) collective-permute-start(f32[288,128]{1,0:T(8,128)S(1)} %total_state.3), channel_id=1, source_target_pairs={{0,2},{2,0},{4,6},{6,4},{8,16},{10,18},{12,20},{14,22},{16,8},{18,... | collective-permute-start | bytes 442376 | tf_op jit(solution)/shard_map/ppermute | solution.py:551
  42.5 5.1 %collective-permute-start.12 = (f32[288,128]{1,0:T(8,128)S(1)}, f32[288,128]{1,0:T(8,128)S(1)}, u32[]{:S(2)}, u32[]{:S(2)}) collective-permute-start(f32[288,128]{1,0:T(8,128)S(1)} %total_state.3), channel_id=1, source_target_pairs={{0,8},{2,10},{4,12},{6,14},{8,0},{10,2},{12,4},{14,6},{16,24},{18,... | collective-permute-start | bytes 442376 | tf_op jit(solution)/shard_map/ppermute | solution.py:551
  47.7 7.7 %collective-permute-start.14 = (f32[288,128]{1,0:T(8,128)S(1)}, f32[288,128]{1,0:T(8,128)S(1)}, u32[]{:S(2)}, u32[]{:S(2)}) collective-permute-start(f32[288,128]{1,0:T(8,128)S(1)} %get-tuple-element.63), channel_id=1, source_target_pairs={{0,6},{2,4},{4,2},{6,0},{8,14},{10,12},{12,10},{14,8},{16,22},{18,... | collective-permute-start | bytes 442376 | tf_op jit(solution)/shard_map/ppermute | solution.py:468
  49.4 6.3 %collective-permute-start.15 = (f32[288,128]{1,0:T(8,128)S(1)}, f32[288,128]{1,0:T(8,128)S(1)}, u32[]{:S(2)}, u32[]{:S(2)}) collective-permute-start(f32[288,128]{1,0:T(8,128)S(1)} %get-tuple-element.64), channel_id=1, source_target_pairs={{0,4},{2,6},{4,0},{6,2},{8,12},{10,14},{12,8},{14,10},{16,20},{18,... | collective-permute-start | bytes 442376 | tf_op jit(solution)/shard_map/ppermute | solution.py:468
  50.4 5.2 %collective-permute-start.16 = (f32[288,128]{1,0:T(8,128)S(1)}, f32[288,128]{1,0:T(8,128)S(1)}, u32[]{:S(2)}, u32[]{:S(2)}) collective-permute-start(f32[288,128]{1,0:T(8,128)S(1)} %get-tuple-element.65), channel_id=1, source_target_pairs={{0,2},{2,0},{4,6},{6,4},{8,10},{10,8},{12,14},{14,12},{16,18},{18,... | collective-permute-start | bytes 442376 | tf_op jit(solution)/shard_map/ppermute | solution.py:468
